TPU v7x, 32 devices: a whole 2x2x4 slice. The times are simulated.
32 devices in a mesh: gx: 4 (over y, core), gy: 8 (over z, x).
Axes of the slice: x: 2, y: 2, z: 4, core: 2. Of those that a mesh axis runs over, the one named last changes fastest.
Arguments:
- states: bfloat16 [32, 512, 768], P(('gx', 'gy')), may hold values from -6 to 6
- encoded: bfloat16 [32, 512, 768], P(('gx', 'gy')), may hold values from -6 to 6
- cotangent: bfloat16 [32, 512, 768], P(('gx', 'gy')), may hold values from -6 to 6
- dec_lens: int32 [32], P(('gx', 'gy')), may hold values from 1 to 512, 10240 in all
- enc_lens: int32 [32], P(('gx', 'gy')), may hold values from 1 to 512, 8192 in all
- self_query: bfloat16 [768, 768], P(('gx', 'gy')), may hold values from -0.02734375 to 0.02734375
- self_key: bfloat16 [768, 768], P(('gx', 'gy')), may hold values from -0.21875 to 0.21875
- self_value: bfloat16 [768, 768], P(('gx', 'gy')), may hold values from -0.21875 to 0.21875
- self_out: bfloat16 [768, 768], P(('gx', 'gy')), may hold values from -1.25 to 1.25
- cross_query: bfloat16 [768, 768], P(('gx', 'gy')), may hold values from -0.02734375 to 0.02734375
- cross_key: bfloat16 [768, 768], P(('gx', 'gy')), may hold values from -0.21875 to 0.21875
- cross_value: bfloat16 [768, 768], P(('gx', 'gy')), may hold values from -0.21875 to 0.21875
- cross_out: bfloat16 [768, 768], P(('gx', 'gy')), may hold values from -1.25 to 1.25
- ffn_gate: bfloat16 [768, 2048], P(('gx', 'gy')), may hold values from -0.21875 to 0.21875
- ffn_up: bfloat16 [768, 2048], P(('gx', 'gy')), may hold values from -0.21875 to 0.21875
- ffn_out: bfloat16 [768, 2048], P(('gx', 'gy')), may hold values from -0.125 to 0.125
- gain_self: bfloat16 [768], P(('gx', 'gy')), may hold values from 0.5 to 1.5
- gain_cross: bfloat16 [768], P(('gx', 'gy')), may hold values from 0.5 to 1.5
- gain_ffn: bfloat16 [768], P(('gx', 'gy')), may hold values from 0.5 to 1.5
- bucket_bias_table: bfloat16 [32, 12], replicated, may hold values from -4 to 4
Outputs:
- output: bfloat16 [32, 512, 768], P(('gx', 'gy'))
- grad_states: bfloat16 [32, 512, 768], P(('gx', 'gy'))
- grad_encoded: bfloat16 [32, 512, 768], P(('gx', 'gy'))
- grad_self_query: float32 [768, 768], P(('gx', 'gy'))
- grad_self_key: float32 [768, 768], P(('gx', 'gy'))
- grad_self_value: float32 [768, 768], P(('gx', 'gy'))
- grad_self_out: float32 [768, 768], P(('gx', 'gy'))
- grad_cross_query: float32 [768, 768], P(('gx', 'gy'))
- grad_cross_key: float32 [768, 768], P(('gx', 'gy'))
- grad_cross_value: float32 [768, 768], P(('gx', 'gy'))
- grad_cross_out: float32 [768, 768], P(('gx', 'gy'))
- grad_ffn_gate: float32 [768, 2048], P(('gx', 'gy'))
- grad_ffn_up: float32 [768, 2048], P(('gx', 'gy'))
- grad_ffn_out: float32 [768, 2048], P(('gx', 'gy'))
- grad_gain_self: float32 [768], P(('gx', 'gy'))
- grad_gain_cross: float32 [768], P(('gx', 'gy'))
- grad_gain_ffn: float32 [768], P(('gx', 'gy'))
- grad_bucket_table: float32 [32, 12], replicated
Inputs may be any that keep to these rules, and one draw needn't show every extreme that they name: Row r holds one decoder sequence of dec_lens[r] tokens in its first slots; the longest has exactly 512. Row r has enc_lens[r] encoder outputs in its first slots; the longest has exactly 512.
All inputs are finite; a program needn't handle non-finite values. No bound on the sum of `dec_lens` or of `enc_lens` on one device may be relied on, other than what follows from the above.
Results may differ from a plain program's by a relative error of at most 0.025.
Values may be sent and summed in bfloat16 or wider, within the bound.
No kernel may reach another device: no remote copies, remote signals or barrier semaphores. Data moves between devices by JAX's collectives and lax.ppermute only.
A program may use at most 192 MiB of HBM per device.

v0:
```python
import math

import jax
import jax.numpy as jnp
from jax import lax
from jax.sharding import PartitionSpec as P

H = 12
HD = 64
NB = 32


norm_eps = 1e-06
masked_score = -1000000000.0
bucket_edges = [int(math.ceil(16 * 8 ** (power / 16.0))) for power in range(1, 16)]


def buckets_of(length):
    places = jnp.arange(length, dtype=jnp.int32)
    distance = jnp.maximum(places[:, None] - places[None, :], 0)
    counted = jnp.zeros_like(distance)
    for edge in bucket_edges:
        counted = counted + (distance >= edge).astype(jnp.int32)
    return jnp.where(distance < 16, distance, 16 + counted)


def rms_norm(values, gain):
    return values * lax.rsqrt(jnp.mean(values * values, axis=-1, keepdims=True) + norm_eps) * gain


def norm_back(values, gain, d_normed):
    normed, pullback = jax.vjp(rms_norm, values, gain)
    return pullback(d_normed)


def gated_unit(first, second):
    return jax.nn.gelu(first, approximate=True) * second


def gated_back(gate_pre, up_pre, d_gated):
    gated, pullback = jax.vjp(gated_unit, gate_pre, up_pre)
    return pullback(d_gated)


def times(left, right):
    return jnp.dot(left, right, preferred_element_type=jnp.float32)


def times_t(left, right):
    return lax.dot_general(
        left, right, (((1,), (1,)), ((), ())), preferred_element_type=jnp.float32
    )


def inner_t(left, right):
    return lax.dot_general(
        left, right, (((0,), (0,)), ((), ())), preferred_element_type=jnp.float32
    )


def head_scores(q_row, k_row, position_bias, allowed):
    q_heads = q_row.reshape(q_row.shape[0], H, HD)
    k_heads = k_row.reshape(k_row.shape[0], H, HD)
    scores = (
        jnp.einsum("qhd,khd->hqk", q_heads, k_heads, preferred_element_type=jnp.float32)
        + position_bias
    )
    return jnp.where(allowed[None], scores, masked_score)


def attend_forward(q_row, k_row, v_row, position_bias, allowed):
    scores = head_scores(q_row, k_row, position_bias, allowed)
    highest = jnp.max(scores, axis=-1, keepdims=True)
    expo = jnp.exp(scores - highest)
    denom = jnp.sum(expo, axis=-1, keepdims=True)
    probs = (expo / denom).astype(jnp.bfloat16)
    v_heads = v_row.reshape(v_row.shape[0], H, HD)
    mixed = jnp.einsum("hqk,khd->qhd", probs, v_heads, preferred_element_type=jnp.float32)
    return (mixed.reshape(q_row.shape[0], H * HD).astype(jnp.bfloat16), highest + jnp.log(denom))


def attend_backward(q_row, k_row, v_row, position_bias, allowed, lse_row, d_mixed):
    scores = head_scores(q_row, k_row, position_bias, allowed)
    probs = jnp.exp(scores - lse_row)
    q_heads = q_row.reshape(q_row.shape[0], H, HD)
    k_heads = k_row.reshape(k_row.shape[0], H, HD)
    v_heads = v_row.reshape(v_row.shape[0], H, HD)
    head_gradients = d_mixed.reshape(d_mixed.shape[0], H, HD)
    d_probs = jnp.einsum(
        "qhd,khd->hqk", head_gradients, v_heads, preferred_element_type=jnp.float32
    )
    d_values = jnp.einsum(
        "hqk,qhd->khd",
        probs.astype(jnp.bfloat16),
        head_gradients,
        preferred_element_type=jnp.float32,
    )
    d_scores = (probs * (d_probs - jnp.sum(probs * d_probs, axis=-1, keepdims=True))).astype(
        jnp.bfloat16
    )
    d_queries = jnp.einsum("hqk,khd->qhd", d_scores, k_heads, preferred_element_type=jnp.float32)
    d_keys = jnp.einsum("hqk,qhd->khd", d_scores, q_heads, preferred_element_type=jnp.float32)
    width = H * HD
    return (
        d_queries.reshape(q_row.shape[0], width).astype(jnp.bfloat16),
        d_keys.reshape(k_row.shape[0], width).astype(jnp.bfloat16),
        d_values.reshape(v_row.shape[0], width).astype(jnp.bfloat16),
        d_scores,
    )


def self_mask(length, dec_len):
    places = jnp.arange(length, dtype=jnp.int32)
    return (places[None, :] <= places[:, None]) & (places[None, :] < dec_len)


def cross_mask(length, enc_length, enc_len):
    return jnp.broadcast_to(
        (jnp.arange(enc_length, dtype=jnp.int32) < enc_len)[None, :], (length, enc_length)
    )


def run_forward(states, encoded, dec_lens, enc_lens, params, position_bias):
    (
        self_query,
        self_key,
        self_value,
        self_out,
        cross_query,
        cross_key,
        cross_value,
        cross_out,
        ffn_gate,
        ffn_up,
        ffn_out,
        gain_self,
        gain_cross,
        gain_ffn,
    ) = params
    rows, length, width = states.shape
    enc_length = encoded.shape[1]
    inputs = states.astype(jnp.float32).reshape(rows * length, width)
    enc_flat = encoded.reshape(rows * enc_length, width)
    normed_one = rms_norm(inputs, gain_self.astype(jnp.float32)).astype(jnp.bfloat16)
    queries = times(normed_one, self_query).astype(jnp.bfloat16).reshape(rows, length, -1)
    keys_one = times(normed_one, self_key).astype(jnp.bfloat16).reshape(rows, length, -1)
    values_one = times(normed_one, self_value).astype(jnp.bfloat16).reshape(rows, length, -1)

    def self_row(pieces):
        return attend_forward(
            pieces[0], pieces[1], pieces[2], position_bias, self_mask(length, pieces[3])
        )

    mixed_one, lse_one = lax.map(self_row, (queries, keys_one, values_one, dec_lens))
    mixed_one_flat = mixed_one.reshape(rows * length, -1)
    hidden_one = inputs + times_t(mixed_one_flat, self_out)
    normed_two = rms_norm(hidden_one, gain_cross.astype(jnp.float32)).astype(jnp.bfloat16)
    cross_queries = times(normed_two, cross_query).astype(jnp.bfloat16).reshape(rows, length, -1)
    cross_keys = times(enc_flat, cross_key).astype(jnp.bfloat16).reshape(rows, enc_length, -1)
    cross_values = times(enc_flat, cross_value).astype(jnp.bfloat16).reshape(rows, enc_length, -1)

    def cross_row(pieces):
        return attend_forward(
            pieces[0], pieces[1], pieces[2], 0.0, cross_mask(length, enc_length, pieces[3])
        )

    mixed_two, lse_two = lax.map(cross_row, (cross_queries, cross_keys, cross_values, enc_lens))
    mixed_two_flat = mixed_two.reshape(rows * length, -1)
    hidden_two = hidden_one + times_t(mixed_two_flat, cross_out)
    normed_three = rms_norm(hidden_two, gain_ffn.astype(jnp.float32)).astype(jnp.bfloat16)
    gate_pre = times(normed_three, ffn_gate)
    up_pre = times(normed_three, ffn_up)
    gated = gated_unit(gate_pre, up_pre).astype(jnp.bfloat16)
    result = hidden_two + times_t(gated, ffn_out)
    return (
        inputs,
        enc_flat,
        normed_one,
        queries,
        keys_one,
        values_one,
        mixed_one_flat,
        lse_one,
        hidden_one,
        normed_two,
        cross_queries,
        cross_keys,
        cross_values,
        mixed_two_flat,
        lse_two,
        hidden_two,
        normed_three,
        gate_pre,
        up_pre,
        gated,
        result,
    )


def per_device(
    states,
    encoded,
    cotangent,
    dec_lens,
    enc_lens,
    self_query,
    self_key,
    self_value,
    self_out,
    cross_query,
    cross_key,
    cross_value,
    cross_out,
    ffn_gate,
    ffn_up,
    ffn_out,
    gain_self,
    gain_cross,
    gain_ffn,
    bucket_bias_table,
):
    gathered = (
        lax.all_gather(self_query, ("gx", "gy"), axis=0, tiled=True),
        lax.all_gather(self_key, ("gx", "gy"), axis=0, tiled=True),
        lax.all_gather(self_value, ("gx", "gy"), axis=0, tiled=True),
        lax.all_gather(self_out, ("gx", "gy"), axis=0, tiled=True),
        lax.all_gather(cross_query, ("gx", "gy"), axis=0, tiled=True),
        lax.all_gather(cross_key, ("gx", "gy"), axis=0, tiled=True),
        lax.all_gather(cross_value, ("gx", "gy"), axis=0, tiled=True),
        lax.all_gather(cross_out, ("gx", "gy"), axis=0, tiled=True),
        lax.all_gather(ffn_gate, ("gx", "gy"), axis=0, tiled=True),
        lax.all_gather(ffn_up, ("gx", "gy"), axis=0, tiled=True),
        lax.all_gather(ffn_out, ("gx", "gy"), axis=0, tiled=True),
        lax.all_gather(gain_self, ("gx", "gy"), axis=0, tiled=True),
        lax.all_gather(gain_cross, ("gx", "gy"), axis=0, tiled=True),
        lax.all_gather(gain_ffn, ("gx", "gy"), axis=0, tiled=True),
    )
    rows, length, width = states.shape
    enc_length = encoded.shape[1]
    buckets = buckets_of(length)
    bucket_ids = jnp.arange(NB, dtype=jnp.int32)
    indicator_matrix = (buckets[None] == bucket_ids[:, None, None]).astype(jnp.bfloat16)
    position_bias = jnp.einsum(
        "eri,ex->xri", indicator_matrix, bucket_bias_table, preferred_element_type=jnp.float32
    )
    first_pass = run_forward(states, encoded, dec_lens, enc_lens, gathered, position_bias)
    output = first_pass[-1].astype(jnp.bfloat16).reshape(states.shape)
    params = (
        lax.all_gather(self_query, ("gx", "gy"), axis=0, tiled=True),
        lax.all_gather(self_key, ("gx", "gy"), axis=0, tiled=True),
        lax.all_gather(self_value, ("gx", "gy"), axis=0, tiled=True),
        lax.all_gather(self_out, ("gx", "gy"), axis=0, tiled=True),
        lax.all_gather(cross_query, ("gx", "gy"), axis=0, tiled=True),
        lax.all_gather(cross_key, ("gx", "gy"), axis=0, tiled=True),
        lax.all_gather(cross_value, ("gx", "gy"), axis=0, tiled=True),
        lax.all_gather(cross_out, ("gx", "gy"), axis=0, tiled=True),
        lax.all_gather(ffn_gate, ("gx", "gy"), axis=0, tiled=True),
        lax.all_gather(ffn_up, ("gx", "gy"), axis=0, tiled=True),
        lax.all_gather(ffn_out, ("gx", "gy"), axis=0, tiled=True),
        lax.all_gather(gain_self, ("gx", "gy"), axis=0, tiled=True),
        lax.all_gather(gain_cross, ("gx", "gy"), axis=0, tiled=True),
        lax.all_gather(gain_ffn, ("gx", "gy"), axis=0, tiled=True),
    )
    (
        w_query,
        w_key,
        w_value,
        w_out,
        c_query,
        c_key,
        c_value,
        c_out,
        w_gate,
        w_up,
        w_down,
        g_self,
        g_cross,
        g_ffn,
    ) = params
    (
        inputs,
        enc_flat,
        normed_one,
        queries,
        keys_one,
        values_one,
        mixed_one_flat,
        lse_one,
        hidden_one,
        normed_two,
        cross_queries,
        cross_keys,
        cross_values,
        mixed_two_flat,
        lse_two,
        hidden_two,
        normed_three,
        gate_pre,
        up_pre,
        gated,
        result,
    ) = run_forward(states, encoded, dec_lens, enc_lens, params, position_bias)
    tokens_here = rows * length
    d_result_low = cotangent.reshape(tokens_here, width)
    d_result = d_result_low.astype(jnp.float32)
    grad_ffn_out = inner_t(d_result_low, gated)
    d_gated = times(d_result_low, w_down)
    gate_gradient, d_up = gated_back(gate_pre, up_pre, d_gated)
    gate_gradient = gate_gradient.astype(jnp.bfloat16)
    d_up = d_up.astype(jnp.bfloat16)
    grad_ffn_gate = inner_t(normed_three, gate_gradient)
    grad_ffn_up = inner_t(normed_three, d_up)
    d_normed_three = times_t(gate_gradient, w_gate) + times_t(d_up, w_up)
    d_hidden_two, grad_gain_ffn = norm_back(hidden_two, g_ffn.astype(jnp.float32), d_normed_three)
    d_hidden_two = d_hidden_two + d_result
    d_attn_two = d_hidden_two.astype(jnp.bfloat16)
    grad_cross_out = inner_t(d_attn_two, mixed_two_flat)
    d_mixed_two = times(d_attn_two, c_out).astype(jnp.bfloat16).reshape(rows, length, -1)

    def cross_back_row(pieces):
        d_q, d_k, d_v, d_scores = attend_backward(
            pieces[0],
            pieces[1],
            pieces[2],
            0.0,
            cross_mask(length, enc_length, pieces[3]),
            pieces[4],
            pieces[5],
        )
        return (d_q, d_k, d_v)

    d_cross_q, d_cross_k, d_cross_v = lax.map(
        cross_back_row, (cross_queries, cross_keys, cross_values, enc_lens, lse_two, d_mixed_two)
    )
    d_cross_q = d_cross_q.reshape(tokens_here, -1)
    d_cross_k = d_cross_k.reshape(rows * enc_length, -1)
    d_cross_v = d_cross_v.reshape(rows * enc_length, -1)
    grad_cross_query = inner_t(normed_two, d_cross_q)
    grad_cross_key = inner_t(enc_flat, d_cross_k)
    grad_cross_value = inner_t(enc_flat, d_cross_v)
    d_normed_two = times_t(d_cross_q, c_query)
    grad_encoded = (times_t(d_cross_k, c_key) + times_t(d_cross_v, c_value)).astype(jnp.bfloat16)
    grad_encoded = grad_encoded.reshape(encoded.shape)
    d_hidden_one, grad_gain_cross = norm_back(hidden_one, g_cross.astype(jnp.float32), d_normed_two)
    d_hidden_one = d_hidden_one + d_hidden_two
    d_attn_one = d_hidden_one.astype(jnp.bfloat16)
    grad_self_out = inner_t(d_attn_one, mixed_one_flat)
    d_mixed_one = times(d_attn_one, w_out).astype(jnp.bfloat16).reshape(rows, length, -1)

    def self_back_row(score_acc, pieces):
        d_q, d_k, d_v, d_scores = attend_backward(
            pieces[0],
            pieces[1],
            pieces[2],
            position_bias,
            self_mask(length, pieces[3]),
            pieces[4],
            pieces[5],
        )
        return (score_acc + d_scores.astype(jnp.float32), (d_q, d_k, d_v))

    score_sum, self_grads = lax.scan(
        self_back_row,
        jnp.zeros((H, length, length), jnp.float32),
        (queries, keys_one, values_one, dec_lens, lse_one, d_mixed_one),
    )
    d_self_q = self_grads[0].reshape(tokens_here, -1)
    d_self_k = self_grads[1].reshape(tokens_here, -1)
    d_self_v = self_grads[2].reshape(tokens_here, -1)
    grad_self_query = inner_t(normed_one, d_self_q)
    grad_self_key = inner_t(normed_one, d_self_k)
    grad_self_value = inner_t(normed_one, d_self_v)
    d_normed_one = (
        times_t(d_self_q, w_query) + times_t(d_self_k, w_key) + times_t(d_self_v, w_value)
    )
    d_inputs, grad_gain_self = norm_back(inputs, g_self.astype(jnp.float32), d_normed_one)
    grad_states = (d_inputs + d_hidden_one).astype(jnp.bfloat16).reshape(states.shape)
    block = min(length, 128)

    def bucket_block(start):
        block_buckets = lax.dynamic_slice_in_dim(buckets, start, block, 0)
        bucket_indicator = (block_buckets[None] == bucket_ids[:, None, None]).astype(jnp.float32)
        part = lax.dynamic_slice_in_dim(score_sum, start, block, 1)
        return jnp.einsum("mrs,nrs->nm", part, bucket_indicator, precision=lax.Precision.HIGHEST)

    table_terms = jnp.sum(
        lax.map(bucket_block, jnp.arange(length // block, dtype=jnp.int32) * block), axis=0
    )
    grad_bucket_table = lax.psum(table_terms, ("gx", "gy"))
    all_partial = (
        lax.psum_scatter(
            grad_self_query.astype(jnp.bfloat16), "gx", scatter_dimension=0, tiled=True
        ).astype(jnp.float32),
        lax.psum_scatter(
            grad_self_key.astype(jnp.bfloat16), "gx", scatter_dimension=0, tiled=True
        ).astype(jnp.float32),
        lax.psum_scatter(
            grad_self_value.astype(jnp.bfloat16), "gx", scatter_dimension=0, tiled=True
        ).astype(jnp.float32),
        lax.psum_scatter(
            grad_self_out.astype(jnp.bfloat16), "gx", scatter_dimension=0, tiled=True
        ).astype(jnp.float32),
        lax.psum_scatter(
            grad_cross_query.astype(jnp.bfloat16), "gx", scatter_dimension=0, tiled=True
        ).astype(jnp.float32),
        lax.psum_scatter(
            grad_cross_key.astype(jnp.bfloat16), "gx", scatter_dimension=0, tiled=True
        ).astype(jnp.float32),
        lax.psum_scatter(
            grad_cross_value.astype(jnp.bfloat16), "gx", scatter_dimension=0, tiled=True
        ).astype(jnp.float32),
        lax.psum_scatter(
            grad_cross_out.astype(jnp.bfloat16), "gx", scatter_dimension=0, tiled=True
        ).astype(jnp.float32),
        lax.psum_scatter(
            grad_ffn_gate.astype(jnp.bfloat16), "gx", scatter_dimension=0, tiled=True
        ).astype(jnp.float32),
        lax.psum_scatter(
            grad_ffn_up.astype(jnp.bfloat16), "gx", scatter_dimension=0, tiled=True
        ).astype(jnp.float32),
        lax.psum_scatter(
            grad_ffn_out.astype(jnp.bfloat16), "gx", scatter_dimension=0, tiled=True
        ).astype(jnp.float32),
        lax.psum_scatter(
            grad_gain_self.astype(jnp.bfloat16), "gx", scatter_dimension=0, tiled=True
        ).astype(jnp.float32),
        lax.psum_scatter(
            grad_gain_cross.astype(jnp.bfloat16), "gx", scatter_dimension=0, tiled=True
        ).astype(jnp.float32),
        lax.psum_scatter(
            grad_gain_ffn.astype(jnp.bfloat16), "gx", scatter_dimension=0, tiled=True
        ).astype(jnp.float32),
    )
    g_sq, g_sk, g_sv, g_so, g_cq, g_ck, g_cv, g_co, g_fg, g_fu, g_fo, g_gs, g_gc, g_gf = (
        lax.psum_scatter(
            all_partial[0].astype(jnp.bfloat16), "gy", scatter_dimension=0, tiled=True
        ).astype(jnp.float32),
        lax.psum_scatter(
            all_partial[1].astype(jnp.bfloat16), "gy", scatter_dimension=0, tiled=True
        ).astype(jnp.float32),
        lax.psum_scatter(
            all_partial[2].astype(jnp.bfloat16), "gy", scatter_dimension=0, tiled=True
        ).astype(jnp.float32),
        lax.psum_scatter(
            all_partial[3].astype(jnp.bfloat16), "gy", scatter_dimension=0, tiled=True
        ).astype(jnp.float32),
        lax.psum_scatter(
            all_partial[4].astype(jnp.bfloat16), "gy", scatter_dimension=0, tiled=True
        ).astype(jnp.float32),
        lax.psum_scatter(
            all_partial[5].astype(jnp.bfloat16), "gy", scatter_dimension=0, tiled=True
        ).astype(jnp.float32),
        lax.psum_scatter(
            all_partial[6].astype(jnp.bfloat16), "gy", scatter_dimension=0, tiled=True
        ).astype(jnp.float32),
        lax.psum_scatter(
            all_partial[7].astype(jnp.bfloat16), "gy", scatter_dimension=0, tiled=True
        ).astype(jnp.float32),
        lax.psum_scatter(
            all_partial[8].astype(jnp.bfloat16), "gy", scatter_dimension=0, tiled=True
        ).astype(jnp.float32),
        lax.psum_scatter(
            all_partial[9].astype(jnp.bfloat16), "gy", scatter_dimension=0, tiled=True
        ).astype(jnp.float32),
        lax.psum_scatter(
            all_partial[10].astype(jnp.bfloat16), "gy", scatter_dimension=0, tiled=True
        ).astype(jnp.float32),
        lax.psum_scatter(
            all_partial[11].astype(jnp.bfloat16), "gy", scatter_dimension=0, tiled=True
        ).astype(jnp.float32),
        lax.psum_scatter(
            all_partial[12].astype(jnp.bfloat16), "gy", scatter_dimension=0, tiled=True
        ).astype(jnp.float32),
        lax.psum_scatter(
            all_partial[13].astype(jnp.bfloat16), "gy", scatter_dimension=0, tiled=True
        ).astype(jnp.float32),
    )
    return (
        output,
        grad_states,
        grad_encoded,
        g_sq,
        g_sk,
        g_sv,
        g_so,
        g_cq,
        g_ck,
        g_cv,
        g_co,
        g_fg,
        g_fu,
        g_fo,
        g_gs,
        g_gc,
        g_gf,
        grad_bucket_table,
    )


def solution(mesh):
    in_specs = (
        P(("gx", "gy"), None, None),
        P(("gx", "gy"), None, None),
        P(("gx", "gy"), None, None),
        P(("gx", "gy")),
        P(("gx", "gy")),
        P(("gx", "gy"), None),
        P(("gx", "gy"), None),
        P(("gx", "gy"), None),
        P(("gx", "gy"), None),
        P(("gx", "gy"), None),
        P(("gx", "gy"), None),
        P(("gx", "gy"), None),
        P(("gx", "gy"), None),
        P(("gx", "gy"), None),
        P(("gx", "gy"), None),
        P(("gx", "gy"), None),
        P(("gx", "gy")),
        P(("gx", "gy")),
        P(("gx", "gy")),
        P(),
    )
    out_specs = (
        P(("gx", "gy"), None, None),
        P(("gx", "gy"), None, None),
        P(("gx", "gy"), None, None),
        P(("gx", "gy"), None),
        P(("gx", "gy"), None),
        P(("gx", "gy"), None),
        P(("gx", "gy"), None),
        P(("gx", "gy"), None),
        P(("gx", "gy"), None),
        P(("gx", "gy"), None),
        P(("gx", "gy"), None),
        P(("gx", "gy"), None),
        P(("gx", "gy"), None),
        P(("gx", "gy"), None),
        P(("gx", "gy")),
        P(("gx", "gy")),
        P(("gx", "gy")),
        P(),
    )
    return jax.shard_map(
        per_device, mesh=mesh, in_specs=in_specs, out_specs=out_specs, check_vma=False
    )
```

profile of v0, /device:TPU:0, one launch (start us, length us, event | category | flops | bytes accessed | tf_op | source)
XLA Modules:
  0.0 1716.4 jit_solution(17993205301003196097)
XLA Ops:
  17.8 42.4 %all-reduce.9 = (bf16[768]{0:T(1024)(128)(2,1)S(1)}, bf16[768]{0:T(1024)(128)(2,1)S(1)}, bf16[768]{0:T(1024)(128)(2,1)S(1)}) all-reduce(bf16[768]{0:T(1024)(128)(2,1)S(1)} %dynamic-update-slice, bf16[768]{0:T(1024)(128)(2,1)S(1)} %dynamic-update-slice.1, bf16[768]{0:T(1024)(128)(2,1)S(1)} %dynamic-update-slice.2), channel_id=1, replica_groups=mesh['gx'=4,'gy'=8] {'gx','gy'}, use_global_device_ids=true, to_apply=%add | all-reduce | flops 2304 | bytes 9216
  60.3 8.5 fusion.6
  68.9 17.7 %copy.91 = f32[512,512,12]{0,1,2:T(8,128)} copy(f32[512,512,12]{1,2,0:T(8,128)} %fusion.6) | data formatting | bytes 25165824 | tf_op jit(solution)/shard_map/eri,ex->xri/dot_general | solution.py:243
  89.8 34.4 %all-gather.16.cloned.1.call-done = bf16[768,768]{1,0:T(8,128)(2,1)} async-done(((bf16[24,768]{1,0:T(8,128)(2,1)}), bf16[768,768]{1,0:T(8,128)(2,1)}) %all-gather.16.cloned.1.call-update) | async-done | bytes 1179664 | tf_op jit(solution)/shard_map/all_gather | solution.py:224
  128.7 51.6 %all-gather.12.cloned.1.call-done = bf16[768,768]{1,0:T(8,128)(2,1)} async-done(((bf16[24,768]{1,0:T(8,128)(2,1)}), bf16[768,768]{1,0:T(8,128)(2,1)}) %all-gather.12.cloned.1.call-update) | async-done | bytes 1179664 | tf_op jit(solution)/shard_map/all_gather | solution.py:225
  184.7 51.6 %all-gather.20.cloned.1.call-done = bf16[768,768]{1,0:T(8,128)(2,1)} async-done(((bf16[24,768]{1,0:T(8,128)(2,1)}), bf16[768,768]{1,0:T(8,128)(2,1)}) %all-gather.20.cloned.1.call-update) | async-done | bytes 1179664 | tf_op jit(solution)/shard_map/all_gather | solution.py:229
  239.5 52.7 %all-gather.24.cloned.1.call-done = bf16[768,768]{1,0:T(8,128)(2,1)} async-done(((bf16[24,768]{1,0:T(8,128)(2,1)}), bf16[768,768]{1,0:T(8,128)(2,1)}) %all-gather.24.cloned.1.call-update) | async-done | bytes 1179664 | tf_op jit(solution)/shard_map/all_gather | solution.py:228
  297.6 6.1 fusion.102
  311.6 36.6 %all-gather.18.cloned.1.call-done = bf16[768,768]{1,0:T(8,128)(2,1)} async-done(((bf16[24,768]{1,0:T(8,128)(2,1)}), bf16[768,768]{1,0:T(8,128)(2,1)}) %all-gather.18.cloned.1.call-update) | async-done | bytes 1179664 | tf_op jit(solution)/shard_map/all_gather | solution.py:226
  350.9 53.5 %all-gather.22.cloned.1.call-done = bf16[768,768]{1,0:T(8,128)(2,1)} async-done(((bf16[24,768]{1,0:T(8,128)(2,1)}), bf16[768,768]{1,0:T(8,128)(2,1)}) %all-gather.22.cloned.1.call-update) | async-done | bytes 1179664 | tf_op jit(solution)/shard_map/all_gather | solution.py:227
  421.7 38.7 %all-gather.26.cloned.1.call-done = bf16[768,768]{1,0:T(8,128)(2,1)} async-done(((bf16[24,768]{1,0:T(8,128)(2,1)}), bf16[768,768]{1,0:T(8,128)(2,1)}) %all-gather.26.cloned.1.call-update) | async-done | bytes 1179664 | tf_op jit(solution)/shard_map/all_gather | solution.py:230
  464.7 56.8 %all-gather.30.cloned.1.call-done = bf16[768,2048]{1,0:T(8,128)(2,1)} async-done(((bf16[24,2048]{1,0:T(8,128)(2,1)}), bf16[768,2048]{1,0:T(8,128)(2,1)}) %all-gather.30.cloned.1.call-update) | async-done | bytes 3145744 | tf_op jit(solution)/shard_map/all_gather | solution.py:232
  521.4 5.9 fusion.104
  527.3 54.8 %all-gather.28.cloned.1.call-done = bf16[768,2048]{1,0:T(8,128)(2,1)} async-done(((bf16[24,2048]{1,0:T(8,128)(2,1)}), bf16[768,2048]{1,0:T(8,128)(2,1)}) %all-gather.28.cloned.1.call-update) | async-done | bytes 3145744 | tf_op jit(solution)/shard_map/all_gather | solution.py:231
  582.2 6.4 fusion.103
  588.6 54.5 %all-gather.32.cloned.1.call-done = bf16[768,2048]{1,0:T(8,128)(2,1)} async-done(((bf16[24,2048]{1,0:T(8,128)(2,1)}), bf16[768,2048]{1,0:T(8,128)(2,1)}) %all-gather.32.cloned.1.call-update) | async-done | bytes 3145744 | tf_op jit(solution)/shard_map/all_gather | solution.py:233
  643.1 9.4 multiply_convert_fusion.2
  663.9 7.5 fusion.53
  676.8 9.2 multiply_reduce_fusion.1
  686.0 7.1 multiply_convert_fusion.1
  721.5 6.7 fusion.50
  731.2 6.3 multiply_reduce_fusion
  737.5 12.1 fusion.101
  786.4 27.9 %reduce-scatter.47.cloned.1.call-done = bf16[192,768]{1,0:T(8,128)(2,1)} async-done(((bf16[768,768]{1,0:T(8,128)(2,1)}), bf16[192,768]{1,0:T(8,128)(2,1)}) %reduce-scatter.47.cloned.1.call-update) | async-done | bytes 294928 | tf_op jit(solution)/shard_map/reduce_scatter | solution.py:400
  814.4 28.3 %reduce-scatter.43.cloned.1.call-done = bf16[192,768]{1,0:T(8,128)(2,1)} async-done(((bf16[768,768]{1,0:T(8,128)(2,1)}), bf16[192,768]{1,0:T(8,128)(2,1)}) %reduce-scatter.43.cloned.1.call-update) | async-done | bytes 294928 | tf_op jit(solution)/shard_map/reduce_scatter | solution.py:397
  842.8 28.1 %reduce-scatter.39.cloned.1.call-done = bf16[192,768]{1,0:T(8,128)(2,1)} async-done(((bf16[768,768]{1,0:T(8,128)(2,1)}), bf16[192,768]{1,0:T(8,128)(2,1)}) %reduce-scatter.39.cloned.1.call-update) | async-done | bytes 294928 | tf_op jit(solution)/shard_map/reduce_scatter | solution.py:394
  870.9 28.4 %reduce-scatter.35.cloned.1.call-done = bf16[192,768]{1,0:T(8,128)(2,1)} async-done(((bf16[768,768]{1,0:T(8,128)(2,1)}), bf16[192,768]{1,0:T(8,128)(2,1)}) %reduce-scatter.35.cloned.1.call-update) | async-done | bytes 294928 | tf_op jit(solution)/shard_map/reduce_scatter | solution.py:391
  899.4 40.3 %reduce-scatter.75.cloned.1.call-done = bf16[192,2048]{1,0:T(8,128)(2,1)} async-done(((bf16[768,2048]{1,0:T(8,128)(2,1)}), bf16[192,2048]{1,0:T(8,128)(2,1)}) %reduce-scatter.75.cloned.1.call-update) | async-done | bytes 786448
  948.5 5.8 all-reduce.11
  954.5 21.6 %all-reduce.10 = (bf16[192]{0:T(256)(128)(2,1)S(1)}, bf16[192]{0:T(256)(128)(2,1)S(1)}, bf16[192]{0:T(256)(128)(2,1)S(1)}) all-reduce(bf16[192]{0:T(256)(128)(2,1)S(1)} %dynamic-slice.11, bf16[192]{0:T(256)(128)(2,1)S(1)} %dynamic-slice.15, bf16[192]{0:T(256)(128)(2,1)S(1)} %dynamic-slice.19), channel_id=25, replica_groups=mesh['gx'=4,'gy'=8] {'gy'}, use_global_device_ids=true, to_apply=%region_36.37.clone | all-reduce | flops 576 | bytes 2304
  980.7 80.1 %while.3 = (s32[]{:T(128)}, f32[4,32,12]{1,2,0:T(8,128)S(1)}, s32[4]{0:T(128)S(1)}, s32[512,512]{1,0:T(8,128)}, f32[12,512,512]{1,2,0:T(8,128)}, /*index=5*/s32[]{:T(128)}, s32[]{:T(128)}, s32[]{:T(128)}) while((s32[]{:T(128)}, f32[4,32,12]{1,2,0:T(8,128)S(1)}, s32[4]{0:T(128)S(1)}, s32[512,512]{1,0:T(8,128)}, ...), condition=%wide.region_44.45_spmd.clone, body=%wide.region_43.44_spmd.clone.sunk | while | flops 304087040 | bytes 16523415 | solution.py:387
  984.2 5.4 constant_dynamic-slice_fusion.4
  995.0 6.1 fusion.181
  1015.2 6.1 fusion.181
  1024.8 5.4 constant_dynamic-slice_fusion.4
  1035.4 6.1 fusion.181
  1054.7 6.1 fusion.181
  1061.5 39.5 %psum.7 = f32[32,12]{0,1:T(8,128)} all-reduce(f32[32,12]{0,1:T(8,128)S(1)} %reduce_sum.161), channel_id=1, replica_groups=mesh['gx'=4,'gy'=8] {'gx','gy'}, use_global_device_ids=true, to_apply=%region_46.47 | all-reduce | flops 384 | bytes 3072 | tf_op jit(solution)/shard_map/psum | solution.py:389
  1112.2 32.5 %reduce-scatter.69.cloned.1.call-done = bf16[24,768]{1,0:T(8,128)(2,1)} async-done(((bf16[192,768]{1,0:T(8,128)(2,1)}), bf16[24,768]{1,0:T(8,128)(2,1)}) %reduce-scatter.69.cloned.1.call-update) | async-done | bytes 36880
  1146.4 59.8 %reduce-scatter.57.cloned.1.call-done = bf16[24,768]{1,0:T(8,128)(2,1)} async-done(((bf16[192,768]{1,0:T(8,128)(2,1)}), bf16[24,768]{1,0:T(8,128)(2,1)}) %reduce-scatter.57.cloned.1.call-update) | async-done | bytes 36880 | tf_op jit(solution)/shard_map/reduce_scatter | solution.py:456
  1207.6 59.9 %reduce-scatter.53.cloned.1.call-done = bf16[24,768]{1,0:T(8,128)(2,1)} async-done(((bf16[192,768]{1,0:T(8,128)(2,1)}), bf16[24,768]{1,0:T(8,128)(2,1)}) %reduce-scatter.53.cloned.1.call-update) | async-done | bytes 36880 | tf_op jit(solution)/shard_map/reduce_scatter | solution.py:447
  1268.9 59.8 %reduce-scatter.49.cloned.1.call-done = bf16[24,768]{1,0:T(8,128)(2,1)} async-done(((bf16[192,768]{1,0:T(8,128)(2,1)}), bf16[24,768]{1,0:T(8,128)(2,1)}) %reduce-scatter.49.cloned.1.call-update) | async-done | bytes 36880 | tf_op jit(solution)/shard_map/reduce_scatter | solution.py:444
  1330.1 60.1 %reduce-scatter.45.cloned.1.call-done = bf16[24,768]{1,0:T(8,128)(2,1)} async-done(((bf16[192,768]{1,0:T(8,128)(2,1)}), bf16[24,768]{1,0:T(8,128)(2,1)}) %reduce-scatter.45.cloned.1.call-update) | async-done | bytes 36880 | tf_op jit(solution)/shard_map/reduce_scatter | solution.py:441
  1391.6 60.0 %reduce-scatter.41.cloned.1.call-done = bf16[24,768]{1,0:T(8,128)(2,1)} async-done(((bf16[192,768]{1,0:T(8,128)(2,1)}), bf16[24,768]{1,0:T(8,128)(2,1)}) %reduce-scatter.41.cloned.1.call-update) | async-done | bytes 36880 | tf_op jit(solution)/shard_map/reduce_scatter | solution.py:438
  1453.0 59.9 %reduce-scatter.37.cloned.1.call-done = bf16[24,768]{1,0:T(8,128)(2,1)} async-done(((bf16[192,768]{1,0:T(8,128)(2,1)}), bf16[24,768]{1,0:T(8,128)(2,1)}) %reduce-scatter.37.cloned.1.call-update) | async-done | bytes 36880 | tf_op jit(solution)/shard_map/reduce_scatter | solution.py:435
  1514.3 63.8 %reduce-scatter.77.cloned.1.call-done = bf16[24,2048]{1,0:T(8,128)(2,1)} async-done(((bf16[192,2048]{1,0:T(8,128)(2,1)}), bf16[24,2048]{1,0:T(8,128)(2,1)}) %reduce-scatter.77.cloned.1.call-update) | async-done | bytes 98320
  1580.1 62.8 %reduce-scatter.65.cloned.1.call-done = bf16[24,2048]{1,0:T(8,128)(2,1)} async-done(((bf16[192,2048]{1,0:T(8,128)(2,1)}), bf16[24,2048]{1,0:T(8,128)(2,1)}) %reduce-scatter.65.cloned.1.call-update) | async-done | bytes 98320 | tf_op jit(solution)/shard_map/reduce_scatter | solution.py:462
  1644.5 63.4 %reduce-scatter.61.cloned.1.call-done = bf16[24,2048]{1,0:T(8,128)(2,1)} async-done(((bf16[192,2048]{1,0:T(8,128)(2,1)}), bf16[24,2048]{1,0:T(8,128)(2,1)}) %reduce-scatter.61.cloned.1.call-update) | async-done | bytes 98320 | tf_op jit(solution)/shard_map/reduce_scatter | solution.py:459
  (306 shorter events, 223.0 us)
Async XLA Ops:
  7.2 229.1 %copy-start = (bf16[1,512,768]{2,1,0:T(8,128)(2,1)S(1)}, bf16[1,512,768]{2,1,0:T(8,128)(2,1)}, u32[]{:S(2)}) copy-start(bf16[1,512,768]{2,1,0:T(8,128)(2,1)} %param.23) | copy-start | bytes 2359300
  7.2 53.1 %copy-start.45 = (bf16[32,12]{0,1:T(8,128)(2,1)S(1)}, bf16[32,12]{0,1:T(8,128)(2,1)}, u32[]{:S(2)}) copy-start(bf16[32,12]{0,1:T(8,128)(2,1)} %param.41) | copy-start | bytes 2308
  7.3 79.3 %all-gather.14.cloned.1.call-start = ((), (), s32[]{:S(2)}) async-start(), calls=%async_computation.23 | async-start | bytes 1216512 | tf_op jit(solution)/shard_map/all_gather | solution.py:223
  8.0 116.2 %all-gather.16.cloned.1.call-start = ((), (), s32[]{:S(2)}) async-start(), calls=%async_computation.24 | async-start | bytes 1216512 | tf_op jit(solution)/shard_map/all_gather | solution.py:224
  8.7 171.6 %all-gather.12.cloned.1.call-start = ((), (), s32[]{:S(2)}) async-start(), calls=%async_computation.22 | async-start | bytes 1216512 | tf_op jit(solution)/shard_map/all_gather | solution.py:225
  9.5 226.8 %all-gather.20.cloned.1.call-start = ((), (), s32[]{:S(2)}) async-start(), calls=%async_computation.26 | async-start | bytes 1216512 | tf_op jit(solution)/shard_map/all_gather | solution.py:229
  10.1 282.2 %all-gather.24.cloned.1.call-start = ((), (), s32[]{:S(2)}) async-start(), calls=%async_computation.28 | async-start | bytes 1216512 | tf_op jit(solution)/shard_map/all_gather | solution.py:228
  10.6 337.6 %all-gather.18.cloned.1.call-start = ((), (), s32[]{:S(2)}) async-start(), calls=%async_computation.25 | async-start | bytes 1216512 | tf_op jit(solution)/shard_map/all_gather | solution.py:226
  11.2 393.1 %all-gather.22.cloned.1.call-start = ((), (), s32[]{:S(2)}) async-start(), calls=%async_computation.27 | async-start | bytes 1216512 | tf_op jit(solution)/shard_map/all_gather | solution.py:227
  12.0 448.5 %all-gather.26.cloned.1.call-start = ((), (), s32[]{:S(2)}) async-start(), calls=%async_computation.29 | async-start | bytes 1216512 | tf_op jit(solution)/shard_map/all_gather | solution.py:230
  12.7 508.7 %all-gather.30.cloned.1.call-start = ((), (), s32[]{:S(2)}) async-start(), calls=%async_computation.31 | async-start | bytes 3244032 | tf_op jit(solution)/shard_map/all_gather | solution.py:232
  13.5 568.7 %all-gather.28.cloned.1.call-start = ((), (), s32[]{:S(2)}) async-start(), calls=%async_computation.30 | async-start | bytes 3244032 | tf_op jit(solution)/shard_map/all_gather | solution.py:231
  14.0 629.0 %all-gather.32.cloned.1.call-start = ((), (), s32[]{:S(2)}) async-start(), calls=%async_computation.32 | async-start | bytes 3244032 | tf_op jit(solution)/shard_map/all_gather | solution.py:233
  14.8 769.0 %reduce-scatter.71.cloned.1.call-start = ((), (), s32[]{:S(2)}) async-start(), calls=%async_computation.51 | async-start | bytes 1474560
  15.4 53.5 %copy-start.6 = (s32[512,512]{1,0:T(8,128)}, s32[512,512]{1,0:T(8,128)S(1)}, u32[]{:S(2)}) copy-start(s32[512,512]{1,0:T(8,128)S(1)} %compare_select_fusion) | copy-start | bytes 3145732
  17.0 51.9 %copy-start.43 = (f32[512]{0:T(512)}, f32[512]{0:T(512)S(1)}, u32[]{:S(2)}) copy-start(f32[512]{0:T(512)S(1)} %fusion.40) | copy-start | bytes 6148
  127.2 53.1 %copy-start.16 = (bf16[1,512,768]{2,1,0:T(8,128)(2,1)S(1)}, bf16[1,512,768]{2,1,0:T(8,128)(2,1)}, u32[]{:S(2)}) copy-start(bf16[1,512,768]{2,1,0:T(8,128)(2,1)} %param.22) | copy-start | bytes 2359300
  184.7 120.8 %copy-start.25 = (bf16[512,768]{0,1:T(8,128)(2,1)}, bf16[512,768]{0,1:T(8,128)(2,1)S(1)}, u32[]{:S(2)}) copy-start(bf16[512,768]{0,1:T(8,128)(2,1)S(1)} %copy.88) | copy-start | bytes 2359300
  350.8 56.5 %copy-start.11 = (f32[512,768]{1,0:T(8,128)}, f32[512,768]{1,0:T(8,128)S(1)}, u32[]{:S(2)}) copy-start(f32[512,768]{1,0:T(8,128)S(1)} %get-tuple-element.315) | copy-start | bytes 4718596
  463.3 191.0 %copy-start.9 = (f32[512,768]{1,0:T(8,128)}, f32[512,768]{1,0:T(8,128)S(1)}, u32[]{:S(2)}) copy-start(f32[512,768]{1,0:T(8,128)S(1)} %get-tuple-element.319) | copy-start | bytes 4718596
  659.9 41.0 %copy-start.7 = (f32[512,768]{1,0:T(8,128)}, f32[512,768]{1,0:T(8,128)S(1)}, u32[]{:S(2)}) copy-start(f32[512,768]{1,0:T(8,128)S(1)} %fusion.44) | copy-start | bytes 4718596
  676.5 108.0 %reduce-scatter.67.cloned.1.call-start = ((), (), s32[]{:S(2)}) async-start(), calls=%async_computation.49 | async-start | bytes 1474560
  700.9 84.2 %reduce-scatter.55.cloned.1.call-start = ((), (), s32[]{:S(2)}) async-start(), calls=%async_computation.43 | async-start | bytes 1474560 | tf_op jit(solution)/shard_map/reduce_scatter | solution.py:412
  704.0 82.2 %reduce-scatter.51.cloned.1.call-start = ((), (), s32[]{:S(2)}) async-start(), calls=%async_computation.41 | async-start | bytes 1474560 | tf_op jit(solution)/shard_map/reduce_scatter | solution.py:403
  711.0 103.4 %reduce-scatter.47.cloned.1.call-start = ((), (), s32[]{:S(2)}) async-start(), calls=%async_computation.39 | async-start | bytes 1474560 | tf_op jit(solution)/shard_map/reduce_scatter | solution.py:400
  716.9 125.8 %reduce-scatter.43.cloned.1.call-start = ((), (), s32[]{:S(2)}) async-start(), calls=%async_computation.37 | async-start | bytes 1474560 | tf_op jit(solution)/shard_map/reduce_scatter | solution.py:397
  731.2 139.7 %reduce-scatter.39.cloned.1.call-start = ((), (), s32[]{:S(2)}) async-start(), calls=%async_computation.35 | async-start | bytes 1474560 | tf_op jit(solution)/shard_map/reduce_scatter | solution.py:394
  755.2 144.2 %reduce-scatter.35.cloned.1.call-start = ((), (), s32[]{:S(2)}) async-start(), calls=%async_computation.33 | async-start | bytes 1474560 | tf_op jit(solution)/shard_map/reduce_scatter | solution.py:391
  762.1 177.6 %reduce-scatter.75.cloned.1.call-start = ((), (), s32[]{:S(2)}) async-start(), calls=%async_computation.53 | async-start | bytes 3932160
  772.4 208.0 %reduce-scatter.63.cloned.1.call-start = ((), (), s32[]{:S(2)}) async-start(), calls=%async_computation.47 | async-start | bytes 3932160 | tf_op jit(solution)/shard_map/reduce_scatter | solution.py:418
  778.6 282.2 %reduce-scatter.59.cloned.1.call-start = ((), (), s32[]{:S(2)}) async-start(), calls=%async_computation.45 | async-start | bytes 3932160 | tf_op jit(solution)/shard_map/reduce_scatter | solution.py:415
  783.7 326.8 %reduce-scatter.73.cloned.1.call-start = ((), (), s32[]{:S(2)}) async-start(), calls=%async_computation.52 | async-start | bytes 331776
  783.8 156.0 %copy-start.55 = (u32[32]{0:T(128)S(1)}, u32[32]{0:T(128)}, u32[]{:S(2)}) copy-start(u32[32]{0:T(128)} %constant.210) | copy-start | bytes 388
  783.8 156.6 %copy-start.54 = (u32[32]{0:T(128)S(1)}, u32[32]{0:T(128)}, u32[]{:S(2)}) copy-start(u32[32]{0:T(128)} %constant.206) | copy-start | bytes 388
  783.8 158.5 %copy-start.42 = (bf16[12,64,512]{2,1,0:T(8,128)(2,1)S(1)}, bf16[12,64,512]{2,1,0:T(8,128)(2,1)}, u32[]{:S(2)}) copy-start(bf16[12,64,512]{2,1,0:T(8,128)(2,1)} %copy-done.41) | copy-start | bytes 2359300
  784.5 360.3 %reduce-scatter.69.cloned.1.call-start = ((), (), s32[]{:S(2)}) async-start(), calls=%async_computation.50 | async-start | bytes 331776
  785.0 421.2 %reduce-scatter.57.cloned.1.call-start = ((), (), s32[]{:S(2)}) async-start(), calls=%async_computation.44 | async-start | bytes 331776 | tf_op jit(solution)/shard_map/reduce_scatter | solution.py:456
  785.8 481.7 %reduce-scatter.53.cloned.1.call-start = ((), (), s32[]{:S(2)}) async-start(), calls=%async_computation.42 | async-start | bytes 331776 | tf_op jit(solution)/shard_map/reduce_scatter | solution.py:447
  786.4 542.3 %reduce-scatter.49.cloned.1.call-start = ((), (), s32[]{:S(2)}) async-start(), calls=%async_computation.40 | async-start | bytes 331776 | tf_op jit(solution)/shard_map/reduce_scatter | solution.py:444
  814.4 575.8 %reduce-scatter.45.cloned.1.call-start = ((), (), s32[]{:S(2)}) async-start(), calls=%async_computation.38 | async-start | bytes 331776 | tf_op jit(solution)/shard_map/reduce_scatter | solution.py:441
  842.7 608.9 %reduce-scatter.41.cloned.1.call-start = ((), (), s32[]{:S(2)}) async-start(), calls=%async_computation.36 | async-start | bytes 331776 | tf_op jit(solution)/shard_map/reduce_scatter | solution.py:438
  870.9 642.0 %reduce-scatter.37.cloned.1.call-start = ((), (), s32[]{:S(2)}) async-start(), calls=%async_computation.34 | async-start | bytes 331776 | tf_op jit(solution)/shard_map/reduce_scatter | solution.py:435
  899.4 678.7 %reduce-scatter.77.cloned.1.call-start = ((), (), s32[]{:S(2)}) async-start(), calls=%async_computation.54 | async-start | bytes 884736
  939.7 703.1 %reduce-scatter.65.cloned.1.call-start = ((), (), s32[]{:S(2)}) async-start(), calls=%async_computation.48 | async-start | bytes 884736 | tf_op jit(solution)/shard_map/reduce_scatter | solution.py:462
  946.1 30.6 %copy-start.44 = (f32[512]{0:T(512)S(1)}, f32[512]{0:T(512)}, u32[]{:S(2)}) copy-start(f32[512]{0:T(512)} %copy-done.43) | copy-start | bytes 6148
  980.5 727.4 %reduce-scatter.61.cloned.1.call-start = ((), (), s32[]{:S(2)}) async-start(), calls=%async_computation.46 | async-start | bytes 884736 | tf_op jit(solution)/shard_map/reduce_scatter | solution.py:459
  980.7 120.3 %copy-start.40 = (bf16[12,64,512]{2,1,0:T(8,128)(2,1)S(1)}, bf16[12,64,512]{2,1,0:T(8,128)(2,1)}, u32[]{:S(2)}) copy-start(bf16[12,64,512]{2,1,0:T(8,128)(2,1)} %copy-done.39) | copy-start | bytes 2359300
  1111.4 598.0 %copy-start.1 = (bf16[1,512,768]{2,1,0:T(8,128)(2,1)S(1)}, bf16[1,512,768]{2,1,0:T(8,128)(2,1)}, u32[]{:S(2)}) copy-start(bf16[1,512,768]{2,1,0:T(8,128)(2,1)} %param.23) | copy-start | bytes 2359300
  (44 other events, 159.0 us)
Sparse Core Ops, SparseCore 0:
  11.1 57.0 all-gather.13
  71.2 52.9 all-gather.15
  127.2 53.0 all-gather.11
  183.2 53.0 all-gather.19
  239.1 53.0 all-gather.23
  295.1 53.0 all-gather.17
  351.2 53.0 all-gather.21
  407.3 53.0 all-gather.25
  463.4 57.9 all-gather.29
  524.3 57.8 all-gather.27
  585.2 57.8 all-gather.31
  676.7 24.5 reduce-scatter.70
  703.9 25.7 reduce-scatter.66
  732.1 25.7 reduce-scatter.54
  760.4 25.6 reduce-scatter.50
  788.6 25.7 reduce-scatter.46
  816.9 25.7 reduce-scatter.42
  845.1 25.7 reduce-scatter.38
  873.6 25.7 reduce-scatter.34
  901.7 37.9 reduce-scatter.74
  942.4 37.9 reduce-scatter.62
  983.0 37.9 reduce-scatter.58
  1024.6 58.8 reduce-scatter.72
  1086.9 57.7 reduce-scatter.68
  1148.4 57.7 reduce-scatter.56
  1209.7 57.7 reduce-scatter.52
  1271.0 57.6 reduce-scatter.48
  1332.3 57.8 reduce-scatter.44
  1393.8 57.6 reduce-scatter.40
  1455.1 57.7 reduce-scatter.36
  1516.5 61.5 reduce-scatter.76
  1581.4 61.4 reduce-scatter.64
  1646.4 61.3 reduce-scatter.60
where the time goes:
time: 1720 us
  waiting for transfers between devices  1230 us (72%)
  matrix products  190 us (11%)
  local copies, waits for them, and re-layouts  114 us (7%)
  blocking collectives  109 us (6%)
  other arithmetic  42 us (2%)
  between operations  18.2 us (1%)
    unnamed x39, waiting for transfers between devices  146 us
    unnamed x3, blocking collectives  69.8 us
    reduce_scatter x1, waiting for transfers between devices, per_device(): lax.psum_scatter(all_partial[8].astype(jnp.bfloat16), 'gy', scatter_dimen...  63.4 us
    reduce_scatter x1, waiting for transfers between devices, per_device(): lax.psum_scatter(all_partial[9].astype(jnp.bfloat16), 'gy', scatter_dimen...  62.8 us
    reduce_scatter x1, waiting for transfers between devices, per_device(): lax.psum_scatter(all_partial[2].astype(jnp.bfloat16), 'gy', scatter_dimen...  60.1 us
    reduce_scatter x1, waiting for transfers between devices, per_device(): lax.psum_scatter(all_partial[1].astype(jnp.bfloat16), 'gy', scatter_dimen...  60 us
    reduce_scatter x1, waiting for transfers between devices, per_device(): lax.psum_scatter(all_partial[4].astype(jnp.bfloat16), 'gy', scatter_dimen...  59.9 us
    reduce_scatter x1, waiting for transfers between devices, per_device(): lax.psum_scatter(all_partial[0].astype(jnp.bfloat16), 'gy', scatter_dimen...  59.9 us
  transfers between devices with their start and end apart: 33, of which 27 were waited for; matrix products, arithmetic and copies ran while one was open for 17% of the time, Pallas kernels for 0%

commit v1 on v0

v1 whole, which is shorter than its diff:
```python
import math

import jax
import jax.numpy as jnp
import numpy as np
from jax import lax
from jax.sharding import PartitionSpec as P

H = 12
HD = 64
NB = 32

norm_eps = 1e-06
masked_score = -1000000000.0
bucket_edges = [int(math.ceil(16 * 8 ** (power / 16.0))) for power in range(1, 16)]

bf16 = jnp.bfloat16
f32 = jnp.float32


def buckets_of(length):
    places = jnp.arange(length, dtype=jnp.int32)
    distance = jnp.maximum(places[:, None] - places[None, :], 0)
    counted = jnp.zeros_like(distance)
    for edge in bucket_edges:
        counted = counted + (distance >= edge).astype(jnp.int32)
    return jnp.where(distance < 16, distance, 16 + counted)


class Cube:
    def __init__(self, mesh):
        self.nx, self.ny = mesh.shape["gx"], mesh.shape["gy"]
        self.n = self.nx * self.ny
        self.core, self.y, self.x = ("gx", 1), ("gx", 2), ("gy", 1)
        self.rest = []
        bit = self.ny // 2
        while bit > 1:
            self.rest.append(("gy", bit))
            bit //= 2
        bit = self.nx // 2
        while bit > 2:
            self.rest.append(("gx", bit))
            bit //= 2

    def send(self, value, step):
        axis, bit = step
        size = self.nx if axis == "gx" else self.ny
        return lax.ppermute(value, axis, [(i, i ^ bit) for i in range(size)])

    def owners(self):
        mask_x, mask_y = np.zeros(self.n, np.int32), np.zeros(self.n, np.int32)
        for place in range(self.n):
            steps = []
            inner, block = place % (self.n // 8), (place // (self.n // 8)) % 4
            for at, step in enumerate(self.rest):
                if (inner >> at) & 1:
                    steps.append(step)
            if block & 1:
                steps.append(self.x)
            if block & 2:
                steps.append(self.y)
            if place >= self.n // 2:
                steps.append(self.core)
            for axis, bit in steps:
                if axis == "gx":
                    mask_x[place] ^= bit
                else:
                    mask_y[place] ^= bit
        gx, gy = lax.axis_index("gx"), lax.axis_index("gy")
        return (gx ^ jnp.asarray(mask_x)) * self.ny + (gy ^ jnp.asarray(mask_y))

    def permutation(self, width):
        rows = width // self.n
        feature = (self.owners()[:, None] * rows + jnp.arange(rows, dtype=jnp.int32)).reshape(1, width)
        return (jnp.arange(width, dtype=jnp.int32)[:, None] == feature).astype(bf16)

    def gather(self, packed):
        own = packed
        for step in self.rest:
            own = jnp.concatenate([own, self.send(own, step)], axis=0)
        half = own.shape[0] // 2
        over_x = self.send(own, self.x)
        over_y = self.send(own, self.y)
        far_one = self.send(over_y[:half], self.x)
        far_two = self.send(over_x[half:], self.y)
        pieces = [own, over_x, over_y, far_one, far_two]
        return pieces + [self.send(piece, self.core) for piece in pieces]

    def reduce(self, low, high):
        total = low + self.send(high, self.core)
        size = total.shape[0] // 4
        half = size // 2
        own, to_x, to_y, far = (total[i * size : (i + 1) * size] for i in range(4))
        got_y = self.send(far[:half], self.x)
        got_x = self.send(far[half:], self.y)
        to_y = jnp.concatenate([to_y[:half] + got_y, to_y[half:]], axis=0)
        to_x = jnp.concatenate([to_x[:half], to_x[half:] + got_x], axis=0)
        own = own + self.send(to_x, self.x) + self.send(to_y, self.y)
        for step in reversed(self.rest):
            half = own.shape[0] // 2
            own = own[:half] + self.send(own[half:], step)
        return own

    def all_sum(self, value):
        for step in [self.core, self.x, self.y] + self.rest:
            value = value + self.send(value, step)
        return value


def times(left, right):
    return jnp.dot(left, right, preferred_element_type=f32)


def times_t(left, right):
    return lax.dot_general(left, right, (((1,), (1,)), ((), ())), preferred_element_type=f32)


def inner_t(left, right):
    return lax.dot_general(left, right, (((0,), (0,)), ((), ())), preferred_element_type=f32)


def norm(values, gain):
    return values * lax.rsqrt(jnp.mean(values * values, axis=-1, keepdims=True) + norm_eps) * gain


def norm_back(values, gain, d_normed):
    normed, pullback = jax.vjp(norm, values, gain)
    return pullback(d_normed)


def gated_unit(first, second):
    return jax.nn.gelu(first, approximate=True) * second


def gated_back(gate_pre, up_pre, d_gated):
    gated, pullback = jax.vjp(gated_unit, gate_pre, up_pre)
    return pullback(d_gated)


def heads(v):
    return v.reshape(v.shape[0], H, HD)


def attend_forward(q, k, v, bias, allowed):
    scores = jnp.einsum("qhd,khd->hqk", heads(q), heads(k), preferred_element_type=f32) + bias
    scores = jnp.where(allowed[None], scores, masked_score)
    highest = jnp.max(scores, axis=-1, keepdims=True)
    expo = jnp.exp(scores - highest)
    probs = (expo / jnp.sum(expo, axis=-1, keepdims=True)).astype(bf16)
    mixed = jnp.einsum("hqk,khd->qhd", probs, heads(v), preferred_element_type=f32)
    return mixed.reshape(q.shape).astype(bf16), probs


def attend_backward(q, k, v, probs, d_mixed):
    d_heads = heads(d_mixed)
    d_probs = jnp.einsum("qhd,khd->hqk", d_heads, heads(v), preferred_element_type=f32)
    d_v = jnp.einsum("hqk,qhd->khd", probs, d_heads, preferred_element_type=f32)
    p = probs.astype(f32)
    d_scores = (p * (d_probs - jnp.sum(p * d_probs, axis=-1, keepdims=True))).astype(bf16)
    d_q = jnp.einsum("hqk,khd->qhd", d_scores, heads(k), preferred_element_type=f32)
    d_k = jnp.einsum("hqk,qhd->khd", d_scores, heads(q), preferred_element_type=f32)
    return (
        d_q.reshape(q.shape).astype(bf16),
        d_k.reshape(q.shape).astype(bf16),
        d_v.reshape(q.shape).astype(bf16),
        d_scores,
    )


def layer(
    cube,
    states,
    encoded,
    cotangent,
    dec_lens,
    enc_lens,
    self_query,
    self_key,
    self_value,
    self_out,
    cross_query,
    cross_key,
    cross_value,
    cross_out,
    ffn_gate,
    ffn_up,
    ffn_out,
    gain_self,
    gain_cross,
    gain_ffn,
    table,
):
    rows, length, width = states.shape
    inner, hidden = self_query.shape[1], ffn_gate.shape[1]
    gains = jnp.stack([gain_self, gain_cross, gain_ffn], axis=1)
    gains = jnp.pad(gains, ((0, 0), (0, 125)))

    def collect(*parts):
        return jnp.concatenate(cube.gather(jnp.concatenate(parts, axis=1)), axis=0)

    first = collect(gains, self_query, self_key, self_value, self_out)
    second = collect(cross_query, cross_key, cross_value, cross_out)
    third = collect(ffn_gate, ffn_up)
    w_down = collect(ffn_out)
    gain_rows = first[:, :3].astype(f32).T
    g_self, g_cross, g_ffn = gain_rows[0:1], gain_rows[1:2], gain_rows[2:3]
    w_qkv, w_so = first[:, 128 : 128 + 3 * inner], first[:, 128 + 3 * inner :]
    c_q, c_kv, c_o = second[:, :inner], second[:, inner : 3 * inner], second[:, 3 * inner :]
    w_gu = third

    perm = cube.permutation(width)
    inputs = times(states[0], perm)
    enc = times(encoded[0], perm).astype(bf16)
    cot = times(cotangent[0], perm).astype(bf16)

    buckets = buckets_of(length)
    ids = jnp.arange(NB, dtype=jnp.int32)
    indicator = (buckets[None] == ids[:, None, None]).astype(bf16)
    bias = jnp.einsum("eri,ex->xri", indicator, table, preferred_element_type=f32)
    places = jnp.arange(length, dtype=jnp.int32)
    self_mask = (places[None, :] <= places[:, None]) & (places[None, :] < dec_lens[0])
    cross_mask = jnp.broadcast_to((places < enc_lens[0])[None, :], (length, length))

    normed_one = norm(inputs, g_self).astype(bf16)
    qkv = times(normed_one, w_qkv).astype(bf16)
    q1, k1, v1 = qkv[:, :inner], qkv[:, inner : 2 * inner], qkv[:, 2 * inner :]
    mixed_one, probs_one = attend_forward(q1, k1, v1, bias, self_mask)
    hidden_one = inputs + times_t(mixed_one, w_so)
    normed_two = norm(hidden_one, g_cross).astype(bf16)
    q2 = times(normed_two, c_q).astype(bf16)
    kv2 = times(enc, c_kv).astype(bf16)
    k2, v2 = kv2[:, :inner], kv2[:, inner:]
    mixed_two, probs_two = attend_forward(q2, k2, v2, 0.0, cross_mask)
    hidden_two = hidden_one + times_t(mixed_two, c_o)
    normed_three = norm(hidden_two, g_ffn).astype(bf16)
    pre = times(normed_three, w_gu)
    gate_pre, up_pre = pre[:, :hidden], pre[:, hidden:]
    gated = gated_unit(gate_pre, up_pre).astype(bf16)
    result = hidden_two + times_t(gated, w_down)
    output = times_t(result.astype(bf16), perm).astype(bf16)

    def give(*parts):
        half = width // 2
        low = jnp.concatenate([part[:half].astype(bf16) for part in parts], axis=1)
        high = jnp.concatenate([part[half:].astype(bf16) for part in parts], axis=1)
        return cube.reduce(low, high).astype(f32)

    grad_fo = give(inner_t(cot, gated))
    d_gated = times(cot, w_down)
    d_gate, d_up = gated_back(gate_pre, up_pre, d_gated)
    d_gu = jnp.concatenate([d_gate.astype(bf16), d_up.astype(bf16)], axis=1)
    grad_gu = give(inner_t(normed_three, d_gu))
    d_normed_three = times_t(d_gu, w_gu)
    d_hidden_two, grad_gf = norm_back(hidden_two, g_ffn, d_normed_three)
    d_hidden_two = d_hidden_two + cot.astype(f32)
    d_attn_two = d_hidden_two.astype(bf16)
    grad_co = inner_t(d_attn_two, mixed_two)
    d_mixed_two = times(d_attn_two, c_o).astype(bf16)
    d_q2, d_k2, d_v2, _ = attend_backward(q2, k2, v2, probs_two, d_mixed_two)
    d_kv2 = jnp.concatenate([d_k2, d_v2], axis=1)
    grad_c = give(grad_co, inner_t(normed_two, d_q2), inner_t(enc, d_kv2))
    d_normed_two = times_t(d_q2, c_q)
    grad_enc = times_t(times_t(d_kv2, c_kv).astype(bf16), perm).astype(bf16)
    d_hidden_one, grad_gc = norm_back(hidden_one, g_cross, d_normed_two)
    d_hidden_one = d_hidden_one + d_hidden_two
    d_attn_one = d_hidden_one.astype(bf16)
    grad_so = inner_t(d_attn_one, mixed_one)
    d_mixed_one = times(d_attn_one, w_so).astype(bf16)
    d_q1, d_k1, d_v1, d_s1 = attend_backward(q1, k1, v1, probs_one, d_mixed_one)
    table_part = jnp.einsum("hri,eri->eh", d_s1, indicator, preferred_element_type=f32)
    grad_table = cube.all_sum(table_part)
    d_qkv = jnp.concatenate([d_q1, d_k1, d_v1], axis=1)
    d_normed_one = times_t(d_qkv, w_qkv)
    d_inputs, grad_gs = norm_back(inputs, g_self, d_normed_one)
    grad_states = times_t((d_inputs + d_hidden_one).astype(bf16), perm).astype(bf16)
    grad_gains = jnp.pad(jnp.concatenate([grad_gs, grad_gc, grad_gf], axis=0).T, ((0, 0), (0, 125)))
    grad_s = give(grad_gains, grad_so, inner_t(normed_one, d_qkv))
    return (
        output[None],
        grad_states[None],
        grad_enc[None],
        grad_s[:, 128 + inner : 128 + 2 * inner],
        grad_s[:, 128 + 2 * inner : 128 + 3 * inner],
        grad_s[:, 128 + 3 * inner :],
        grad_s[:, 128 : 128 + inner],
        grad_c[:, inner : 2 * inner],
        grad_c[:, 2 * inner : 3 * inner],
        grad_c[:, 3 * inner :],
        grad_c[:, :inner],
        grad_gu[:, :hidden],
        grad_gu[:, hidden:],
        grad_fo,
        grad_s[:, 0],
        grad_s[:, 1],
        grad_s[:, 2],
        grad_table,
    )


def solution(mesh):
    cube = Cube(mesh)
    both = ("gx", "gy")
    row, flat, one = P(both, None, None), P(both, None), P(both)
    in_specs = (row, row, row, one, one) + (flat,) * 11 + (one,) * 3 + (P(),)
    out_specs = (row, row, row) + (flat,) * 11 + (one,) * 3 + (P(),)

    def per_device(*args):
        return layer(cube, *args)

    return jax.shard_map(per_device, mesh=mesh, in_specs=in_specs, out_specs=out_specs, check_vma=False)
```

time: 1720 us -> 553 us (0.32)
  waiting for transfers between devices: 1230 us -> 137 us
  blocking collectives: 109 us -> 0 us
  starting transfers between devices: 2.26 us -> 70.2 us
  local copies, waits for them, and re-layouts: 114 us -> 92.5 us
  other arithmetic: 42 us -> 62.9 us
    reduce_scatter x16 -> x0, waiting for transfers between devices: 602 us -> none  [the longest x1 63.4 us: per_device(): lax.psum_scatter(all_partial[8].astype(jnp.bfloat16), 'gy', scatter_dimen...]
    all_gather x11 -> x0, waiting for transfers between devices: 485 us -> none  [the longest x1 56.8 us: per_device(): lax.all_gather(ffn_up, ('gx', 'gy'), axis=0, tiled=True)]
    unnamed x39 -> x0, waiting for transfers between devices: 146 us -> none
    ppermute x0 -> x77, waiting for transfers between devices: none -> 137 us  [send(): return lax.ppermute(value, axis, [(i, i ^ bit) for i in range(size)])]
    ppermute x0 -> x77, starting transfers between devices: none -> 70.2 us  [send(): return lax.ppermute(value, axis, [(i, i ^ bit) for i in range(size)])]
    unnamed x3 -> x0, blocking collectives: 69.8 us -> none
    dynamic_slice x16 -> x0, local copies, waits for them, and re-layouts: 48 us -> none  [the longest x8 41.7 us: bucket_block(): part = lax.dynamic_slice_in_dim(score_sum, start, block, 1)]
    dot_general x28 -> x22, matrix products: 134 us -> 91.4 us  [the longest x10 32.8 us: times(): return jnp.dot(left, right, preferred_element_type=f32)]
  transfers between devices with their start and end apart: 33 -> 77, of which waited for: 27 -> 29; matrix products, arithmetic and copies ran while one was open for 17% -> 37% of each run, Pallas kernels for 0% -> 0%
where the time goes in v1:
time: 553 us; the launch traced here: 546 us
  matrix products  179 us (32%)
  waiting for transfers between devices  137 us (25%)
  local copies, waits for them, and re-layouts  92.5 us (17%)
  starting transfers between devices  70.2 us (13%)
  other arithmetic  62.9 us (11%)
    ppermute x77, waiting for transfers between devices, send(): return lax.ppermute(value, axis, [(i, i ^ bit) for i in range(size)])  137 us
    ppermute x77, starting transfers between devices, send(): return lax.ppermute(value, axis, [(i, i ^ bit) for i in range(size)])  70.2 us
    unnamed x201, local copies, waits for them, and re-layouts  48.1 us
    dot_general x8, matrix products, times_t(): lax.dot_general(left, right, (((1,), (1,)), ((), ())), preferred_element_...  34 us
    dot_general x10, matrix products, times(): return jnp.dot(left, right, preferred_element_type=f32)  32.8 us
    sub x2, matrix products, attend_forward(): expo = jnp.exp(scores - highest)  30.8 us
    dot_general x7, matrix products, inner_t(): lax.dot_general(left, right, (((0,), (0,)), ((), ())), preferred_element_...  22.4 us
    convert_element_type x2, other arithmetic, attend_forward(): probs = (expo / jnp.sum(expo, axis=-1, keepdims=True)).astype(bf16)  18.2 us
  transfers between devices with their start and end apart: 77, of which 29 were waited for; matrix products, arithmetic and copies ran while one was open for 37% of the time, Pallas kernels for 0%

profile of v1, /device:TPU:0, one launch (start us, length us, event | category | flops | bytes accessed | tf_op | source)
XLA Modules:
  0.0 545.6 jit_solution(17514075385623724155)
XLA Ops:
  0.7 4.1 collective-permute-start.33
  34.5 8.7 %fusion.3 = f32[512,512,12]{0,2,1:T(8,128)} fusion(s32[512,512]{0,1:T(8,128)S(1)} %compare_select_fusion, bf16[32,12]{0,1:T(8,128)(2,1)S(1)} %copy-done.49), kind=kOutput, calls=%fused_computation.4 | convolution fusion | flops 209715200 | bytes 13632256 | tf_op jit(solution)/shard_map/eri,ex->xri/dot_general | solution.py:219
  60.8 4.1 collective-permute-done.1
  66.7 5.1 collective-permute-done.23
  78.4 15.6 %collective-permute-done.37 = bf16[48,2048]{1,0:T(8,128)(2,1)S(1)} collective-permute-done((bf16[48,2048]{1,0:T(8,128)(2,1)S(1)}, bf16[48,2048]{1,0:T(8,128)(2,1)S(1)}, u32[]{:S(2)}, u32[]{:S(2)}) %collective-permute-start.37) | collective-permute-done | bytes 196640 | tf_op jit(solution)/shard_map/ppermute | solution.py:48
  94.4 5.3 collective-permute-done.38
  103.6 12.7 %collective-permute-done.2 = bf16[96,3200]{1,0:T(8,128)(2,1)} collective-permute-done((bf16[96,3200]{1,0:T(8,128)(2,1)S(1)}, bf16[96,3200]{1,0:T(8,128)(2,1)}, u32[]{:S(2)}, u32[]{:S(2)}) %collective-permute-start.2) | collective-permute-done | bytes 614432 | tf_op jit(solution)/shard_map/ppermute | solution.py:48
  126.4 7.7 %collective-permute-done.15 = bf16[48,3072]{1,0:T(8,128)(2,1)S(1)} collective-permute-done((bf16[48,3072]{1,0:T(8,128)(2,1)S(1)}, bf16[48,3072]{1,0:T(8,128)(2,1)S(1)}, u32[]{:S(2)}, u32[]{:S(2)}) %collective-permute-start.15) | collective-permute-done | bytes 294944 | tf_op jit(solution)/shard_map/ppermute | solution.py:48
  135.8 5.7 %collective-permute-done.16 = bf16[48,3072]{1,0:T(8,128)(2,1)S(1)} collective-permute-done((bf16[48,3072]{1,0:T(8,128)(2,1)S(1)}, bf16[48,3072]{1,0:T(8,128)(2,1)S(1)}, u32[]{:S(2)}, u32[]{:S(2)}) %collective-permute-start.16) | collective-permute-done | bytes 294944 | tf_op jit(solution)/shard_map/ppermute | solution.py:48
  143.2 7.0 %collective-permute-done.24 = bf16[96,4096]{1,0:T(8,128)(2,1)S(1)} collective-permute-done((bf16[96,4096]{1,0:T(8,128)(2,1)}, bf16[96,4096]{1,0:T(8,128)(2,1)S(1)}, u32[]{:S(2)}, u32[]{:S(2)}) %collective-permute-start.24) | collective-permute-done | bytes 786464 | tf_op jit(solution)/shard_map/ppermute | solution.py:48
  154.5 4.2 collective-permute-done.4
  161.1 5.2 collective-permute-done.5
  185.7 4.1 convolution_convert_fusion.2
  193.2 20.4 %fusion.145 = (f32[12,512]{1,0:T(8,128)S(1)}, f32[12,512,512]{1,2,0:T(8,128)}) fusion(f32[512,512,12]{0,2,1:T(8,128)} %fusion.3, pred[512,512]{0,1:T(8,128)(4,1)S(1)} %copy-done.34, bf16[512,12,64]{0,2,1:T(8,128)(2,1)S(1)} %bitcast.151, bf16[512,12,64]{0,2,1:T(8,128)(2,1)S(1)} %bitcast.143), kind=kOutput, calls=%fused_computation.321 | convolution fusion | flops 415236608 | bytes 27025408 | tf_op jit(solution)/shard_map/sub | solution.py:148
  213.6 9.1 %divide_convert_fusion.1 = bf16[12,512,512]{1,2,0:T(8,128)(2,1)} fusion(f32[12,512,512]{1,2,0:T(8,128)} %get-tuple-element.115, f32[12,512]{1,0:T(8,128)S(1)} %get-tuple-element.114), kind=kLoop, calls=%fused_computation.19 | loop fusion | flops 6291456 | bytes 18898944 | tf_op jit(solution)/shard_map/convert_element_type | solution.py:149
  222.7 4.0 convolution_convert_fusion.19
  229.7 3.7 convolution_convert_fusion.11
  235.7 10.4 %fusion.146 = (f32[12,512]{1,0:T(8,128)S(1)}, f32[12,512,512]{1,2,0:T(8,128)}) fusion(pred[512]{0:T(512)(128)(4,1)S(1)} %copy-done.57, bf16[512,12,64]{0,2,1:T(8,128)(2,1)} %bitcast.163, bf16[512,12,64]{0,2,1:T(8,128)(2,1)S(1)} %bitcast.157), kind=kOutput, calls=%fused_computation.322 | convolution fusion | flops 412090880 | bytes 14180864 | tf_op jit(solution)/shard_map/sub | solution.py:148
  246.2 9.2 %divide_convert_fusion = bf16[12,512,512]{1,2,0:T(8,128)(2,1)} fusion(f32[12,512,512]{1,2,0:T(8,128)} %get-tuple-element.119, f32[12,512]{1,0:T(8,128)S(1)} %get-tuple-element.118), kind=kLoop, calls=%fused_computation.17 | loop fusion | flops 6291456 | bytes 18898944 | tf_op jit(solution)/shard_map/convert_element_type | solution.py:149
  255.3 3.9 convolution_convert_fusion.18
  273.6 6.1 %fusion.129 = f32[512,4096]{1,0:T(8,128)S(1)} fusion(bf16[768,4096]{1,0:T(8,128)(2,1)} %constant_dynamic-update-slice_fusion.42, f32[512,768]{0,1:T(8,128)S(1)} %get-tuple-element.121, f32[768]{0:T(1024)S(1)} %get-tuple-element.24, f32[512]{0:T(512)S(1)} %fusion.120), kind=kOutput, calls=%fused_computation.305 | convolution fusion | flops 3222405120 | bytes 16258048 | tf_op jit(solution)/shard_map/dot_general | solution.py:111
  279.7 6.8 %fusion.23 = (bf16[512,2048]{1,0:T(8,128)(2,1)}, bf16[512,2048]{1,0:T(8,128)(2,1)}, bf16[512,2048]{1,0:T(8,128)(2,1)}) fusion(f32[512,4096]{1,0:T(8,128)S(1)} %fusion.129, bf16[768,512]{1,0:T(8,128)(2,1)S(1)} %copy-done.35, bf16[768,2048]{1,0:T(8,128)(2,1)S(1)} %copy-done.54), kind=kOutput, calls=%fused_computation.37 | convolution fusion | flops 1637875712 | bytes 18612224 | tf_op jit(solution)/shard_map/dot_general | solution.py:111
  286.5 6.2 %fusion.62 = bf16[1,512,768]{2,1,0:T(8,128)(2,1)} fusion(s32[768]{0:T(1024)S(1)} %copy-done.51, f32[512,768]{0,1:T(8,128)S(1)} %copy-done.7, bf16[512,2048]{1,0:T(8,128)(2,1)} %get-tuple-element.32, bf16[768,2048]{1,0:T(8,128)(2,1)} %copy-done.53), kind=kOutput, calls=%fused_computation.117 | convolution fusion | flops 2216361984 | bytes 7605248 | tf_op jit(solution)/shard_map/dot_general | solution.py:115
  292.8 5.4 convolution_convert_fusion.3
  298.2 6.4 %multiply_reduce_fusion = (bf16[768]{0:T(1024)(128)(2,1)S(1)}, f32[512]{0:T(512)S(1)}, f32[512,768]{0,1:T(8,128)S(1)}) fusion(f32[512,768]{0,1:T(8,128)S(1)} %copy-done.7, f32[512]{0:T(512)S(1)} %fusion.120, f32[768]{0:T(1024)S(1)} %get-tuple-element.24, bf16[768,4096]{1,0:T(8,128)(2,1)} %constant_dynamic-update-slice_fusion.42, ...), kind=kOutput, calls=%fused_computation.83 | convolution fusion | flops 3231972096 | bytes 13640192 | tf_op jit(solution)/shard_map/dot_general | solution.py:115
  304.6 6.0 %convolution_convert_fusion = bf16[768,4096]{1,0:T(8,128)(2,1)} fusion(bf16[512,2048]{1,0:T(8,128)(2,1)S(1)} %copy-done.61, bf16[512,2048]{1,0:T(8,128)(2,1)S(1)} %copy-done.60, f32[512,768]{0,1:T(8,128)S(1)} %copy-done.7, f32[768]{0:T(1024)S(1)} %get-tuple-element.24, f32[512]{0:T(512)S(1)} %fusion.120), kind=kOutput, calls=%fused_computation.24 | convolution fusion | flops 3233939456 | bytes 12063744 | tf_op jit(solution)/shard_map/dot_general | solution.py:119
  313.0 3.2 convolution_convert_fusion.10
  318.5 6.1 %convolution_convert_fusion.12 = bf16[12,64,512]{2,1,0:T(8,128)(2,1)} fusion(bf16[512,12,64]{0,2,1:T(8,128)(2,1)} %bitcast.153, bf16[12,512,512]{1,2,0:T(8,128)(2,1)} %divide_convert_fusion), kind=kOutput, calls=%fused_computation.102 | convolution fusion | flops 403046400 | bytes 7864320 | tf_op jit(solution)/shard_map/hqk,qhd->khd/dot_general | solution.py:157
  324.7 7.7 %fusion.8 = (f32[12,512]{1,0:T(8,128)S(1)}, f32[12,512,512]{1,2,0:T(8,128)}) fusion(bf16[12,512,512]{1,2,0:T(8,128)(2,1)S(1)} %bitcast.136, bf16[512,12,64]{0,2,1:T(8,128)(2,1)} %bitcast.154, bf16[512,12,64]{0,2,1:T(8,128)(2,1)S(1)} %bitcast.142), kind=kOutput, calls=%fused_computation.13 | convolution fusion | flops 412084224 | bytes 20471808 | tf_op jit(solution)/shard_map/qhd,khd->hqk/dot_general | solution.py:156
  332.4 7.1 %fusion.9 = bf16[12,512,512]{1,2,0:T(8,128)(2,1)S(1)} fusion(f32[12,512,512]{1,2,0:T(8,128)} %get-tuple-element.124, f32[12,512]{1,0:T(8,128)S(1)} %get-tuple-element.123, f32[12,512,512]{1,2,0:T(8,128)S(1)} %bitcast.140, f32[12,512]{1,0:T(8,128)S(1)} %get-tuple-element.118), kind=kLoop, calls=%fused_computation.14 | loop fusion | flops 18874368 | bytes 31506432 | tf_op jit(solution)/shard_map/convert_element_type | solution.py:159
  356.6 5.2 convolution_convert_fusion.14
  361.8 7.7 %fusion.6 = (f32[12,512]{1,0:T(8,128)S(1)}, f32[12,512,512]{1,2,0:T(8,128)}) fusion(bf16[12,512,512]{1,2,0:T(8,128)(2,1)S(1)} %bitcast.134, bf16[512,12,64]{0,2,1:T(8,128)(2,1)} %bitcast.156, bf16[512,12,64]{0,2,1:T(8,128)(2,1)S(1)} %bitcast.146), kind=kOutput, calls=%fused_computation.11 | convolution fusion | flops 412084224 | bytes 20471808 | tf_op jit(solution)/shard_map/qhd,khd->hqk/dot_general | solution.py:156
  369.6 6.9 %fusion.7 = bf16[12,512,512]{1,2,0:T(8,128)(2,1)S(1)} fusion(f32[12,512,512]{1,2,0:T(8,128)} %get-tuple-element.127, f32[12,512]{1,0:T(8,128)S(1)} %get-tuple-element.126, f32[12,512,512]{1,2,0:T(8,128)S(1)} %bitcast.138, f32[12,512]{1,0:T(8,128)S(1)} %get-tuple-element.114), kind=kLoop, calls=%fused_computation.12 | loop fusion | flops 18874368 | bytes 31506432 | tf_op jit(solution)/shard_map/convert_element_type | solution.py:159
  376.5 8.1 %fusion.70 = f32[32,12]{0,1:T(8,128)S(1)} fusion(bf16[12,512,512]{1,2,0:T(8,128)(2,1)S(1)} %fusion.7, s32[512,512]{0,1:T(8,128)S(1)} %copy-done.17), kind=kOutput, calls=%fused_computation.125 | convolution fusion | flops 209715200 | bytes 7341568 | tf_op jit(solution)/shard_map/hri,eri->eh/dot_general | solution.py:270
  388.0 5.3 multiply_reduce_fusion.2
  393.3 3.9 convolution_convert_fusion.1
  424.2 5.0 fusion.63
  438.0 4.8 fusion.61
  443.0 4.0 slice.507
  462.8 3.4 collective-permute-done.71
  472.6 3.8 collective-permute-done.45
  480.8 8.2 %collective-permute-done.55 = bf16[96,3072]{1,0:T(8,128)(2,1)S(1)} collective-permute-done((bf16[96,3072]{1,0:T(8,128)(2,1)S(1)}, bf16[96,3072]{1,0:T(8,128)(2,1)S(1)}, u32[]{:S(2)}, u32[]{:S(2)}) %collective-permute-start.55) | collective-permute-done | bytes 589856 | tf_op jit(solution)/shard_map/ppermute | solution.py:48
  490.7 11.4 %collective-permute-done.48 = bf16[96,3200]{1,0:T(8,128)(2,1)S(1)} collective-permute-done((bf16[96,3200]{1,0:T(8,128)(2,1)S(1)}, bf16[96,3200]{1,0:T(8,128)(2,1)S(1)}, u32[]{:S(2)}, u32[]{:S(2)}) %collective-permute-start.48) | collective-permute-done | bytes 614432 | tf_op jit(solution)/shard_map/ppermute | solution.py:48
  502.4 3.6 collective-permute-done.61
  513.6 9.0 %collective-permute-done.57 = bf16[24,3072]{1,0:T(8,128)(2,1)S(1)} collective-permute-done((bf16[24,3072]{1,0:T(8,128)(2,1)S(1)}, bf16[24,3072]{1,0:T(8,128)(2,1)S(1)}, u32[]{:S(2)}, u32[]{:S(2)}) %collective-permute-start.57) | collective-permute-done | bytes 147488 | tf_op jit(solution)/shard_map/ppermute | solution.py:48
  527.4 6.9 %collective-permute-done.63 = bf16[48,4096]{1,0:T(8,128)(2,1)S(1)} collective-permute-done((bf16[48,4096]{1,0:T(8,128)(2,1)S(1)}, bf16[48,4096]{1,0:T(8,128)(2,1)S(1)}, u32[]{:S(2)}, u32[]{:S(2)}) %collective-permute-start.63) | collective-permute-done | bytes 393248 | tf_op jit(solution)/shard_map/ppermute | solution.py:48
  534.4 4.2 collective-permute-start.64
  539.3 5.0 collective-permute-done.64
  (478 shorter events, 224.2 us)
Async XLA Ops:
  0.7 43.1 %collective-permute-start.33 = (bf16[24,2048]{1,0:T(8,128)(2,1)}, bf16[24,2048]{1,0:T(8,128)(2,1)}, u32[]{:S(2)}, u32[]{:S(2)}) collective-permute-start(bf16[24,2048]{1,0:T(8,128)(2,1)} %param.37), channel_id=1, source_target_pairs={{0,4},{1,5},{2,6},{3,7},{4,0},{5,1},{6,2},{7,3},{8,12},{9,13},{10,... | collective-permute-start | bytes 294920 | tf_op jit(solution)/shard_map/ppermute | solution.py:48
  10.4 37.0 %collective-permute-start.11 = (bf16[24,3072]{1,0:T(8,128)(2,1)}, bf16[24,3072]{1,0:T(8,128)(2,1)S(1)}, u32[]{:S(2)}, u32[]{:S(2)}) collective-permute-start(bf16[24,3072]{1,0:T(8,128)(2,1)} %get-tuple-element.94), channel_id=1, source_target_pairs={{0,4},{1,5},{2,6},{3,7},{4,0},{5,1},{6,2},{7,3},{8,12},{9,13},{10,... | collective-permute-start | bytes 442376 | tf_op jit(solution)/shard_map/ppermute | solution.py:48
  17.5 31.2 %collective-permute-start = (bf16[24,3200]{1,0:T(8,128)(2,1)}, bf16[24,3200]{1,0:T(8,128)(2,1)}, u32[]{:S(2)}, u32[]{:S(2)}) collective-permute-start(bf16[24,3200]{1,0:T(8,128)(2,1)} %get-tuple-element.102), channel_id=1, source_target_pairs={{0,4},{1,5},{2,6},{3,7},{4,0},{5,1},{6,2},{7,3},{8,12},{9,13},{10,... | collective-permute-start | bytes 460808 | tf_op jit(solution)/shard_map/ppermute | solution.py:48
  23.5 29.7 %collective-permute-start.22 = (bf16[24,4096]{1,0:T(8,128)(2,1)}, bf16[24,4096]{1,0:T(8,128)(2,1)}, u32[]{:S(2)}, u32[]{:S(2)}) collective-permute-start(bf16[24,4096]{1,0:T(8,128)(2,1)} %get-tuple-element.90), channel_id=1, source_target_pairs={{0,4},{1,5},{2,6},{3,7},{4,0},{5,1},{6,2},{7,3},{8,12},{9,13},{10,... | collective-permute-start | bytes 589832 | tf_op jit(solution)/shard_map/ppermute | solution.py:48
  44.7 11.5 %collective-permute-start.34 = (bf16[48,2048]{1,0:T(8,128)(2,1)S(1)}, bf16[48,2048]{1,0:T(8,128)(2,1)S(1)}, u32[]{:S(2)}, u32[]{:S(2)}) collective-permute-start(bf16[48,2048]{1,0:T(8,128)(2,1)S(1)} %pad_maximum_fusion.27), channel_id=1, source_target_pairs={{0,2},{1,3},{2,0},{3,1},{4,6},{5,7},{6,4},{7,5},{8,10},{9,11},{10,... | collective-permute-start | bytes 589832 | tf_op jit(solution)/shard_map/ppermute | solution.py:48
  49.7 15.2 %collective-permute-start.1 = (bf16[48,3200]{1,0:T(8,128)(2,1)S(1)}, bf16[48,3200]{1,0:T(8,128)(2,1)S(1)}, u32[]{:S(2)}, u32[]{:S(2)}) collective-permute-start(bf16[48,3200]{1,0:T(8,128)(2,1)S(1)} %pad_maximum_fusion.25), channel_id=1, source_target_pairs={{0,2},{1,3},{2,0},{3,1},{4,6},{5,7},{6,4},{7,5},{8,10},{9,11},{10,... | collective-permute-start | bytes 921608 | tf_op jit(solution)/shard_map/ppermute | solution.py:48
  54.2 17.7 %collective-permute-start.23 = (bf16[48,4096]{1,0:T(8,128)(2,1)S(1)}, bf16[48,4096]{1,0:T(8,128)(2,1)S(1)}, u32[]{:S(2)}, u32[]{:S(2)}) collective-permute-start(bf16[48,4096]{1,0:T(8,128)(2,1)S(1)} %pad_maximum_fusion.22), channel_id=1, source_target_pairs={{0,2},{1,3},{2,0},{3,1},{4,6},{5,7},{6,4},{7,5},{8,10},{9,11},{10,... | collective-permute-start | bytes 1179656 | tf_op jit(solution)/shard_map/ppermute | solution.py:48
  56.2 43.5 %collective-permute-start.39 = (bf16[96,2048]{1,0:T(8,128)(2,1)S(1)}, bf16[96,2048]{1,0:T(8,128)(2,1)S(1)}, u32[]{:S(2)}, u32[]{:S(2)}) collective-permute-start(bf16[96,2048]{1,0:T(8,128)(2,1)S(1)} %get-tuple-element.84), channel_id=1, source_target_pairs={{0,8},{8,0},{16,24},{24,16},{1,9},{9,1},{17,25},{25,17},{2,10},{10... | collective-permute-start | bytes 1179656 | tf_op jit(solution)/shard_map/ppermute | solution.py:48
  56.3 19.9 %collective-permute-start.36 = (bf16[96,2048]{1,0:T(8,128)(2,1)S(1)}, bf16[96,2048]{1,0:T(8,128)(2,1)S(1)}, u32[]{:S(2)}, u32[]{:S(2)}) collective-permute-start(bf16[96,2048]{1,0:T(8,128)(2,1)S(1)} %get-tuple-element.84), channel_id=1, source_target_pairs={{0,16},{8,24},{16,0},{24,8},{1,17},{9,25},{17,1},{25,9},{2,18},{10... | collective-permute-start | bytes 1179656 | tf_op jit(solution)/shard_map/ppermute | solution.py:48
  58.4 19.4 %collective-permute-start.35 = (bf16[96,2048]{1,0:T(8,128)(2,1)S(1)}, bf16[96,2048]{1,0:T(8,128)(2,1)S(1)}, u32[]{:S(2)}, u32[]{:S(2)}) collective-permute-start(bf16[96,2048]{1,0:T(8,128)(2,1)S(1)} %get-tuple-element.84), channel_id=1, source_target_pairs={{0,1},{1,0},{2,3},{3,2},{4,5},{5,4},{6,7},{7,6},{8,9},{9,8},{10,11... | collective-permute-start | bytes 1179656 | tf_op jit(solution)/shard_map/ppermute | solution.py:48
  65.0 76.6 %collective-permute-start.17 = (bf16[96,3072]{1,0:T(8,128)(2,1)S(1)}, bf16[96,3072]{1,0:T(8,128)(2,1)S(1)}, u32[]{:S(2)}, u32[]{:S(2)}) collective-permute-start(bf16[96,3072]{1,0:T(8,128)(2,1)S(1)} %pad_maximum_fusion.19), channel_id=1, source_target_pairs={{0,8},{8,0},{16,24},{24,16},{1,9},{9,1},{17,25},{25,17},{2,10},{10... | collective-permute-start | bytes 1769480 | tf_op jit(solution)/shard_map/ppermute | solution.py:48
  71.9 30.1 %collective-permute-start.14 = (bf16[96,3072]{1,0:T(8,128)(2,1)S(1)}, bf16[96,3072]{1,0:T(8,128)(2,1)S(1)}, u32[]{:S(2)}, u32[]{:S(2)}) collective-permute-start(bf16[96,3072]{1,0:T(8,128)(2,1)S(1)} %pad_maximum_fusion.19), channel_id=1, source_target_pairs={{0,16},{8,24},{16,0},{24,8},{1,17},{9,25},{17,1},{25,9},{2,18},{10... | collective-permute-start | bytes 1769480 | tf_op jit(solution)/shard_map/ppermute | solution.py:48
  76.2 24.0 %collective-permute-start.13 = (bf16[96,3072]{1,0:T(8,128)(2,1)S(1)}, bf16[96,3072]{1,0:T(8,128)(2,1)S(1)}, u32[]{:S(2)}, u32[]{:S(2)}) collective-permute-start(bf16[96,3072]{1,0:T(8,128)(2,1)S(1)} %pad_maximum_fusion.19), channel_id=1, source_target_pairs={{0,1},{1,0},{2,3},{3,2},{4,5},{5,4},{6,7},{7,6},{8,9},{9,8},{10,11... | collective-permute-start | bytes 1769480 | tf_op jit(solution)/shard_map/ppermute | solution.py:48
  77.7 16.3 %collective-permute-start.37 = (bf16[48,2048]{1,0:T(8,128)(2,1)S(1)}, bf16[48,2048]{1,0:T(8,128)(2,1)S(1)}, u32[]{:S(2)}, u32[]{:S(2)}) collective-permute-start(bf16[48,2048]{1,0:T(8,128)(2,1)S(1)} %slice.462), channel_id=1, source_target_pairs={{0,1},{1,0},{2,3},{3,2},{4,5},{5,4},{6,7},{7,6},{8,9},{9,8},{10,11... | collective-permute-start | bytes 589832 | tf_op jit(solution)/shard_map/ppermute | solution.py:48
  99.7 67.4 %collective-permute-start.6 = (bf16[96,3200]{1,0:T(8,128)(2,1)S(1)}, bf16[96,3200]{1,0:T(8,128)(2,1)S(1)}, u32[]{:S(2)}, u32[]{:S(2)}) collective-permute-start(bf16[96,3200]{1,0:T(8,128)(2,1)S(1)} %pad_maximum_fusion.16), channel_id=1, source_target_pairs={{0,8},{8,0},{16,24},{24,16},{1,9},{9,1},{17,25},{25,17},{2,10},{10... | collective-permute-start | bytes 1843208 | tf_op jit(solution)/shard_map/ppermute | solution.py:48
  99.7 18.6 %collective-permute-start.3 = (bf16[96,3200]{1,0:T(8,128)(2,1)S(1)}, bf16[96,3200]{1,0:T(8,128)(2,1)}, u32[]{:S(2)}, u32[]{:S(2)}) collective-permute-start(bf16[96,3200]{1,0:T(8,128)(2,1)S(1)} %pad_maximum_fusion.16), channel_id=1, source_target_pairs={{0,16},{8,24},{16,0},{24,8},{1,17},{9,25},{17,1},{25,9},{2,18},{10... | collective-permute-start | bytes 1843208 | tf_op jit(solution)/shard_map/ppermute | solution.py:48
  100.2 16.2 %collective-permute-start.2 = (bf16[96,3200]{1,0:T(8,128)(2,1)S(1)}, bf16[96,3200]{1,0:T(8,128)(2,1)}, u32[]{:S(2)}, u32[]{:S(2)}) collective-permute-start(bf16[96,3200]{1,0:T(8,128)(2,1)S(1)} %pad_maximum_fusion.16), channel_id=1, source_target_pairs={{0,1},{1,0},{2,3},{3,2},{4,5},{5,4},{6,7},{7,6},{8,9},{9,8},{10,11... | collective-permute-start | bytes 1843208 | tf_op jit(solution)/shard_map/ppermute | solution.py:48
  101.9 40.3 %collective-permute-start.25 = (bf16[96,4096]{1,0:T(8,128)(2,1)}, bf16[96,4096]{1,0:T(8,128)(2,1)S(1)}, u32[]{:S(2)}, u32[]{:S(2)}) collective-permute-start(bf16[96,4096]{1,0:T(8,128)(2,1)} %pad_maximum_fusion.11), channel_id=1, source_target_pairs={{0,16},{8,24},{16,0},{24,8},{1,17},{9,25},{17,1},{25,9},{2,18},{10... | collective-permute-start | bytes 2359304 | tf_op jit(solution)/shard_map/ppermute | solution.py:48
  125.9 24.3 %collective-permute-start.24 = (bf16[96,4096]{1,0:T(8,128)(2,1)}, bf16[96,4096]{1,0:T(8,128)(2,1)S(1)}, u32[]{:S(2)}, u32[]{:S(2)}) collective-permute-start(bf16[96,4096]{1,0:T(8,128)(2,1)} %pad_maximum_fusion.11), channel_id=1, source_target_pairs={{0,1},{1,0},{2,3},{3,2},{4,5},{5,4},{6,7},{7,6},{8,9},{9,8},{10,11... | collective-permute-start | bytes 2359304 | tf_op jit(solution)/shard_map/ppermute | solution.py:48
  141.5 124.0 %collective-permute-start.28 = (bf16[96,4096]{1,0:T(8,128)(2,1)}, bf16[96,4096]{1,0:T(8,128)(2,1)}, u32[]{:S(2)}, u32[]{:S(2)}) collective-permute-start(bf16[96,4096]{1,0:T(8,128)(2,1)} %pad_maximum_fusion.11), channel_id=1, source_target_pairs={{0,8},{8,0},{16,24},{24,16},{1,9},{9,1},{17,25},{25,17},{2,10},{10... | collective-permute-start | bytes 2359304 | tf_op jit(solution)/shard_map/ppermute | solution.py:48
  141.6 27.0 %collective-permute-start.19 = (bf16[96,3072]{1,0:T(8,128)(2,1)S(1)}, bf16[96,3072]{1,0:T(8,128)(2,1)S(1)}, u32[]{:S(2)}, u32[]{:S(2)}) collective-permute-start(bf16[96,3072]{1,0:T(8,128)(2,1)S(1)} %collective-permute-done.14), channel_id=1, source_target_pairs={{0,8},{8,0},{16,24},{24,16},{1,9},{9,1},{17,25},{25,17},{2,10},{10... | collective-permute-start | bytes 1769480 | tf_op jit(solution)/shard_map/ppermute | solution.py:48
  142.2 26.1 %collective-permute-start.18 = (bf16[96,3072]{1,0:T(8,128)(2,1)S(1)}, bf16[96,3072]{1,0:T(8,128)(2,1)S(1)}, u32[]{:S(2)}, u32[]{:S(2)}) collective-permute-start(bf16[96,3072]{1,0:T(8,128)(2,1)S(1)} %collective-permute-done.13), channel_id=1, source_target_pairs={{0,8},{8,0},{16,24},{24,16},{1,9},{9,1},{17,25},{25,17},{2,10},{10... | collective-permute-start | bytes 1769480 | tf_op jit(solution)/shard_map/ppermute | solution.py:48
  166.2 12.7 %collective-permute-start.8 = (bf16[96,3200]{1,0:T(8,128)(2,1)}, bf16[96,3200]{1,0:T(8,128)(2,1)}, u32[]{:S(2)}, u32[]{:S(2)}) collective-permute-start(bf16[96,3200]{1,0:T(8,128)(2,1)} %collective-permute-done.3), channel_id=1, source_target_pairs={{0,8},{8,0},{16,24},{24,16},{1,9},{9,1},{17,25},{25,17},{2,10},{10... | collective-permute-start | bytes 1843208 | tf_op jit(solution)/shard_map/ppermute | solution.py:48
  170.0 91.3 %collective-permute-start.26 = (bf16[48,4096]{1,0:T(8,128)(2,1)}, bf16[48,4096]{1,0:T(8,128)(2,1)}, u32[]{:S(2)}, u32[]{:S(2)}) collective-permute-start(bf16[48,4096]{1,0:T(8,128)(2,1)} %slice.458), channel_id=1, source_target_pairs={{0,1},{1,0},{2,3},{3,2},{4,5},{5,4},{6,7},{7,6},{8,9},{9,8},{10,11... | collective-permute-start | bytes 1179656 | tf_op jit(solution)/shard_map/ppermute | solution.py:48
  171.7 90.1 %collective-permute-start.27 = (bf16[48,4096]{1,0:T(8,128)(2,1)}, bf16[48,4096]{1,0:T(8,128)(2,1)}, u32[]{:S(2)}, u32[]{:S(2)}) collective-permute-start(bf16[48,4096]{1,0:T(8,128)(2,1)} %slice.459), channel_id=1, source_target_pairs={{0,16},{8,24},{16,0},{24,8},{1,17},{9,25},{17,1},{25,9},{2,18},{10... | collective-permute-start | bytes 1179656 | tf_op jit(solution)/shard_map/ppermute | solution.py:48
  176.9 93.0 %collective-permute-start.30 = (bf16[96,4096]{1,0:T(8,128)(2,1)}, bf16[96,4096]{1,0:T(8,128)(2,1)}, u32[]{:S(2)}, u32[]{:S(2)}) collective-permute-start(bf16[96,4096]{1,0:T(8,128)(2,1)} %copy-done.32), channel_id=1, source_target_pairs={{0,8},{8,0},{16,24},{24,16},{1,9},{9,1},{17,25},{25,17},{2,10},{10... | collective-permute-start | bytes 2359304 | tf_op jit(solution)/shard_map/ppermute | solution.py:48
  183.2 84.4 %collective-permute-start.29 = (bf16[96,4096]{1,0:T(8,128)(2,1)}, bf16[96,4096]{1,0:T(8,128)(2,1)}, u32[]{:S(2)}, u32[]{:S(2)}) collective-permute-start(bf16[96,4096]{1,0:T(8,128)(2,1)} %copy-done.33), channel_id=1, source_target_pairs={{0,8},{8,0},{16,24},{24,16},{1,9},{9,1},{17,25},{25,17},{2,10},{10... | collective-permute-start | bytes 2359304 | tf_op jit(solution)/shard_map/ppermute | solution.py:48
  401.3 17.3 %collective-permute-start.65 = (bf16[384,2048]{1,0:T(8,128)(2,1)}, bf16[384,2048]{1,0:T(8,128)(2,1)}, u32[]{:S(2)}, u32[]{:S(2)}) collective-permute-start(bf16[384,2048]{1,0:T(8,128)(2,1)} %slice.522), channel_id=1, source_target_pairs={{0,8},{8,0},{16,24},{24,16},{1,9},{9,1},{17,25},{25,17},{2,10},{10... | collective-permute-start | bytes 4718600 | tf_op jit(solution)/shard_map/ppermute | solution.py:48
  410.1 43.0 %collective-permute-start.51 = (bf16[384,3072]{1,0:T(8,128)(2,1)}, bf16[384,3072]{1,0:T(8,128)(2,1)}, u32[]{:S(2)}, u32[]{:S(2)}) collective-permute-start(bf16[384,3072]{1,0:T(8,128)(2,1)} %pad_maximum_fusion.5), channel_id=1, source_target_pairs={{0,8},{8,0},{16,24},{24,16},{1,9},{9,1},{17,25},{25,17},{2,10},{10... | collective-permute-start | bytes 7077896 | tf_op jit(solution)/shard_map/ppermute | solution.py:48
  418.1 11.0 %collective-permute-start.74 = (f32[32,12]{0,1:T(8,128)S(1)}, f32[32,12]{0,1:T(8,128)S(1)}, u32[]{:S(2)}, u32[]{:S(2)}) collective-permute-start(f32[32,12]{0,1:T(8,128)S(1)} %add.385), channel_id=1, source_target_pairs={{0,16},{8,24},{16,0},{24,8},{1,17},{9,25},{17,1},{25,9},{2,18},{10... | collective-permute-start | bytes 4616 | tf_op jit(solution)/shard_map/ppermute | solution.py:48
  434.5 15.8 %collective-permute-start.69 = (bf16[96,2048]{1,0:T(8,128)(2,1)}, bf16[96,2048]{1,0:T(8,128)(2,1)}, u32[]{:S(2)}, u32[]{:S(2)}) collective-permute-start(bf16[96,2048]{1,0:T(8,128)(2,1)} %pad_maximum_fusion.24), channel_id=1, source_target_pairs={{0,16},{8,24},{16,0},{24,8},{1,17},{9,25},{17,1},{25,9},{2,18},{10... | collective-permute-start | bytes 1179656 | tf_op jit(solution)/shard_map/ppermute | solution.py:48
  435.7 14.5 %collective-permute-start.67 = (bf16[96,2048]{1,0:T(8,128)(2,1)}, bf16[96,2048]{1,0:T(8,128)(2,1)}, u32[]{:S(2)}, u32[]{:S(2)}) collective-permute-start(bf16[96,2048]{1,0:T(8,128)(2,1)} %pad_maximum_fusion.23), channel_id=1, source_target_pairs={{0,1},{1,0},{2,3},{3,2},{4,5},{5,4},{6,7},{7,6},{8,9},{9,8},{10,11... | collective-permute-start | bytes 1179656 | tf_op jit(solution)/shard_map/ppermute | solution.py:48
  437.3 22.3 %collective-permute-start.44 = (bf16[384,3200]{1,0:T(8,128)(2,1)}, bf16[384,3200]{1,0:T(8,128)(2,1)}, u32[]{:S(2)}, u32[]{:S(2)}) collective-permute-start(bf16[384,3200]{1,0:T(8,128)(2,1)} %pad_maximum_fusion.3), channel_id=1, source_target_pairs={{0,8},{8,0},{16,24},{24,16},{1,9},{9,1},{17,25},{25,17},{2,10},{10... | collective-permute-start | bytes 7372808 | tf_op jit(solution)/shard_map/ppermute | solution.py:48
  437.4 12.0 %collective-permute-start.76 = (f32[32,12]{0,1:T(8,128)S(1)}, f32[32,12]{0,1:T(8,128)S(1)}, u32[]{:S(2)}, u32[]{:S(2)}) collective-permute-start(f32[32,12]{0,1:T(8,128)S(1)} %add.387), channel_id=1, source_target_pairs={{0,2},{1,3},{2,0},{3,1},{4,6},{5,7},{6,4},{7,5},{8,10},{9,11},{10,... | collective-permute-start | bytes 4616 | tf_op jit(solution)/shard_map/ppermute | solution.py:48
  449.4 29.3 %collective-permute-start.58 = (bf16[384,4096]{1,0:T(8,128)(2,1)}, bf16[384,4096]{1,0:T(8,128)(2,1)S(1)}, u32[]{:S(2)}, u32[]{:S(2)}) collective-permute-start(bf16[384,4096]{1,0:T(8,128)(2,1)} %slice.507), channel_id=1, source_target_pairs={{0,8},{8,0},{16,24},{24,16},{1,9},{9,1},{17,25},{25,17},{2,10},{10... | collective-permute-start | bytes 9437192 | tf_op jit(solution)/shard_map/ppermute | solution.py:48
  456.1 12.3 %collective-permute-start.54 = (bf16[48,3072]{1,0:T(8,128)(2,1)S(1)}, bf16[48,3072]{1,0:T(8,128)(2,1)S(1)}, u32[]{:S(2)}, u32[]{:S(2)}) collective-permute-start(bf16[48,3072]{1,0:T(8,128)(2,1)S(1)} %get-tuple-element.49), channel_id=1, source_target_pairs={{0,1},{1,0},{2,3},{3,2},{4,5},{5,4},{6,7},{7,6},{8,9},{9,8},{10,11... | collective-permute-start | bytes 884744 | tf_op jit(solution)/shard_map/ppermute | solution.py:48
  456.7 11.7 %collective-permute-start.52 = (bf16[48,3072]{1,0:T(8,128)(2,1)S(1)}, bf16[48,3072]{1,0:T(8,128)(2,1)S(1)}, u32[]{:S(2)}, u32[]{:S(2)}) collective-permute-start(bf16[48,3072]{1,0:T(8,128)(2,1)S(1)} %get-tuple-element.50), channel_id=1, source_target_pairs={{0,16},{8,24},{16,0},{24,8},{1,17},{9,25},{17,1},{25,9},{2,18},{10... | collective-permute-start | bytes 884744 | tf_op jit(solution)/shard_map/ppermute | solution.py:48
  468.5 20.5 %collective-permute-start.55 = (bf16[96,3072]{1,0:T(8,128)(2,1)S(1)}, bf16[96,3072]{1,0:T(8,128)(2,1)S(1)}, u32[]{:S(2)}, u32[]{:S(2)}) collective-permute-start(bf16[96,3072]{1,0:T(8,128)(2,1)S(1)} %pad_maximum_fusion.21), channel_id=1, source_target_pairs={{0,16},{8,24},{16,0},{24,8},{1,17},{9,25},{17,1},{25,9},{2,18},{10... | collective-permute-start | bytes 1769480 | tf_op jit(solution)/shard_map/ppermute | solution.py:48
  469.1 21.4 %collective-permute-start.53 = (bf16[96,3072]{1,0:T(8,128)(2,1)S(1)}, bf16[96,3072]{1,0:T(8,128)(2,1)S(1)}, u32[]{:S(2)}, u32[]{:S(2)}) collective-permute-start(bf16[96,3072]{1,0:T(8,128)(2,1)S(1)} %pad_maximum_fusion.20), channel_id=1, source_target_pairs={{0,1},{1,0},{2,3},{3,2},{4,5},{5,4},{6,7},{7,6},{8,9},{9,8},{10,11... | collective-permute-start | bytes 1769480 | tf_op jit(solution)/shard_map/ppermute | solution.py:48
  476.5 25.7 %collective-permute-start.48 = (bf16[96,3200]{1,0:T(8,128)(2,1)S(1)}, bf16[96,3200]{1,0:T(8,128)(2,1)S(1)}, u32[]{:S(2)}, u32[]{:S(2)}) collective-permute-start(bf16[96,3200]{1,0:T(8,128)(2,1)S(1)} %pad_maximum_fusion.18), channel_id=1, source_target_pairs={{0,16},{8,24},{16,0},{24,8},{1,17},{9,25},{17,1},{25,9},{2,18},{10... | collective-permute-start | bytes 1843208 | tf_op jit(solution)/shard_map/ppermute | solution.py:48
  478.1 24.0 %collective-permute-start.46 = (bf16[96,3200]{1,0:T(8,128)(2,1)S(1)}, bf16[96,3200]{1,0:T(8,128)(2,1)S(1)}, u32[]{:S(2)}, u32[]{:S(2)}) collective-permute-start(bf16[96,3200]{1,0:T(8,128)(2,1)S(1)} %pad_maximum_fusion.17), channel_id=1, source_target_pairs={{0,1},{1,0},{2,3},{3,2},{4,5},{5,4},{6,7},{7,6},{8,9},{9,8},{10,11... | collective-permute-start | bytes 1843208 | tf_op jit(solution)/shard_map/ppermute | solution.py:48
  479.2 26.7 %collective-permute-start.61 = (bf16[48,4096]{1,0:T(8,128)(2,1)S(1)}, bf16[48,4096]{1,0:T(8,128)(2,1)S(1)}, u32[]{:S(2)}, u32[]{:S(2)}) collective-permute-start(bf16[48,4096]{1,0:T(8,128)(2,1)S(1)} %get-tuple-element.37), channel_id=1, source_target_pairs={{0,1},{1,0},{2,3},{3,2},{4,5},{5,4},{6,7},{7,6},{8,9},{9,8},{10,11... | collective-permute-start | bytes 1179656 | tf_op jit(solution)/shard_map/ppermute | solution.py:48
  489.0 18.4 %collective-permute-start.59 = (bf16[48,4096]{1,0:T(8,128)(2,1)S(1)}, bf16[48,4096]{1,0:T(8,128)(2,1)S(1)}, u32[]{:S(2)}, u32[]{:S(2)}) collective-permute-start(bf16[48,4096]{1,0:T(8,128)(2,1)S(1)} %get-tuple-element.38), channel_id=1, source_target_pairs={{0,16},{8,24},{16,0},{24,8},{1,17},{9,25},{17,1},{25,9},{2,18},{10... | collective-permute-start | bytes 1179656 | tf_op jit(solution)/shard_map/ppermute | solution.py:48
  490.6 19.8 %collective-permute-start.56 = (bf16[48,3072]{1,0:T(8,128)(2,1)S(1)}, bf16[48,3072]{1,0:T(8,128)(2,1)S(1)}, u32[]{:S(2)}, u32[]{:S(2)}) collective-permute-start(bf16[48,3072]{1,0:T(8,128)(2,1)S(1)} %slice.499), channel_id=1, source_target_pairs={{0,2},{1,3},{2,0},{3,1},{4,6},{5,7},{6,4},{7,5},{8,10},{9,11},{10,... | collective-permute-start | bytes 884744 | tf_op jit(solution)/shard_map/ppermute | solution.py:48
  507.5 17.1 %collective-permute-start.62 = (bf16[96,4096]{1,0:T(8,128)(2,1)S(1)}, bf16[96,4096]{1,0:T(8,128)(2,1)S(1)}, u32[]{:S(2)}, u32[]{:S(2)}) collective-permute-start(bf16[96,4096]{1,0:T(8,128)(2,1)S(1)} %pad_maximum_fusion.13), channel_id=1, source_target_pairs={{0,16},{8,24},{16,0},{24,8},{1,17},{9,25},{17,1},{25,9},{2,18},{10... | collective-permute-start | bytes 2359304 | tf_op jit(solution)/shard_map/ppermute | solution.py:48
  509.4 17.0 %collective-permute-start.60 = (bf16[96,4096]{1,0:T(8,128)(2,1)S(1)}, bf16[96,4096]{1,0:T(8,128)(2,1)S(1)}, u32[]{:S(2)}, u32[]{:S(2)}) collective-permute-start(bf16[96,4096]{1,0:T(8,128)(2,1)S(1)} %pad_maximum_fusion.12), channel_id=1, source_target_pairs={{0,1},{1,0},{2,3},{3,2},{4,5},{5,4},{6,7},{7,6},{8,9},{9,8},{10,11... | collective-permute-start | bytes 2359304 | tf_op jit(solution)/shard_map/ppermute | solution.py:48
  510.5 12.2 %collective-permute-start.57 = (bf16[24,3072]{1,0:T(8,128)(2,1)S(1)}, bf16[24,3072]{1,0:T(8,128)(2,1)S(1)}, u32[]{:S(2)}, u32[]{:S(2)}) collective-permute-start(bf16[24,3072]{1,0:T(8,128)(2,1)S(1)} %slice.501), channel_id=1, source_target_pairs={{0,4},{1,5},{2,6},{3,7},{4,0},{5,1},{6,2},{7,3},{8,12},{9,13},{10,... | collective-permute-start | bytes 442376 | tf_op jit(solution)/shard_map/ppermute | solution.py:48
  510.9 15.8 %collective-permute-start.50 = (bf16[24,3200]{1,0:T(8,128)(2,1)S(1)}, bf16[24,3200]{1,0:T(8,128)(2,1)S(1)}, u32[]{:S(2)}, u32[]{:S(2)}) collective-permute-start(bf16[24,3200]{1,0:T(8,128)(2,1)S(1)} %slice.480), channel_id=1, source_target_pairs={{0,4},{1,5},{2,6},{3,7},{4,0},{5,1},{6,2},{7,3},{8,12},{9,13},{10,... | collective-permute-start | bytes 460808 | tf_op jit(solution)/shard_map/ppermute | solution.py:48
  (105 other events, 1169.4 us)

commit v2 on v1

v2 whole, which is shorter than its diff:
```python
import math

import jax
import jax.numpy as jnp
import numpy as np
from jax import lax
from jax.experimental import pallas as pl
from jax.experimental.pallas import tpu as pltpu
from jax.sharding import PartitionSpec as P

H = 12
HD = 64
NB = 32

norm_eps = 1e-06
masked_score = -1000000000.0
bucket_edges = [int(math.ceil(16 * 8 ** (power / 16.0))) for power in range(1, 16)]

bf16 = jnp.bfloat16
f32 = jnp.float32


def tie(*values):
    return lax.optimization_barrier(values)


class Cube:
    def __init__(self, mesh):
        self.nx, self.ny = mesh.shape["gx"], mesh.shape["gy"]
        self.n = self.nx * self.ny
        self.core, self.y, self.x = ("gx", 1), ("gx", 2), ("gy", 1)
        self.rest = []
        bit = self.ny // 2
        while bit > 1:
            self.rest.append(("gy", bit))
            bit //= 2
        bit = self.nx // 2
        while bit > 2:
            self.rest.append(("gx", bit))
            bit //= 2

    def send(self, value, step):
        axis, bit = step
        size = self.nx if axis == "gx" else self.ny
        return lax.ppermute(value, axis, [(i, i ^ bit) for i in range(size)])

    def owners(self):
        mask_x, mask_y = np.zeros(self.n, np.int32), np.zeros(self.n, np.int32)
        for place in range(self.n):
            steps = []
            inner, block = place % (self.n // 8), (place // (self.n // 8)) % 4
            for at_bit, step in enumerate(self.rest):
                if (inner >> at_bit) & 1:
                    steps.append(step)
            if block & 1:
                steps.append(self.x)
            if block & 2:
                steps.append(self.y)
            if place >= self.n // 2:
                steps.append(self.core)
            for axis, bit in steps:
                if axis == "gx":
                    mask_x[place] ^= bit
                else:
                    mask_y[place] ^= bit
        gx, gy = lax.axis_index("gx"), lax.axis_index("gy")
        return (gx ^ jnp.asarray(mask_x)) * self.ny + (gy ^ jnp.asarray(mask_y))

    def permutation(self, width):
        rows = width // self.n
        feature = (self.owners()[:, None] * rows + jnp.arange(rows, dtype=jnp.int32)).reshape(1, width)
        return (jnp.arange(width, dtype=jnp.int32)[:, None] == feature).astype(bf16)

    def all_sum(self, value):
        for step in [self.core, self.x, self.y] + self.rest:
            value = value + self.send(value, step)
        return value


class Gather:
    def __init__(self, cube, packed):
        self.cube, self.own = cube, packed

    def line(self, steps):
        for step in steps:
            self.own = jnp.concatenate([self.own, self.cube.send(self.own, step)], axis=0)

    def plane(self):
        self.over_x = self.cube.send(self.own, self.cube.x)
        self.over_y = self.cube.send(self.own, self.cube.y)

    def far(self):
        half = self.own.shape[0] // 2
        self.far_one = self.cube.send(self.over_y[:half], self.cube.x)
        self.far_two = self.cube.send(self.over_x[half:], self.cube.y)

    def across(self):
        pieces = [self.own, self.over_x, self.over_y, self.far_one, self.far_two]
        self.pieces = pieces + [self.cube.send(piece, self.cube.core) for piece in pieces]


class Reduce:
    def __init__(self, cube, low, high):
        self.cube, self.low = cube, low
        self.got = cube.send(high, cube.core)

    def far(self):
        cube = self.cube
        self.own, self.to_x, self.to_y, far_x, far_y = core_add(self.low, self.got)
        self.got_y, self.got_x = cube.send(far_x, cube.x), cube.send(far_y, cube.y)

    def plane(self):
        cube = self.cube
        to_x, to_y = plane_add(self.to_x, self.got_x, self.to_y, self.got_y)
        self.got_x, self.got_y = cube.send(to_x, cube.x), cube.send(to_y, cube.y)

    def line(self):
        steps = list(reversed(self.cube.rest))
        self.own, away = own_add(self.own, self.got_x, self.got_y)
        self.got = self.cube.send(away, steps[0])

    def rest(self):
        steps = list(reversed(self.cube.rest))
        for step in steps[1:]:
            self.own, away = line_add(self.own, self.got)
            self.got = self.cube.send(away, step)

    def last(self, widths):
        return last_add(self.own, self.got, widths)


TILE = 128
HALF = 384


def nn(left, right):
    return lax.dot_general(left, right, (((1,), (0,)), ((), ())), preferred_element_type=f32)


def nt(left, right):
    return lax.dot_general(left, right, (((1,), (1,)), ((), ())), preferred_element_type=f32)


def tn(left, right):
    return lax.dot_general(left, right, (((0,), (0,)), ((), ())), preferred_element_type=f32)


def at(start, size):
    return pl.ds(pl.multiple_of(start, TILE), size)


VMEM = pl.BlockSpec(memory_space=pltpu.VMEM)
SMEM = pl.BlockSpec(memory_space=pltpu.SMEM)
ANY = pl.BlockSpec(memory_space=pl.ANY)


def shape(dims, kind):
    return jax.ShapeDtypeStruct(dims, kind)


def call(body, name, ins, outs, scratch, cost, *args):
    return pl.pallas_call(
        body,
        out_shape=[o[0] for o in outs],
        in_specs=ins,
        out_specs=[o[1] for o in outs],
        scratch_shapes=scratch,
        compiler_params=pltpu.CompilerParams(vmem_limit_bytes=60 * 2**20),
        cost_estimate=pl.CostEstimate(flops=0, bytes_accessed=int(cost * 3.6e6), transcendentals=0),
        name=name,
    )(*args)


def halves(value):
    lane = lax.broadcasted_iota(jnp.int32, value, 1)
    return (lane < HD, lane >= HD)


def inverse_rms(v):
    return lax.rsqrt(jnp.mean(v * v, axis=-1, keepdims=True) + norm_eps)


def norm_back(v, gain, dy, r):
    scaled = dy * gain
    mean = jnp.mean(scaled * v, axis=-1, keepdims=True)
    d_v = (scaled - v * (mean * (r * r))) * r
    return d_v, jnp.sum(dy * (v * r), axis=0, keepdims=True)


def softmax_rows(scores):
    top = jnp.max(scores, axis=-1, keepdims=True)
    expo = jnp.exp(scores - top)
    return (expo * (1.0 / jnp.sum(expo, axis=-1, keepdims=True))).astype(bf16)


def bias_body(lines, out):
    def one(i, _):
        line = lines[pl.ds(i, 1), :]
        wide = jnp.broadcast_to(line, (TILE, 2 * TILE))
        out[i] = pltpu.roll(wide, 0, 1, stride=1, stride_axis=0)[:, :TILE]
        return 0

    lax.fori_loop(0, out.shape[0], one, 0)


def copy_pieces(pieces, weights, sems, start=0):
    copies, row, cols = [], 0, weights.shape[1]
    for i, piece in enumerate(pieces):
        size = piece.shape[0]
        source = piece.at[:, pl.ds(start, cols)]
        copies.append(pltpu.make_async_copy(source, weights.at[pl.ds(row, size), :], sems.at[i]))
        copies[-1].start()
        row += size
    return copies


def wait(copies):
    for copy in copies:
        copy.wait()


def loop(count, body):
    def step(i, carry):
        body(i)
        return carry

    lax.fori_loop(0, count, step, 0)


WIDE = 2 * TILE


def wide(i, start=0):
    return pl.ds(pl.multiple_of(start + i * WIDE, TILE), WIDE)


def self_pairs(first, count, dec_len, bias, qkv, mixed, probs, probs_out, out_sems):
    tokens, inner = qkv.shape[0], qkv.shape[1] // 3
    blocks = tokens // TILE
    places = lax.broadcasted_iota(jnp.int32, (1, tokens), 1)
    limit = jnp.where(places < dec_len[0], 0.0, masked_score)

    def pair(i):
        lanes = at((first + i) * TILE, TILE)
        keys = qkv[:, at(inner + (first + i) * TILE, TILE)]
        values = qkv[:, at(2 * inner + (first + i) * TILE, TILE)]
        both = halves((TILE, TILE))
        for block in range(blocks):
            rows = pl.ds(block * TILE, TILE)
            seen = (block + 1) * TILE
            queries = qkv[rows, lanes]
            result = None
            for side in range(2):
                mine = jnp.where(both[side], queries, jnp.zeros_like(queries))
                scores = nt(mine, keys[:seen])
                strip = [bias[(2 * (first + i) + side) * blocks + block - j] for j in range(block + 1)]
                strip = strip[0] if block == 0 else jnp.concatenate(strip, axis=1)
                p = softmax_rows(scores + strip + limit[:, :seen])
                probs[2 * i + side, rows, pl.ds(0, seen)] = p
                got = nn(p, values[:seen])
                result = got if side == 0 else jnp.where(both[0], result, got)
            mixed[rows, at(i * TILE, TILE)] = result.astype(bf16)
        pltpu.make_async_copy(probs.at[pl.ds(2 * i, 2)], probs_out.at[pl.ds(2 * i, 2)], out_sems.at[i]).start()

    loop(count, pair)
    for i in range(count):
        pltpu.make_async_copy(probs.at[pl.ds(2 * i, 2)], probs_out.at[pl.ds(2 * i, 2)], out_sems.at[i]).wait()


def self_one_body(count, dec_len, x, bias, *refs):
    pieces, (gains, normed, qkv, mixed, probs_out, weights, probs, sems, out_sems) = refs[:10], refs[10:]
    copies = copy_pieces(pieces, weights, sems)
    xs = x[...].astype(f32)
    scaled = xs * inverse_rms(xs)
    wait(copies)
    gain_rows = jnp.transpose(weights[:, :TILE].astype(f32))
    gains[...] = gain_rows[:8]
    normed[...] = (scaled * gain_rows[0:1]).astype(bf16)

    def project(i):
        qkv[:, wide(i)] = nn(normed[...], weights[:, wide(i, TILE)]).astype(bf16)

    loop(qkv.shape[1] // WIDE, project)
    self_pairs(0, count, dec_len, bias, qkv, mixed, probs, probs_out, out_sems)


def self_two_body(first, count, dec_len, bias, qkv, mixed, probs_out, probs, out_sems):
    self_pairs(first, count, dec_len, bias, qkv, mixed, probs, probs_out, out_sems)


def cross_pairs(first, count, enc_len, queries, kv, mixed, probs, probs_out, out_sems):
    blocks, inner = queries.shape[0] // TILE, queries.shape[1]
    places = lax.broadcasted_iota(jnp.int32, (1, kv.shape[0]), 1)
    limit = jnp.where(places < enc_len[0], 0.0, masked_score)

    def pair(i):
        lanes = at((first + i) * TILE, TILE)
        keys = kv[:, lanes]
        values = kv[:, at(inner + (first + i) * TILE, TILE)]
        both = halves((TILE, TILE))
        for block in range(blocks):
            rows = pl.ds(block * TILE, TILE)
            here = queries[rows, lanes]
            result = None
            for side in range(2):
                mine = jnp.where(both[side], here, jnp.zeros_like(here))
                p = softmax_rows(nt(mine, keys) + limit)
                probs[2 * i + side, rows, :] = p
                got = nn(p, values)
                result = got if side == 0 else jnp.where(both[0], result, got)
            mixed[rows, at(i * TILE, TILE)] = result.astype(bf16)
        pltpu.make_async_copy(probs.at[pl.ds(2 * i, 2)], probs_out.at[pl.ds(2 * i, 2)], out_sems.at[i]).start()

    loop(count, pair)
    for i in range(count):
        pltpu.make_async_copy(probs.at[pl.ds(2 * i, 2)], probs_out.at[pl.ds(2 * i, 2)], out_sems.at[i]).wait()


def cross_one_body(count, enc_len, x, mixed_a, mixed_b, enc, gains, *refs):
    pieces, (hidden, normed, queries, kv, mixed, probs_out, weights, probs, sems, out_sems) = refs[:10], refs[10:]
    copies = copy_pieces(pieces, weights, sems)
    inner = queries.shape[1]
    part = mixed_a.shape[1]
    wait(copies)

    def enter(i):
        rows = wide(i)
        got = nt(mixed_a[...], weights[rows, pl.ds(0, part)]) + nt(mixed_b[...], weights[rows, pl.ds(part, inner - part)])
        hidden[:, rows] = x[:, rows].astype(f32) + got

    loop(hidden.shape[1] // WIDE, enter)
    v = hidden[...]
    normed[...] = (v * inverse_rms(v) * gains[1:2]).astype(bf16)

    def project_q(i):
        queries[:, wide(i)] = nn(normed[...], weights[:, wide(i, inner)]).astype(bf16)

    def project_kv(i):
        kv[:, wide(i)] = nn(enc[...], weights[:, wide(i, 2 * inner)]).astype(bf16)

    loop(inner // WIDE, project_q)
    loop(2 * inner // WIDE, project_kv)
    cross_pairs(0, count, enc_len, queries, kv, mixed, probs, probs_out, out_sems)


def cross_two_body(first, count, enc_len, hidden, queries, kv, mixed_a, *refs):
    pieces, (hidden_out, mixed, probs_out, weights, probs, sems, out_sems) = refs[:10], refs[10:]
    inner = queries.shape[1]
    part = mixed_a.shape[1]
    copies = copy_pieces(pieces, weights, sems, 4 * inner)
    cross_pairs(first, count, enc_len, queries, kv, mixed, probs, probs_out, out_sems)
    wait(copies)

    def leave(i):
        rows = wide(i)
        got = nt(mixed_a[...], weights[rows, pl.ds(0, part)]) + nt(mixed[...], weights[rows, pl.ds(part, inner - part)])
        hidden_out[:, rows] = hidden[:, rows] + got

    loop(hidden.shape[1] // WIDE, leave)


root_two_over_pi = math.sqrt(2.0 / math.pi)


def ffn_one_body(hidden, cot, gains, *refs):
    pieces, (normed, gated, slope, act, low, high, weights, sems) = refs[:10], refs[10:]
    copies = copy_pieces(pieces, weights, sems)
    ff = gated.shape[1]
    v = hidden[...]
    normed[...] = (v * inverse_rms(v) * gains[2:3]).astype(bf16)
    turned = jnp.transpose(cot[...])
    wait(copies)

    def unit(i):
        cols = wide(i)
        gate = nn(normed[...], weights[:, cols])
        up = nn(normed[...], weights[:, wide(i, ff)])
        square = gate * gate
        bend = jnp.tanh(root_two_over_pi * gate * (1.0 + 0.044715 * square))
        half = 0.5 * (1.0 + bend)
        gelu = gate * half
        steep = half + 0.5 * gate * (1.0 - bend * bend) * (root_two_over_pi * (1.0 + 3 * 0.044715 * square))
        units = (gelu * up).astype(bf16)
        gated[:, cols] = units
        slope[:, cols] = (up * steep).astype(bf16)
        act[:, cols] = gelu.astype(bf16)
        part = nn(turned, units)
        low[:, cols] = part[:HALF].astype(bf16)
        high[:, cols] = part[HALF:].astype(bf16)

    loop(ff // WIDE, unit)


def ffn_two_body(cot, normed, slope, act, *refs):
    pieces, (low, high, d_gu, weights, sems) = refs[:10], refs[10:]
    copies = copy_pieces(pieces, weights, sems)
    ff = slope.shape[1]
    turned = jnp.transpose(normed[...])
    wait(copies)

    def unit(i):
        cols, other = wide(i), wide(i, ff)
        d_gated = nn(cot[...], weights[:, cols])
        d_gate = (d_gated * slope[:, cols].astype(f32)).astype(bf16)
        d_up = (d_gated * act[:, cols].astype(f32)).astype(bf16)
        d_gu[:, cols] = d_gate
        d_gu[:, other] = d_up
        part = nn(turned, d_gate)
        low[:, cols] = part[:HALF].astype(bf16)
        high[:, cols] = part[HALF:].astype(bf16)
        part = nn(turned, d_up)
        low[:, other] = part[:HALF].astype(bf16)
        high[:, other] = part[HALF:].astype(bf16)

    loop(ff // WIDE, unit)


def ffn_three_body(hidden, cot, gains, d_gu, *refs):
    pieces, (d_hidden, d_low, d_gain, weights, sems) = refs[:10], refs[10:]
    copies = copy_pieces(pieces, weights, sems)
    wait(copies)

    def back(i):
        d_hidden[:, wide(i)] = nt(d_gu[...], weights[wide(i), :])

    loop(hidden.shape[1] // WIDE, back)
    v = hidden[...]
    d_v, d_g = norm_back(v, gains[2:3], d_hidden[...], inverse_rms(v))
    d_v = d_v + cot[...].astype(f32)
    d_hidden[...] = d_v
    d_low[...] = d_v.astype(bf16)
    d_gain[...] = d_g


def output_body(hidden, gated, perm, *refs):
    pieces, (out, weights, held, sems) = refs[:10], refs[10:]
    copies = copy_pieces(pieces, weights, sems)
    wait(copies)

    def leave(i):
        held[:, wide(i)] = (hidden[:, wide(i)] + nt(gated[...], weights[wide(i), :])).astype(bf16)

    def place(i):
        out[:, wide(i)] = nt(held[...], perm[wide(i), :]).astype(bf16)

    loop(hidden.shape[1] // WIDE, leave)
    loop(hidden.shape[1] // WIDE, place)


def enc_body(d_kv_a, d_kv_b, perm, *refs):
    pieces, (out, weights, held, sems) = refs[:10], refs[10:]
    inner = held.shape[1]
    copies = copy_pieces(pieces, weights, sems, 2 * inner)
    part = d_kv_a.shape[1] // 2
    rest = inner - part
    wait(copies)

    def leave(i):
        rows = wide(i)
        got = nt(d_kv_a[:, pl.ds(0, part)], weights[rows, pl.ds(0, part)])
        got = got + nt(d_kv_b[:, pl.ds(0, rest)], weights[rows, pl.ds(part, rest)])
        got = got + nt(d_kv_a[:, pl.ds(part, part)], weights[rows, pl.ds(inner, part)])
        got = got + nt(d_kv_b[:, pl.ds(rest, rest)], weights[rows, pl.ds(inner + part, rest)])
        held[:, rows] = got.astype(bf16)

    def place(i):
        out[:, wide(i)] = nt(held[...], perm[wide(i), :]).astype(bf16)

    loop(out.shape[1] // WIDE, leave)
    loop(out.shape[1] // WIDE, place)


def attention_back(side, rows, seen, p, d_mixed, mixed, keys, values, d_scores):
    lanes = halves((TILE, TILE))[side]
    d_out = jnp.where(lanes, d_mixed, jnp.zeros_like(d_mixed))
    delta = jnp.sum(d_out.astype(f32) * mixed.astype(f32), axis=-1, keepdims=True)
    d_s = (p.astype(f32) * (nt(d_out, values) - delta)).astype(bf16)
    d_scores[side, rows, pl.ds(0, seen)] = d_s
    return d_s, nn(d_s, keys)


def fetch_probs(probs_in, probs, in_sems):
    copies = []
    for i in range(probs.shape[0] // 2):
        copies.append(pltpu.make_async_copy(probs_in.at[pl.ds(2 * i, 2)], probs.at[pl.ds(2 * i, 2)], in_sems.at[i]))
        copies[-1].start()


def cross_back_pairs(first, count, queries, kv, mixed, d_mixed, probs_in, probs, in_sems, d_q, d_kv, d_scores):
    blocks, inner = queries.shape[0] // TILE, queries.shape[1]

    def pair(i):
        pltpu.make_async_copy(probs_in.at[pl.ds(2 * i, 2)], probs.at[pl.ds(2 * i, 2)], in_sems.at[i]).wait()
        lanes, mine = at((first + i) * TILE, TILE), at(i * TILE, TILE)
        keys, values = kv[:, lanes], kv[:, at(inner + (first + i) * TILE, TILE)]
        d_mix, here = d_mixed[:, lanes], queries[:, lanes]
        both, zero = halves(keys.shape), jnp.zeros_like(keys)
        d_k = d_v = None
        for side in range(2):
            my_keys = jnp.where(both[side], keys, zero)
            for block in range(blocks):
                rows = pl.ds(block * TILE, TILE)
                span = slice(block * TILE, (block + 1) * TILE)
                p = probs[2 * i + side, rows, :]
                _, part = attention_back(side, rows, kv.shape[0], p, d_mix[span], mixed[rows, mine], my_keys, values, d_scores)
                if side == 0:
                    d_q[rows, mine] = part.astype(bf16)
                else:
                    d_q[rows, mine] = (d_q[rows, mine].astype(f32) + part).astype(bf16)
            part_v = tn(probs[2 * i + side], jnp.where(both[side], d_mix, zero))
            part_k = tn(d_scores[side], jnp.where(both[side], here, zero))
            d_v = part_v if side == 0 else d_v + part_v
            d_k = part_k if side == 0 else d_k + part_k
        d_kv[:, mine] = d_k.astype(bf16)
        d_kv[:, at((count + i) * TILE, TILE)] = d_v.astype(bf16)

    loop(count, pair)


def cross_back_one_body(count, d_low, queries, kv, mixed, *refs):
    pieces, probs_in, (d_mixed, d_q, d_kv, weights, probs, d_scores, sems, in_sems) = refs[:10], refs[10], refs[11:]
    inner = queries.shape[1]
    copies = copy_pieces(pieces, weights, sems, 4 * inner)
    fetch_probs(probs_in, probs, in_sems)
    wait(copies)

    def enter(i):
        d_mixed[:, wide(i)] = nn(d_low[...], weights[:, wide(i)]).astype(bf16)

    loop(inner // WIDE, enter)
    cross_back_pairs(0, count, queries, kv, mixed, d_mixed, probs_in, probs, in_sems, d_q, d_kv, d_scores)


def put(low, high, cols, part):
    low[:, cols] = part[:HALF].astype(bf16)
    high[:, cols] = part[HALF:].astype(bf16)


def cross_back_two_body(first, count, *refs):
    (hidden, d_hidden, d_low, enc, gains, normed, queries, kv, mixed_a, mixed_b, one_a, one_b, d_mixed, d_q_a, d_kv_a) = refs[:15]
    pieces, probs_in = refs[15:25], refs[25]
    low, high, d_kv_b, d_out, d_out_low, d_gain, weights, probs, d_q_b, d_scores, sems, in_sems = refs[26:]
    inner = queries.shape[1]
    part = mixed_a.shape[1]
    rest = inner - part
    copies = copy_pieces(pieces, weights, sems, inner)
    fetch_probs(probs_in, probs, in_sems)
    cross_back_pairs(first, count, queries, kv, mixed_b, d_mixed, probs_in, probs, in_sems, d_q_b, d_kv_b, d_scores)
    wait(copies)

    def back(i):
        got = nt(d_q_a[...], weights[wide(i), pl.ds(0, part)]) + nt(d_q_b[...], weights[wide(i), pl.ds(part, rest)])
        d_out[:, wide(i)] = got

    loop(hidden.shape[1] // WIDE, back)
    v = hidden[...]
    d_v, d_g = norm_back(v, gains[1:2], d_out[...], inverse_rms(v))
    d_v = d_v + d_hidden[...]
    d_out[...] = d_v
    d_out_low[...] = d_v.astype(bf16)
    d_gain[...] = d_g
    turned = jnp.transpose(d_out_low[...])
    put(low, high, pl.ds(0, part), nn(turned, one_a[...]))
    put(low, high, pl.ds(part, rest), nn(turned, one_b[...]))
    turned = jnp.transpose(normed[...])
    put(low, high, pl.ds(inner, part), nn(turned, d_q_a[...]))
    put(low, high, pl.ds(inner + part, rest), nn(turned, d_q_b[...]))
    turned = jnp.transpose(enc[...])
    for i in range(2):
        put(low, high, pl.ds((2 + i) * inner, part), nn(turned, d_kv_a[:, pl.ds(i * part, part)]))
        put(low, high, pl.ds((2 + i) * inner + part, rest), nn(turned, d_kv_b[:, pl.ds(i * rest, rest)]))
    turned = jnp.transpose(d_low[...])
    put(low, high, pl.ds(4 * inner, part), nn(turned, mixed_a[...]))
    put(low, high, pl.ds(4 * inner + part, rest), nn(turned, mixed_b[...]))


def self_back_pairs(first, count, qkv, mixed, d_mixed, probs_in, probs, in_sems, d_qkv, d_scores, work, sums):
    tokens, inner = qkv.shape[0], qkv.shape[1] // 3
    blocks = tokens // TILE

    def pair(i):
        pltpu.make_async_copy(probs_in.at[pl.ds(2 * i, 2)], probs.at[pl.ds(2 * i, 2)], in_sems.at[i]).wait()
        lanes, mine = at((first + i) * TILE, TILE), at(i * TILE, TILE)
        here, keys = qkv[:, lanes], qkv[:, at(inner + (first + i) * TILE, TILE)]
        values = qkv[:, at(2 * inner + (first + i) * TILE, TILE)]
        d_mix = d_mixed[:, lanes]
        both, zero = halves(keys.shape), jnp.zeros_like(keys)
        for side in range(2):
            head = 2 * i + side
            my_keys = jnp.where(both[side], keys, zero)
            diagonal = [None] * blocks
            for block in range(blocks):
                rows = pl.ds(block * TILE, TILE)
                span = slice(block * TILE, (block + 1) * TILE)
                seen = (block + 1) * TILE
                p = probs[head, rows, pl.ds(0, seen)]
                d_s, part = attention_back(
                    side, rows, seen, p, d_mix[span], mixed[rows, mine], my_keys[:seen], values[:seen], d_scores
                )
                wider = d_s.astype(f32)
                for j in range(block + 1):
                    tile = wider[:, j * TILE : (j + 1) * TILE]
                    apart = block - j
                    diagonal[apart] = tile if diagonal[apart] is None else diagonal[apart] + tile
                if side == 0:
                    d_qkv[rows, mine] = part.astype(bf16)
                else:
                    d_qkv[rows, mine] = (d_qkv[rows, mine].astype(f32) + part).astype(bf16)
            for apart in range(blocks):
                tile = jnp.concatenate([diagonal[apart], jnp.zeros((TILE, TILE), f32)], axis=1)
                folded = tile[:8]
                for group in range(1, TILE // 8):
                    folded = folded + pltpu.roll(tile[group * 8 : group * 8 + 8], 2 * TILE - 8 * group, 1)
                sums[head * blocks + apart] = folded
            d_o = jnp.where(both[side], d_mix, zero)
            q_o = jnp.where(both[side], here, zero)
            for j in range(blocks):
                start = j * TILE
                rows, out_rows = pl.ds(start, tokens - start), pl.ds(start, TILE)
                part_v = tn(probs[head, rows, pl.ds(start, TILE)], d_o[start:])
                part_k = tn(d_scores[side, rows, pl.ds(start, TILE)], q_o[start:])
                if side == 0:
                    work[0, out_rows, :] = part_v
                    work[1, out_rows, :] = part_k
                else:
                    d_qkv[out_rows, at((count + i) * TILE, TILE)] = (work[1, out_rows, :] + part_k).astype(bf16)
                    d_qkv[out_rows, at((2 * count + i) * TILE, TILE)] = (work[0, out_rows, :] + part_v).astype(bf16)

    loop(count, pair)


def self_back_one_body(count, d_low, normed, qkv, mixed, *refs):
    pieces, probs_in = refs[:10], refs[10]
    low, high, d_mixed, d_qkv, sums, weights, probs, d_scores, work, sems, in_sems = refs[11:]
    inner = qkv.shape[1] // 3
    copies = copy_pieces(pieces, weights, sems)
    fetch_probs(probs_in, probs, in_sems)
    turned = jnp.transpose(normed[...])
    wait(copies)

    def enter(i):
        d_mixed[:, wide(i)] = nn(d_low[...], weights[:, wide(i)]).astype(bf16)

    loop(inner // WIDE, enter)
    self_back_pairs(0, count, qkv, mixed, d_mixed, probs_in, probs, in_sems, d_qkv, d_scores, work, sums)
    part = count * TILE

    def grads(i):
        cols = pl.ds(pl.multiple_of(i * part, TILE), part)
        put(low, high, cols, nn(turned, d_qkv[:, cols]))

    loop(3, grads)


def self_back_two_body(first, count, *refs):
    x, d_hidden, gains, normed, qkv, mixed, gain_c, gain_f, d_mixed, d_qkv_a, perm = refs[:11]
    pieces, probs_in = refs[11:21], refs[21]
    low, high, d_x, sums, weights, probs, d_qkv, d_scores, work, total, sems, in_sems = refs[22:]
    inner = qkv.shape[1] // 3
    copies = copy_pieces(pieces, weights, sems, TILE)
    fetch_probs(probs_in, probs, in_sems)
    turned = jnp.transpose(normed[...])
    self_back_pairs(first, count, qkv, mixed, d_mixed, probs_in, probs, in_sems, d_qkv, d_scores, work, sums)
    wait(copies)
    part, rest = inner - count * TILE, count * TILE

    def back(i):
        got = None
        for j in range(3):
            one = nt(d_qkv_a[:, pl.ds(j * part, part)], weights[wide(i), pl.ds(j * inner, part)])
            got = one if got is None else got + one
            got = got + nt(d_qkv[:, pl.ds(j * rest, rest)], weights[wide(i), pl.ds(j * inner + part, rest)])
        total[:, wide(i)] = got

    loop(x.shape[1] // WIDE, back)
    v = x[...].astype(f32)
    d_v, d_g = norm_back(v, gains[0:1], total[...], inverse_rms(v))
    d_x[...] = (d_v + d_hidden[...]).astype(bf16)
    rows = jnp.concatenate([d_g, gain_c[...], gain_f[...], jnp.zeros((TILE - 3, d_g.shape[1]), f32)], axis=0)
    put(low, high, pl.ds(0, TILE), jnp.transpose(rows))

    def grads(i):
        cols = pl.ds(pl.multiple_of(i * rest, TILE), rest)
        put(low, high, pl.ds(pl.multiple_of(TILE + i * rest, TILE), rest), nn(turned, d_qkv[:, cols]))

    loop(3, grads)


def place_body(value, perm, out):
    def place(i):
        out[:, wide(i)] = nt(value[...], perm[wide(i), :]).astype(bf16)

    loop(out.shape[1] // WIDE, place)


def pack_body(*refs):
    gains, sq, sk, sv, so, cq, ck, cv, co, fg, fu, fo, first, second, third, fourth = refs
    for out, parts in ((first, (gains, sq, sk, sv)), (second, (so, cq, ck, cv, co)), (third, (fg, fu)), (fourth, (fo,))):
        start = 0
        for part in parts:
            out[:, pl.ds(start, part.shape[1])] = part[...]
            start += part.shape[1]


def core_add_body(low, got, own, to_x, to_y, far_x, far_y):
    size = HALF // 4
    total = low[...].astype(f32) + got[...].astype(f32)
    total = total.astype(bf16)
    own[...] = total[:size]
    to_x[...] = total[size : 2 * size]
    to_y[...] = total[2 * size : 3 * size]
    far_x[...] = total[3 * size : 3 * size + size // 2]
    far_y[...] = total[3 * size + size // 2 :]


def core_add(low, got):
    rows, cols = low.shape
    size = rows // 4
    steps = max(n for n in (5, 4, 3, 2, 1) if cols % (n * TILE) == 0)
    block = cols // steps
    sizes = (size, size, size, size // 2, size // 2)
    return pl.pallas_call(
        core_add_body,
        grid=(steps,),
        out_shape=[shape((s, cols), bf16) for s in sizes],
        in_specs=[pl.BlockSpec((rows, block), lambda i: (0, i))] * 2,
        out_specs=[pl.BlockSpec((s, block), lambda i: (0, i)) for s in sizes],
        compiler_params=pltpu.CompilerParams(vmem_limit_bytes=48 * 2**20),
        cost_estimate=pl.CostEstimate(flops=rows * cols, bytes_accessed=6 * rows * cols, transcendentals=0),
        name="core_add",
    )(low, got)


def plane_add_body(to_x, got_x, to_y, got_y, out_x, out_y):
    half = got_x.shape[0]
    out_x[pl.ds(0, half), :] = to_x[pl.ds(0, half), :]
    out_x[pl.ds(half, half), :] = (to_x[pl.ds(half, half), :].astype(f32) + got_x[...].astype(f32)).astype(bf16)
    out_y[pl.ds(0, half), :] = (to_y[pl.ds(0, half), :].astype(f32) + got_y[...].astype(f32)).astype(bf16)
    out_y[pl.ds(half, half), :] = to_y[pl.ds(half, half), :]


def plane_add(to_x, got_x, to_y, got_y):
    return call(
        plane_add_body, "plane_add", [VMEM] * 4, [(shape(to_x.shape, bf16), VMEM)] * 2, [], 2.0, to_x, got_x, to_y, got_y
    )


def own_add_body(own, got_x, got_y, keep, away):
    half = keep.shape[0]
    total = own[...].astype(f32) + got_x[...].astype(f32) + got_y[...].astype(f32)
    keep[...] = total[:half].astype(bf16)
    away[...] = total[half:].astype(bf16)


def own_add(own, got_x, got_y):
    half = shape((own.shape[0] // 2, own.shape[1]), bf16)
    return call(own_add_body, "own_add", [VMEM] * 3, [(half, VMEM)] * 2, [], 2.0, own, got_x, got_y)


def line_add_body(own, got, keep, away):
    half = keep.shape[0]
    total = own[...].astype(f32) + got[...].astype(f32)
    keep[...] = total[:half].astype(bf16)
    away[...] = total[half:].astype(bf16)


def line_add(own, got):
    half = shape((own.shape[0] // 2, own.shape[1]), bf16)
    return call(line_add_body, "line_add", [VMEM] * 2, [(half, VMEM)] * 2, [], 1.5, own, got)


def last_add_body(own, got, *outs):
    start = 0
    for out in outs:
        cols = pl.ds(start, out.shape[1])
        out[...] = own[:, cols].astype(f32) + got[:, cols].astype(f32)
        start += out.shape[1]


def last_add(own, got, widths):
    outs = [(shape((own.shape[0], w), f32), VMEM) for w in widths]
    return call(last_add_body, "last_add", [VMEM] * 2, outs, [], 1.5, own, got)


def bucket_of(distance):
    bucket = np.where(distance < 16, distance, 16)
    for edge in bucket_edges:
        bucket = bucket + (distance >= edge)
    return np.maximum(bucket, 0)


def split_last_body(own_a, got_a, own_b, got_b, gains, *outs):
    part = own_a.shape[1] // 3
    rest = (own_b.shape[1] - TILE) // 3
    gains[...] = own_b[:, pl.ds(0, TILE)].astype(f32) + got_b[:, pl.ds(0, TILE)].astype(f32)
    for i, out in enumerate(outs):
        cols = pl.ds(i * part, part)
        out[:, pl.ds(0, part)] = own_a[:, cols].astype(f32) + got_a[:, cols].astype(f32)
        cols = pl.ds(TILE + i * rest, rest)
        out[:, pl.ds(part, rest)] = own_b[:, cols].astype(f32) + got_b[:, cols].astype(f32)


def layer(
    cube,
    states,
    encoded,
    cotangent,
    dec_lens,
    enc_lens,
    self_query,
    self_key,
    self_value,
    self_out,
    cross_query,
    cross_key,
    cross_value,
    cross_out,
    ffn_gate,
    ffn_up,
    ffn_out,
    gain_self,
    gain_cross,
    gain_ffn,
    table,
):
    _, tokens, width = states.shape
    enc_tokens = encoded.shape[1]
    inner, ff = self_query.shape[1], ffn_gate.shape[1]
    own_rows = self_query.shape[0]
    blocks = tokens // TILE
    pairs = inner // TILE
    early = pairs // 2
    late = pairs - early
    part, rest = early * TILE, late * TILE
    sems = pltpu.SemaphoreType.DMA

    def weight_mem(cols):
        return pltpu.VMEM((width, cols), bf16)

    def mem(*dims):
        return pltpu.VMEM(dims, bf16)

    gains_in = jnp.pad(jnp.stack([gain_self, gain_cross, gain_ffn], axis=1), ((0, 0), (0, TILE - 3)))
    widths = (TILE + 3 * inner, 5 * inner, 2 * ff, ff)
    packed = call(
        pack_body,
        "pack",
        [VMEM] * 12,
        [(shape((own_rows, w), bf16), VMEM) for w in widths],
        [],
        2.0,
        *(gains_in, self_query, self_key, self_value, self_out, cross_query, cross_key, cross_value, cross_out, ffn_gate, ffn_up, ffn_out),
    )
    A, B, C, D = (Gather(cube, p) for p in packed)
    perm = cube.permutation(width)
    x = nn(states[0], perm).astype(bf16)

    lane = np.arange(2 * TILE)
    signed = np.where(lane < TILE, lane, lane - 2 * TILE)
    distance = np.arange(blocks)[:, None] * TILE - signed[None, :]
    chosen = (np.arange(NB)[:, None] == bucket_of(distance).reshape(1, -1)).astype(np.float32)
    lines = lax.dot_general(table, jnp.asarray(chosen, bf16), (((0,), (0,)), ((), ())), preferred_element_type=f32)
    lines = jnp.where(jnp.asarray(distance.reshape(1, -1) >= 0), lines, masked_score)
    lines = lines.reshape(H * blocks, 2 * TILE)
    (bias,) = call(bias_body, "bias", [VMEM], [(shape((H * blocks, TILE, TILE), f32), VMEM)], [], 7.0, lines)
    enc = nn(encoded[0], perm).astype(bf16)
    cot = nn(cotangent[0], perm).astype(bf16)

    token_bf = shape((tokens, width), bf16)
    token_f32 = shape((tokens, width), f32)
    row_f32 = shape((1, width), f32)

    A.line(cube.rest)
    A.own, B.own, C.own, D.own = tie(A.own, B.own, C.own, D.own)
    A.plane()
    B.line(cube.rest[:1])
    A.own, A.over_x, A.over_y, B.own, C.own, D.own, enc, cot, bias = tie(A.own, A.over_x, A.over_y, B.own, C.own, D.own, enc, cot, bias)
    A.far()
    B.line(cube.rest[1:])
    A.far_one, A.far_two, B.own, C.own, D.own = tie(A.far_one, A.far_two, B.own, C.own, D.own)
    A.across()
    B.plane()
    C.line(cube.rest[:1])
    gains, normed_one, qkv, mixed_one_a, probs_one_a = call(
        lambda *refs: self_one_body(early, *refs),
        "self_one",
        [SMEM, VMEM, VMEM] + [ANY] * 10,
        [
            (shape((8, width), f32), VMEM),
            (token_bf, VMEM),
            (shape((tokens, 3 * inner), bf16), VMEM),
            (shape((tokens, part), bf16), VMEM),
            (shape((2 * early, tokens, tokens), bf16), ANY),
        ],
        [weight_mem(widths[0]), mem(2 * early, tokens, tokens), sems((10,)), sems((early,))],
        16.0,
        *(dec_lens, x, bias, *A.pieces),
    )
    qkv, B.own, B.over_x, B.over_y, C.own, D.own = tie(qkv, B.own, B.over_x, B.over_y, C.own, D.own)
    B.far()
    C.line(cube.rest[1:])
    mixed_one_b, probs_one_b = call(
        lambda *refs: self_two_body(early, late, *refs),
        "self_two",
        [SMEM, VMEM, VMEM],
        [(shape((tokens, rest), bf16), VMEM), (shape((2 * late, tokens, tokens), bf16), ANY)],
        [mem(2 * late, tokens, tokens), sems((late,))],
        13.0,
        *(dec_lens, bias, qkv),
    )
    mixed_one_b, B.own, B.over_x, B.over_y, B.far_one, B.far_two, C.own, D.own = tie(
        mixed_one_b, B.own, B.over_x, B.over_y, B.far_one, B.far_two, C.own, D.own
    )
    B.across()
    C.plane()
    D.line(cube.rest[:1])
    hidden_one, normed_two, q_two, kv_two, mixed_two_a, probs_two_a = call(
        lambda *refs: cross_one_body(early, *refs),
        "cross_one",
        [SMEM] + [VMEM] * 5 + [ANY] * 10,
        [
            (token_f32, VMEM),
            (token_bf, VMEM),
            (shape((tokens, inner), bf16), VMEM),
            (shape((enc_tokens, 2 * inner), bf16), VMEM),
            (shape((tokens, part), bf16), VMEM),
            (shape((2 * early, tokens, enc_tokens), bf16), ANY),
        ],
        [weight_mem(4 * inner), mem(2 * early, tokens, enc_tokens), sems((10,)), sems((early,))],
        18.0,
        *(enc_lens, x, mixed_one_a, mixed_one_b, enc, gains, *B.pieces),
    )
    q_two, C.own, C.over_x, C.over_y, D.own = tie(q_two, C.own, C.over_x, C.over_y, D.own)
    C.far()
    D.line(cube.rest[1:])
    hidden_two, mixed_two_b, probs_two_b = call(
        lambda *refs: cross_two_body(early, late, *refs),
        "cross_two",
        [SMEM] + [VMEM] * 4 + [ANY] * 10,
        [(token_f32, VMEM), (shape((tokens, rest), bf16), VMEM), (shape((2 * late, tokens, enc_tokens), bf16), ANY)],
        [weight_mem(inner), mem(2 * late, tokens, enc_tokens), sems((10,)), sems((late,))],
        14.0,
        *(enc_lens, hidden_one, q_two, kv_two, mixed_two_a, *B.pieces),
    )
    hidden_two, C.own, C.over_x, C.over_y, C.far_one, C.far_two, D.own = tie(
        hidden_two, C.own, C.over_x, C.over_y, C.far_one, C.far_two, D.own
    )
    C.across()
    D.plane()
    units = shape((tokens, ff), bf16)
    half_ff = shape((HALF, ff), bf16)
    normed_three, gated, slope, act, fo_low, fo_high = call(
        ffn_one_body,
        "ffn_one",
        [VMEM] * 3 + [ANY] * 10,
        [(token_bf, VMEM)] + [(units, VMEM)] * 3 + [(half_ff, VMEM)] * 2,
        [weight_mem(2 * ff), sems((10,))],
        14.0,
        *(hidden_two, cot, gains, *C.pieces),
    )
    fo_low, fo_high, slope, D.own, D.over_x, D.over_y = tie(fo_low, fo_high, slope, D.own, D.over_x, D.over_y)
    D.far()
    R1 = Reduce(cube, fo_low, fo_high)
    D.across()
    half_gu = shape((HALF, 2 * ff), bf16)
    gu_low, gu_high, d_gu = call(
        ffn_two_body,
        "ffn_two",
        [VMEM] * 4 + [ANY] * 10,
        [(half_gu, VMEM), (half_gu, VMEM), (shape((tokens, 2 * ff), bf16), VMEM)],
        [weight_mem(ff), sems((10,))],
        14.0,
        *(cot, normed_three, slope, act, *D.pieces),
    )
    R1.got, gu_low, gu_high, d_gu = tie(R1.got, gu_low, gu_high, d_gu)
    R1.far()
    R2 = Reduce(cube, gu_low, gu_high)
    d_hidden_two, d_low_two, gain_f = call(
        ffn_three_body,
        "ffn_three",
        [VMEM] * 4 + [ANY] * 10,
        [(token_f32, VMEM), (token_bf, VMEM), (row_f32, VMEM)],
        [weight_mem(2 * ff), sems((10,))],
        8.0,
        *(hidden_two, cot, gains, d_gu, *C.pieces),
    )
    R1.got_x, R1.got_y, R2.got, d_low_two = tie(R1.got_x, R1.got_y, R2.got, d_low_two)
    R1.plane()
    R2.far()
    d_mixed_two, d_q_a, d_kv_a = call(
        lambda *refs: cross_back_one_body(early, *refs),
        "cross_back_one",
        [VMEM] * 4 + [ANY] * 11,
        [
            (shape((tokens, inner), bf16), VMEM),
            (shape((tokens, part), bf16), VMEM),
            (shape((enc_tokens, 2 * part), bf16), VMEM),
        ],
        [
            weight_mem(inner),
            mem(2 * early, tokens, enc_tokens),
            mem(2, tokens, enc_tokens),
            sems((10,)),
            sems((early,)),
        ],
        14.0,
        *(d_low_two, q_two, kv_two, mixed_two_a, *B.pieces, probs_two_a),
    )
    R1.got_x, R1.got_y, R2.got_x, R2.got_y, d_mixed_two = tie(R1.got_x, R1.got_y, R2.got_x, R2.got_y, d_mixed_two)
    R1.line()
    R2.plane()
    half_cross = shape((HALF, 5 * inner), bf16)
    cross_low, cross_high, d_kv_b, d_hidden_one, d_low_one, gain_c = call(
        lambda *refs: cross_back_two_body(early, late, *refs),
        "cross_back_two",
        [VMEM] * 15 + [ANY] * 11,
        [
            (half_cross, VMEM),
            (half_cross, VMEM),
            (shape((enc_tokens, 2 * rest), bf16), VMEM),
            (token_f32, VMEM),
            (token_bf, VMEM),
            (row_f32, VMEM),
        ],
        [
            weight_mem(inner),
            mem(2 * late, tokens, enc_tokens),
            mem(tokens, rest),
            mem(2, tokens, enc_tokens),
            sems((10,)),
            sems((late,)),
        ],
        20.0,
        *(hidden_one, d_hidden_two, d_low_two, enc, gains, normed_two, q_two, kv_two, mixed_two_a, mixed_two_b),
        *(mixed_one_a, mixed_one_b, d_mixed_two, d_q_a, d_kv_a, *B.pieces, probs_two_b),
    )
    R1.got, R2.got_x, R2.got_y, cross_low, cross_high, d_low_one = tie(
        R1.got, R2.got_x, R2.got_y, cross_low, cross_high, d_low_one
    )
    R3 = Reduce(cube, cross_low, cross_high)
    R1.rest()
    R2.line()
    (output,) = call(
        output_body,
        "output",
        [VMEM] * 3 + [ANY] * 10,
        [(token_bf, VMEM)],
        [weight_mem(ff), mem(tokens, width), sems((10,))],
        7.0,
        *(tie(hidden_two, cross_low)[0], gated, perm, *D.pieces),
    )
    R3.got, output, d_low_one = tie(R3.got, output, d_low_one)
    R3.far()
    half_a = shape((HALF, 3 * part), bf16)
    sums_a_shape = shape((2 * early * blocks, 8, 2 * TILE), f32)
    self_low_a, self_high_a, d_mixed_one, d_qkv_a, sums_a = call(
        lambda *refs: self_back_one_body(early, *refs),
        "self_back_one",
        [VMEM] * 4 + [ANY] * 11,
        [
            (half_a, VMEM),
            (half_a, VMEM),
            (shape((tokens, inner), bf16), VMEM),
            (shape((tokens, 3 * part), bf16), VMEM),
            (sums_a_shape, VMEM),
        ],
        [
            weight_mem(inner),
            mem(2 * early, tokens, tokens),
            mem(2, tokens, tokens),
            pltpu.VMEM((2, tokens, TILE), f32),
            sems((10,)),
            sems((early,)),
        ],
        16.0,
        *(d_low_one, normed_one, qkv, mixed_one_a, *B.pieces, probs_one_a),
    )
    R1.got, R2.got, R3.got_x, R3.got_y, self_low_a, self_high_a, d_qkv_a = tie(
        R1.got, R2.got, R3.got_x, R3.got_y, self_low_a, self_high_a, d_qkv_a
    )
    R4 = Reduce(cube, self_low_a, self_high_a)
    R3.plane()
    R2.rest()
    (g_fo,) = R1.last((ff,))
    half_b = shape((HALF, TILE + 3 * rest), bf16)
    sums_b_shape = shape((2 * late * blocks, 8, 2 * TILE), f32)
    self_low_b, self_high_b, d_x, sums_b = call(
        lambda *refs: self_back_two_body(early, late, *refs),
        "self_back_two",
        [VMEM] * 11 + [ANY] * 11,
        [(half_b, VMEM), (half_b, VMEM), (token_bf, VMEM), (sums_b_shape, VMEM)],
        [
            weight_mem(3 * inner),
            mem(2 * late, tokens, tokens),
            mem(tokens, 3 * rest),
            mem(2, tokens, tokens),
            pltpu.VMEM((2, tokens, TILE), f32),
            pltpu.VMEM((tokens, width), f32),
            sems((10,)),
            sems((late,)),
        ],
        18.0,
        *(x, d_hidden_one, gains, normed_one, qkv, mixed_one_b, gain_c, gain_f, d_mixed_one, d_qkv_a, perm),
        *(*A.pieces, probs_one_b),
    )
    R4.got, R3.got_x, R3.got_y, R2.got, self_low_b, self_high_b, d_x, sums_b = tie(
        R4.got, R3.got_x, R3.got_y, R2.got, self_low_b, self_high_b, d_x, sums_b
    )
    R5 = Reduce(cube, self_low_b, self_high_b)
    R4.far()
    R3.line()
    (grad_enc,) = call(
        enc_body,
        "grad_encoded",
        [VMEM] * 3 + [ANY] * 10,
        [(shape((enc_tokens, width), bf16), VMEM)],
        [weight_mem(2 * inner), mem(enc_tokens, width), sems((10,))],
        7.0,
        *(tie(d_kv_a, sums_b)[0], d_kv_b, perm, *B.pieces),
    )
    R5.far()
    R4.plane()
    R3.rest()
    (grad_states,) = call(place_body, "grad_states", [VMEM] * 2, [(token_bf, VMEM)], [], 3.0, d_x, perm)
    g_fg, g_fu = R2.last((ff, ff))

    apart = distance[:, None, :] + np.arange(8)[None, :, None]
    counted = (np.arange(NB)[:, None] == bucket_of(apart).reshape(1, -1)) & (apart.reshape(1, -1) >= 0)
    sums = jnp.concatenate([sums_a, sums_b], axis=0).reshape(H, blocks * 16 * TILE)
    table_part = lax.dot_general(
        jnp.asarray(counted.astype(np.float32)), sums, (((1,), (1,)), ((), ())), precision=lax.Precision.HIGHEST
    )
    grad_table = cube.all_sum(table_part)

    R5.plane()
    R4.line()
    g_so, g_cq, g_ck, g_cv, g_co = R3.last((inner,) * 5)
    R5.line()
    R4.rest()
    R5.rest()
    sizes = (TILE, inner, inner, inner)
    g_gains, g_sq, g_sk, g_sv = call(
        split_last_body,
        "last_self",
        [VMEM] * 4,
        [(shape((own_rows, w), f32), VMEM) for w in sizes],
        [],
        1.5,
        *(R4.own, R4.got, R5.own, R5.got),
    )
    return (
        output[None],
        grad_states[None],
        grad_enc[None],
        g_sq,
        g_sk,
        g_sv,
        g_so,
        g_cq,
        g_ck,
        g_cv,
        g_co,
        g_fg,
        g_fu,
        g_fo,
        g_gains[:, 0],
        g_gains[:, 1],
        g_gains[:, 2],
        grad_table,
    )


def solution(mesh):
    cube = Cube(mesh)
    both = ("gx", "gy")
    row, flat, one = P(both, None, None), P(both, None), P(both)
    in_specs = (row, row, row, one, one) + (flat,) * 11 + (one,) * 3 + (P(),)
    out_specs = (row, row, row) + (flat,) * 11 + (one,) * 3 + (P(),)

    def per_device(*args):
        return layer(cube, *args)

    return jax.shard_map(per_device, mesh=mesh, in_specs=in_specs, out_specs=out_specs, check_vma=False)
```

time: 553 us -> 447 us (0.81)
  Pallas kernels: 0 us -> 261 us
  matrix products: 179 us -> 6.28 us
  waiting for transfers between devices: 137 us -> 58.9 us
  local copies, waits for them, and re-layouts: 92.5 us -> 32 us
  other arithmetic: 62.9 us -> 5.45 us
  starting transfers between devices: 70.2 us -> 76.8 us
    pallas_call x0 -> x40, Pallas kernels: none -> 261 us  [the longest x35 251 us: call(): pl.pallas_call(body, out_shape=[o[0] for o in outs], in_specs=ins, out_sp...]
    dot_general x37 -> x5, matrix products: 148 us -> 6.28 us  [the longest x3 5.23 us: nn(): lax.dot_general(left, right, (((1,), (0,)), ((), ())), preferred_element_...]
    ppermute x77 -> x84, waiting for transfers between devices: 137 us -> 58.9 us  [send(): return lax.ppermute(value, axis, [(i, i ^ bit) for i in range(size)])]
    convert_element_type x8 -> x1, other arithmetic: 33 us -> 1.46 us  [permutation(): return (jnp.arange(width, dtype=jnp.int32)[:, None] == feature).astype(bf16)]
    sub x2 -> x0, matrix products: 30.8 us -> none  [attend_forward(): expo = jnp.exp(scores - highest)]
    slice x46 -> x9, local copies, waits for them, and re-layouts: 31.1 us -> 3.71 us  [the longest x1 1.55 us: layer(): g_gains[:, 2]]
    unnamed x201 -> x200, local copies, waits for them, and re-layouts: 48.1 us -> 26.8 us
    add x18 -> x0, other arithmetic: 11.3 us -> none  [the longest x4 7.18 us: reduce(): total = low + self.send(high, self.core)]
  transfers between devices with their start and end apart: 77 -> 84, of which waited for: 29 -> 25; matrix products, arithmetic and copies ran while one was open for 37% -> 3% of each run, Pallas kernels for 0% -> 57%
where the time goes in v2:
time: 447 us; the launch traced here: 444 us
  Pallas kernels  261 us (58%)
  starting transfers between devices  76.8 us (17%)
  waiting for transfers between devices  58.9 us (13%)
  local copies, waits for them, and re-layouts  32 us (7%)
  matrix products  6.28 us (1%)
  other arithmetic  5.45 us (1%)
    pallas_call x35, Pallas kernels, call(): pl.pallas_call(body, out_shape=[o[0] for o in outs], in_specs=ins, out_sp...  251 us
    ppermute x84, starting transfers between devices, send(): return lax.ppermute(value, axis, [(i, i ^ bit) for i in range(size)])  76.8 us
    ppermute x84, waiting for transfers between devices, send(): return lax.ppermute(value, axis, [(i, i ^ bit) for i in range(size)])  58.9 us
    unnamed x200, local copies, waits for them, and re-layouts  26.8 us
    pallas_call x5, Pallas kernels, core_add(): pl.pallas_call(core_add_body, grid=(steps,), out_shape=[shape((s, cols),...  9.62 us
  transfers between devices with their start and end apart: 84, of which 25 were waited for; matrix products, arithmetic and copies ran while one was open for 3% of the time, Pallas kernels for 57%

profile of v2, /device:TPU:0, one launch (start us, length us, event | category | flops | bytes accessed | tf_op | source)
XLA Modules:
  0.0 443.6 jit_solution(18115316554117386589)
XLA Ops:
  2.1 2.0 pack.1
  4.1 4.1 collective-permute-start
  10.8 3.3 collective-permute-done
  16.8 4.3 collective-permute-done.1
  24.1 3.3 collective-permute-start.4
  28.1 7.6 %bias.1.refs_2_.refs_1_ = f32[48,128,128]{2,1,0:T(8,128)} custom-call(f32[48,256]{1,0:T(8,128)} %reshape.59.lines), custom_call_target="tpu_custom_call" | custom-call | bytes 25200000 | tf_op jit(solution)/shard_map/bias/pallas_call | solution.py:162
  38.8 6.2 %collective-permute-done.7 = bf16[48,3840]{1,0:T(8,128)(2,1)S(1)} collective-permute-done((bf16[48,3840]{1,0:T(8,128)(2,1)S(1)}, bf16[48,3840]{1,0:T(8,128)(2,1)S(1)}, u32[]{:S(2)}, u32[]{:S(2)}) %collective-permute-start.7) | collective-permute-done | bytes 368672 | tf_op jit(solution)/shard_map/ppermute | solution.py:45
  48.9 2.5 collective-permute-start.15
  54.1 7.1 %collective-permute-done.15 = bf16[24,4096]{1,0:T(8,128)(2,1)S(1)} collective-permute-done((bf16[24,4096]{1,0:T(8,128)(2,1)S(1)}, bf16[24,4096]{1,0:T(8,128)(2,1)S(1)}, u32[]{:S(2)}, u32[]{:S(2)}) %collective-permute-start.15) | collective-permute-done | bytes 196640 | tf_op jit(solution)/shard_map/ppermute | solution.py:45
  63.6 18.9 %self_one.1 = (f32[8,768]{1,0:T(8,128)}, bf16[512,768]{1,0:T(8,128)(2,1)}, bf16[512,2304]{1,0:T(8,128)(2,1)}, bf16[512,384]{1,0:T(8,128)(2,1)}, bf16[6,512,512]{2,1,0:T(8,128)(2,1)}) custom-call(s32[1]{0:T(128)S(6)} %copy.62.refs_0_, bf16[512,768]{1,0:T(8,128)(2,1)} %fusion.9.refs_1_.refs_0_, f32[48,128,128]{2,1,0:T(8,128)} %bias.1.refs_2_.refs_1_, ...), custom_call_target="tpu_custom_call" | custom-call | bytes 57600000 | tf_op jit(solution)/shard_map/self_one/pallas_call | solution.py:162
  82.6 13.1 %self_two.1 = (bf16[512,384]{1,0:T(8,128)(2,1)}, bf16[6,512,512]{2,1,0:T(8,128)(2,1)}) custom-call(s32[1]{0:T(128)S(6)} %copy.62.refs_0_, f32[48,128,128]{2,1,0:T(8,128)} %bias.1.refs_2_.refs_1_, bf16[512,2304]{1,0:T(8,128)(2,1)} %get-tuple-element.245.refs_2_.refs_4_), custom_call_target="tpu_custom_call" | custom-call | bytes 46800000 | tf_op jit(solution)/shard_map/self_two/pallas_call | solution.py:162
  99.0 7.8 %collective-permute-done.16.refs_9_.refs_8_.refs_7_.refs_18_.refs_3_ = bf16[48,3840]{1,0:T(8,128)(2,1)S(1)} collective-permute-done((bf16[48,3840]{1,0:T(8,128)(2,1)S(1)}, bf16[48,3840]{1,0:T(8,128)(2,1)S(1)}, u32[]{:S(2)}, u32[]{:S(2)}) %collective-permute-start.16) | collective-permute-done | bytes 368672 | tf_op jit(solution)/shard_map/ppermute | solution.py:45
  107.8 3.0 collective-permute-start.26
  112.8 3.0 collective-permute-done.26
  121.1 21.1 %cross_one.1 = (f32[512,768]{1,0:T(8,128)}, bf16[512,768]{1,0:T(8,128)(2,1)}, bf16[512,768]{1,0:T(8,128)(2,1)}, bf16[512,1536]{1,0:T(8,128)(2,1)}, bf16[512,384]...) custom-call(s32[1]{0:T(128)S(6)} %copy.63.refs_0_, bf16[512,768]{1,0:T(8,128)(2,1)} %fusion.9.refs_1_.refs_0_, ...), custom_call_target="tpu_custom_call" | custom-call | bytes 64800000 | tf_op jit(solution)/shard_map/cross_one/pallas_call | solution.py:162
  146.9 14.8 %cross_two.1 = (f32[512,768]{1,0:T(8,128)}, bf16[512,384]{1,0:T(8,128)(2,1)}, bf16[6,512,512]{2,1,0:T(8,128)(2,1)}) custom-call(s32[1]{0:T(128)S(6)} %copy.63.refs_0_, f32[512,768]{1,0:T(8,128)} %get-tuple-element.260.refs_1_.refs_0_, bf16[512,768]{1,0:T(8,128)(2,1)} %get-tuple-element.264.refs_2_.refs_1_.refs_6_, ...), custom_call_target="tpu_custom_call" | custom-call | bytes 50400000 | tf_op jit(solution)/shard_map/cross_two/pallas_call | solution.py:162
  162.9 3.0 collective-permute-done.33.refs_8_
  169.7 17.0 %ffn_one.1 = (bf16[512,768]{1,0:T(8,128)(2,1)}, bf16[512,2048]{1,0:T(8,128)(2,1)}, bf16[512,2048]{1,0:T(8,128)(2,1)}, bf16[512,2048]{1,0:T(8,128)(2,1)}, bf16[38...) custom-call(f32[512,768]{1,0:T(8,128)} %get-tuple-element.335.hidden, bf16[512,768]{1,0:T(8,128)(2,1)} %fusion.7.cot, ...), custom_call_target="tpu_custom_call" | custom-call | bytes 50400000 | tf_op jit(solution)/shard_map/ffn_one/pallas_call | solution.py:162
  189.9 4.4 collective-permute-done.38.refs_3_
  197.9 18.7 %ffn_two.1 = (bf16[384,4096]{1,0:T(8,128)(2,1)}, bf16[384,4096]{1,0:T(8,128)(2,1)}, bf16[512,4096]{1,0:T(8,128)(2,1)}) custom-call(bf16[512,768]{1,0:T(8,128)(2,1)} %fusion.7.cot, bf16[512,768]{1,0:T(8,128)(2,1)} %get-tuple-element.285.normed, bf16[512,2048]{1,0:T(8,128)(2,1)} %get-tuple-element.286.slope, bf16[512,2048]{1,0:T(8,128)(2,1)} %get-tuple-element.287.act, ...), custom_call_target="tpu_custom_call" | custom-call | bytes 50400000 | tf_op jit(solution)/shard_map/ffn_two/pallas_call | solution.py:162
  222.3 11.7 %ffn_three.1 = (f32[512,768]{1,0:T(8,128)}, bf16[512,768]{1,0:T(8,128)(2,1)}, f32[1,768]{1,0:T(1,128)}) custom-call(f32[512,768]{1,0:T(8,128)} %get-tuple-element.335.hidden, bf16[512,768]{1,0:T(8,128)(2,1)} %fusion.7.cot, f32[8,768]{1,0:T(8,128)} %get-tuple-element.254.refs_5_.gains.refs_4_.refs_2_, bf16[512,4096]{1,0:T(8,128)(2,1)} %get-tuple-element.300.d_gu, ...), custom_call_target="tpu_custom_call" | custom-call | bytes 28800000 | tf_op jit(solution)/shard_map/ffn_three/pallas_call | solution.py:162
  234.8 2.2 plane_add.5
  238.8 3.8 core_add.6
  247.6 12.6 %cross_back_one.1 = (bf16[512,768]{1,0:T(8,128)(2,1)}, bf16[512,384]{1,0:T(8,128)(2,1)}, bf16[512,768]{1,0:T(8,128)(2,1)}) custom-call(bf16[512,768]{1,0:T(8,128)(2,1)} %get-tuple-element.311.refs_0_.refs_2_, bf16[512,768]{1,0:T(8,128)(2,1)} %get-tuple-element.264.refs_2_.refs_1_.refs_6_, bf16[512,1536]{1,0:T(8,128)(2,1)} %get-tuple-element.265.refs_3_.refs_2_.refs_7_, ...), custom_call_target="tpu_custom_call" | custom-call | bytes 50400000 | tf_op jit(solution)/shard_map/cross_back_one/pallas_call | solution.py:162
  261.1 2.9 plane_add.6
  265.8 2.1 own_add.5
  267.9 2.0 collective-permute-start.52
  269.9 21.9 %cross_back_two.1 = (bf16[384,3840]{1,0:T(8,128)(2,1)}, bf16[384,3840]{1,0:T(8,128)(2,1)}, bf16[512,768]{1,0:T(8,128)(2,1)}, f32[512,768]{1,0:T(8,128)}, bf16[512,768]{1,0:T(8,128)(2,1)}, /*index=5*/f32[1,768]{1,0:T(1,128)}) custom-call(f32[512,768]{1,0:T(8,128)} %get-tuple-element.260.refs_1_.refs_0_, f32[512,768]{1,0:T(8,128)} %get-tuple-element.323.refs_1_, ...), custom_call_target="tpu_custom_call" | custom-call | bytes 72000000 | tf_op jit(solution)/shard_map/cross_back_two/pallas_call | solution.py:162
  293.0 2.7 own_add.6
  297.2 8.8 %output.1 = bf16[512,768]{1,0:T(8,128)(2,1)} custom-call(f32[512,768]{1,0:T(8,128)} %get-tuple-element.335.hidden, bf16[512,2048]{1,0:T(8,128)(2,1)} %get-tuple-element.336.gated, bf16[768,768]{1,0:T(8,128)(2,1)} %fusion.perm.refs_10_, bf16[96,2048]{1,0:T(8,128)(2,1)} %copy-done.31, bf16[96,2048]{1,0:T(8,128)(2,1)} %copy-done.37, ...), custom_call_target="tpu_custom_call" | custom-call | bytes 25200000 | tf_op jit(solution)/shard_map/output/pallas_call | solution.py:162
  306.0 3.9 core_add.7
  316.6 3.3 collective-permute-start.56
  319.9 14.2 %self_back_one.1 = (bf16[384,1152]{1,0:T(8,128)(2,1)}, bf16[384,1152]{1,0:T(8,128)(2,1)}, bf16[512,768]{1,0:T(8,128)(2,1)}, bf16[512,1152]{1,0:T(8,128)(2,1)}, f32[24,8,256]{2,1,0:T(8,128)}) custom-call(bf16[512,768]{1,0:T(8,128)(2,1)} %get-tuple-element.349.refs_0_, bf16[512,768]{1,0:T(8,128)(2,1)} %get-tuple-element.350.refs_1_.refs_3_, ...), custom_call_target="tpu_custom_call" | custom-call | bytes 57600000 | tf_op jit(solution)/shard_map/self_back_one/pallas_call | solution.py:162
  335.1 2.8 plane_add.7
  341.4 18.9 %self_back_two.1 = (bf16[384,1280]{1,0:T(8,128)(2,1)}, bf16[384,1280]{1,0:T(8,128)(2,1)}, bf16[512,768]{1,0:T(8,128)(2,1)}, f32[24,8,256]{2,1,0:T(8,128)}) custom-call(bf16[512,768]{1,0:T(8,128)(2,1)} %fusion.9.refs_1_.refs_0_, f32[512,768]{1,0:T(8,128)} %get-tuple-element.365.refs_1_, f32[8,768]{1,0:T(8,128)} %get-tuple-element.254.refs_5_.gains.refs_4_.refs_2_, ...), custom_call_target="tpu_custom_call" | custom-call | bytes 64800000 | tf_op jit(solution)/shard_map/self_back_two/pallas_call | solution.py:162
  360.4 2.8 collective-permute-done.70.got
  371.8 2.6 own_add.9
  376.2 2.0 plane_add.9
  381.2 2.0 plane_add.8
  387.2 2.0 own_add.8
  396.7 2.6 collective-permute-start.78
  401.5 2.5 collective-permute-start.69
  409.6 2.9 collective-permute-done.80
  413.8 2.4 collective-permute-done.81
  416.1 2.5 collective-permute-start.82
  418.6 2.1 collective-permute-done.82
  423.5 3.6 grad_states.1
  428.9 7.7 %grad_encoded.1 = bf16[512,768]{1,0:T(8,128)(2,1)} custom-call(bf16[512,768]{1,0:T(8,128)(2,1)} %get-tuple-element.377.refs_14_.d_kv_a, bf16[512,768]{1,0:T(8,128)(2,1)} %get-tuple-element.378.d_kv_b, bf16[768,768]{1,0:T(8,128)(2,1)} %fusion.perm.refs_10_, bf16[96,3840]{1,0:T(8,128)(2,1)} %copy-done.21, bf16[96,3840]{1,0:T(8,128)(2,1)} %copy-done.22, ...), custom_call_target="tpu_custom_call" | custom-call | bytes 25200000 | tf_op jit(solution)/shard_map/grad_encoded/pallas_call | solution.py:162
  (397 shorter events, 123.8 us)
Async XLA Ops:
  4.1 10.0 %collective-permute-start = (bf16[24,2432]{1,0:T(8,128)(2,1)}, bf16[24,2432]{1,0:T(8,128)(2,1)S(1)}, u32[]{:S(2)}, u32[]{:S(2)}) collective-permute-start(bf16[24,2432]{1,0:T(8,128)(2,1)} %get-tuple-element.223), channel_id=1, source_target_pairs={{0,4},{1,5},{2,6},{3,7},{4,0},{5,1},{6,2},{7,3},{8,12},{9,13},{10,... | collective-permute-start | bytes 350216 | tf_op jit(solution)/shard_map/ppermute | solution.py:45
  21.2 14.5 %collective-permute-start.2 = (bf16[96,2432]{1,0:T(8,128)(2,1)S(1)}, bf16[96,2432]{1,0:T(8,128)(2,1)S(1)}, u32[]{:S(2)}, u32[]{:S(2)}) collective-permute-start(bf16[96,2432]{1,0:T(8,128)(2,1)S(1)} %pad_maximum_fusion.2.refs_3_.refs_11_), channel_id=1, source_target_pairs={{0,1},{1,0},{2,3},{3,2},{4,5},{5,4},{6,7},{7,6},{8,9},{9,8},{10,11... | collective-permute-start | bytes 1400840 | tf_op jit(solution)/shard_map/ppermute | solution.py:45
  22.6 13.2 %collective-permute-start.3 = (bf16[96,2432]{1,0:T(8,128)(2,1)S(1)}, bf16[96,2432]{1,0:T(8,128)(2,1)S(1)}, u32[]{:S(2)}, u32[]{:S(2)}) collective-permute-start(bf16[96,2432]{1,0:T(8,128)(2,1)S(1)} %pad_maximum_fusion.2.refs_3_.refs_11_), channel_id=1, source_target_pairs={{0,16},{8,24},{16,0},{24,8},{1,17},{9,25},{17,1},{25,9},{2,18},{10... | collective-permute-start | bytes 1400840 | tf_op jit(solution)/shard_map/ppermute | solution.py:45
  24.1 11.6 %collective-permute-start.4 = (bf16[24,3840]{1,0:T(8,128)(2,1)S(1)}, bf16[24,3840]{1,0:T(8,128)(2,1)S(1)}, u32[]{:S(2)}, u32[]{:S(2)}) collective-permute-start(bf16[24,3840]{1,0:T(8,128)(2,1)S(1)} %copy-done.83), channel_id=1, source_target_pairs={{0,4},{1,5},{2,6},{3,7},{4,0},{5,1},{6,2},{7,3},{8,12},{9,13},{10,... | collective-permute-start | bytes 552968 | tf_op jit(solution)/shard_map/ppermute | solution.py:45
  37.6 16.2 %collective-permute-start.9 = (bf16[96,2432]{1,0:T(8,128)(2,1)S(1)}, bf16[96,2432]{1,0:T(8,128)(2,1)S(1)}, u32[]{:S(2)}, u32[]{:S(2)}) collective-permute-start(bf16[96,2432]{1,0:T(8,128)(2,1)S(1)} %collective-permute-done.2.refs_4_.refs_12_), channel_id=1, source_target_pairs={{0,8},{8,0},{16,24},{24,16},{1,9},{9,1},{17,25},{25,17},{2,10},{10... | collective-permute-start | bytes 1400840 | tf_op jit(solution)/shard_map/ppermute | solution.py:45
  46.1 36.4 %collective-permute-start.13 = (bf16[96,3840]{1,0:T(8,128)(2,1)S(1)}, bf16[96,3840]{1,0:T(8,128)(2,1)S(1)}, u32[]{:S(2)}, u32[]{:S(2)}) collective-permute-start(bf16[96,3840]{1,0:T(8,128)(2,1)S(1)} %pad_maximum_fusion.1.refs_6_.refs_5_.refs_4_.refs_15_.refs_0_), channel_id=1, source_target_pairs={{0,1},{1,0},{2,3},{3,2},{4,5},{5,4},{6,7},{7,6},{8,9},{9,8},{10,11... | collective-permute-start | bytes 2211848 | tf_op jit(solution)/shard_map/ppermute | solution.py:45
  47.6 34.9 %collective-permute-start.14 = (bf16[96,3840]{1,0:T(8,128)(2,1)S(1)}, bf16[96,3840]{1,0:T(8,128)(2,1)S(1)}, u32[]{:S(2)}, u32[]{:S(2)}) collective-permute-start(bf16[96,3840]{1,0:T(8,128)(2,1)S(1)} %pad_maximum_fusion.1.refs_6_.refs_5_.refs_4_.refs_15_.refs_0_), channel_id=1, source_target_pairs={{0,16},{8,24},{16,0},{24,8},{1,17},{9,25},{17,1},{25,9},{2,18},{10... | collective-permute-start | bytes 2211848 | tf_op jit(solution)/shard_map/ppermute | solution.py:45
  48.1 13.2 %collective-permute-start.10 = (bf16[96,2432]{1,0:T(8,128)(2,1)S(1)}, bf16[96,2432]{1,0:T(8,128)(2,1)S(1)}, u32[]{:S(2)}, u32[]{:S(2)}) collective-permute-start(bf16[96,2432]{1,0:T(8,128)(2,1)S(1)} %collective-permute-done.3.refs_5_.refs_13_), channel_id=1, source_target_pairs={{0,8},{8,0},{16,24},{24,16},{1,9},{9,1},{17,25},{25,17},{2,10},{10... | collective-permute-start | bytes 1400840 | tf_op jit(solution)/shard_map/ppermute | solution.py:45
  48.9 12.3 %collective-permute-start.15 = (bf16[24,4096]{1,0:T(8,128)(2,1)S(1)}, bf16[24,4096]{1,0:T(8,128)(2,1)S(1)}, u32[]{:S(2)}, u32[]{:S(2)}) collective-permute-start(bf16[24,4096]{1,0:T(8,128)(2,1)S(1)} %copy-done.81), channel_id=1, source_target_pairs={{0,4},{1,5},{2,6},{3,7},{4,0},{5,1},{6,2},{7,3},{8,12},{9,13},{10,... | collective-permute-start | bytes 589832 | tf_op jit(solution)/shard_map/ppermute | solution.py:45
  82.5 15.5 %collective-permute-start.18 = (bf16[48,4096]{1,0:T(8,128)(2,1)S(1)}, bf16[48,4096]{1,0:T(8,128)(2,1)S(1)}, u32[]{:S(2)}, u32[]{:S(2)}) collective-permute-start(bf16[48,4096]{1,0:T(8,128)(2,1)S(1)} %pad_maximum_fusion.3), channel_id=1, source_target_pairs={{0,2},{1,3},{2,0},{3,1},{4,6},{5,7},{6,4},{7,5},{8,10},{9,11},{10,... | collective-permute-start | bytes 1179656 | tf_op jit(solution)/shard_map/ppermute | solution.py:45
  95.8 11.0 %collective-permute-start.16 = (bf16[48,3840]{1,0:T(8,128)(2,1)S(1)}, bf16[48,3840]{1,0:T(8,128)(2,1)S(1)}, u32[]{:S(2)}, u32[]{:S(2)}) collective-permute-start(bf16[48,3840]{1,0:T(8,128)(2,1)S(1)} %slice.35), channel_id=1, source_target_pairs={{0,1},{1,0},{2,3},{3,2},{4,5},{5,4},{6,7},{7,6},{8,9},{9,8},{10,11... | collective-permute-start | bytes 1105928 | tf_op jit(solution)/shard_map/ppermute | solution.py:45
  96.4 10.8 %collective-permute-start.17 = (bf16[48,3840]{1,0:T(8,128)(2,1)S(1)}, bf16[48,3840]{1,0:T(8,128)(2,1)S(1)}, u32[]{:S(2)}, u32[]{:S(2)}) collective-permute-start(bf16[48,3840]{1,0:T(8,128)(2,1)S(1)} %slice.36), channel_id=1, source_target_pairs={{0,16},{8,24},{16,0},{24,8},{1,17},{9,25},{17,1},{25,9},{2,18},{10... | collective-permute-start | bytes 1105928 | tf_op jit(solution)/shard_map/ppermute | solution.py:45
  110.8 31.4 %collective-permute-start.24 = (bf16[96,4096]{1,0:T(8,128)(2,1)}, bf16[96,4096]{1,0:T(8,128)(2,1)}, u32[]{:S(2)}, u32[]{:S(2)}) collective-permute-start(bf16[96,4096]{1,0:T(8,128)(2,1)} %pad_maximum_fusion.refs_0_), channel_id=1, source_target_pairs={{0,1},{1,0},{2,3},{3,2},{4,5},{5,4},{6,7},{7,6},{8,9},{9,8},{10,11... | collective-permute-start | bytes 2359304 | tf_op jit(solution)/shard_map/ppermute | solution.py:45
  111.6 30.6 %collective-permute-start.25 = (bf16[96,4096]{1,0:T(8,128)(2,1)}, bf16[96,4096]{1,0:T(8,128)(2,1)}, u32[]{:S(2)}, u32[]{:S(2)}) collective-permute-start(bf16[96,4096]{1,0:T(8,128)(2,1)} %pad_maximum_fusion.refs_0_), channel_id=1, source_target_pairs={{0,16},{8,24},{16,0},{24,8},{1,17},{9,25},{17,1},{25,9},{2,18},{10... | collective-permute-start | bytes 2359304 | tf_op jit(solution)/shard_map/ppermute | solution.py:45
  142.3 19.4 %collective-permute-start.29 = (bf16[48,2048]{1,0:T(8,128)(2,1)S(1)}, bf16[48,2048]{1,0:T(8,128)(2,1)S(1)}, u32[]{:S(2)}, u32[]{:S(2)}) collective-permute-start(bf16[48,2048]{1,0:T(8,128)(2,1)S(1)} %copy-done.53), channel_id=1, source_target_pairs={{0,2},{1,3},{2,0},{3,1},{4,6},{5,7},{6,4},{7,5},{8,10},{9,11},{10,... | collective-permute-start | bytes 589832 | tf_op jit(solution)/shard_map/ppermute | solution.py:45
  143.4 18.3 %collective-permute-start.27 = (bf16[48,4096]{1,0:T(8,128)(2,1)S(1)}, bf16[48,4096]{1,0:T(8,128)(2,1)S(1)}, u32[]{:S(2)}, u32[]{:S(2)}) collective-permute-start(bf16[48,4096]{1,0:T(8,128)(2,1)S(1)} %slice.37), channel_id=1, source_target_pairs={{0,1},{1,0},{2,3},{3,2},{4,5},{5,4},{6,7},{7,6},{8,9},{9,8},{10,11... | collective-permute-start | bytes 1179656 | tf_op jit(solution)/shard_map/ppermute | solution.py:45
  145.5 16.3 %collective-permute-start.28 = (bf16[48,4096]{1,0:T(8,128)(2,1)S(1)}, bf16[48,4096]{1,0:T(8,128)(2,1)S(1)}, u32[]{:S(2)}, u32[]{:S(2)}) collective-permute-start(bf16[48,4096]{1,0:T(8,128)(2,1)S(1)} %slice.38), channel_id=1, source_target_pairs={{0,16},{8,24},{16,0},{24,8},{1,17},{9,25},{17,1},{25,9},{2,18},{10... | collective-permute-start | bytes 1179656 | tf_op jit(solution)/shard_map/ppermute | solution.py:45
  165.9 20.8 %collective-permute-start.35 = (bf16[96,2048]{1,0:T(8,128)(2,1)S(1)}, bf16[96,2048]{1,0:T(8,128)(2,1)S(1)}, u32[]{:S(2)}, u32[]{:S(2)}) collective-permute-start(bf16[96,2048]{1,0:T(8,128)(2,1)S(1)} %pad_maximum_fusion.4.refs_0_), channel_id=1, source_target_pairs={{0,1},{1,0},{2,3},{3,2},{4,5},{5,4},{6,7},{7,6},{8,9},{9,8},{10,11... | collective-permute-start | bytes 1179656 | tf_op jit(solution)/shard_map/ppermute | solution.py:45
  166.8 19.9 %collective-permute-start.36 = (bf16[96,2048]{1,0:T(8,128)(2,1)S(1)}, bf16[96,2048]{1,0:T(8,128)(2,1)S(1)}, u32[]{:S(2)}, u32[]{:S(2)}) collective-permute-start(bf16[96,2048]{1,0:T(8,128)(2,1)S(1)} %pad_maximum_fusion.4.refs_0_), channel_id=1, source_target_pairs={{0,16},{8,24},{16,0},{24,8},{1,17},{9,25},{17,1},{25,9},{2,18},{10... | collective-permute-start | bytes 1179656 | tf_op jit(solution)/shard_map/ppermute | solution.py:45
  186.8 29.9 %collective-permute-start.37 = (bf16[384,2048]{1,0:T(8,128)(2,1)}, bf16[384,2048]{1,0:T(8,128)(2,1)S(1)}, u32[]{:S(2)}, u32[]{:S(2)}) collective-permute-start(bf16[384,2048]{1,0:T(8,128)(2,1)} %get-tuple-element.284), channel_id=1, source_target_pairs={{0,8},{8,0},{16,24},{24,16},{1,9},{9,1},{17,25},{25,17},{2,10},{10... | collective-permute-start | bytes 4718600 | tf_op jit(solution)/shard_map/ppermute | solution.py:45
  216.7 17.4 %collective-permute-start.47 = (bf16[384,4096]{1,0:T(8,128)(2,1)}, bf16[384,4096]{1,0:T(8,128)(2,1)}, u32[]{:S(2)}, u32[]{:S(2)}) collective-permute-start(bf16[384,4096]{1,0:T(8,128)(2,1)} %get-tuple-element.299), channel_id=1, source_target_pairs={{0,8},{8,0},{16,24},{24,16},{1,9},{9,1},{17,25},{25,17},{2,10},{10... | collective-permute-start | bytes 9437192 | tf_op jit(solution)/shard_map/ppermute | solution.py:45
  220.0 14.0 %collective-permute-start.45 = (bf16[48,2048]{1,0:T(8,128)(2,1)S(1)}, bf16[48,2048]{1,0:T(8,128)(2,1)S(1)}, u32[]{:S(2)}, u32[]{:S(2)}) collective-permute-start(bf16[48,2048]{1,0:T(8,128)(2,1)S(1)} %get-tuple-element.297), channel_id=1, source_target_pairs={{0,16},{8,24},{16,0},{24,8},{1,17},{9,25},{17,1},{25,9},{2,18},{10... | collective-permute-start | bytes 589832 | tf_op jit(solution)/shard_map/ppermute | solution.py:45
  221.4 12.6 %collective-permute-start.46 = (bf16[48,2048]{1,0:T(8,128)(2,1)S(1)}, bf16[48,2048]{1,0:T(8,128)(2,1)S(1)}, u32[]{:S(2)}, u32[]{:S(2)}) collective-permute-start(bf16[48,2048]{1,0:T(8,128)(2,1)S(1)} %get-tuple-element.298), channel_id=1, source_target_pairs={{0,1},{1,0},{2,3},{3,2},{4,5},{5,4},{6,7},{7,6},{8,9},{9,8},{10,11... | collective-permute-start | bytes 589832 | tf_op jit(solution)/shard_map/ppermute | solution.py:45
  237.0 23.2 %collective-permute-start.48 = (bf16[96,2048]{1,0:T(8,128)(2,1)}, bf16[96,2048]{1,0:T(8,128)(2,1)S(1)}, u32[]{:S(2)}, u32[]{:S(2)}) collective-permute-start(bf16[96,2048]{1,0:T(8,128)(2,1)} %get-tuple-element.305), channel_id=1, source_target_pairs={{0,1},{1,0},{2,3},{3,2},{4,5},{5,4},{6,7},{7,6},{8,9},{9,8},{10,11... | collective-permute-start | bytes 1179656 | tf_op jit(solution)/shard_map/ppermute | solution.py:45
  238.1 22.1 %collective-permute-start.49 = (bf16[96,2048]{1,0:T(8,128)(2,1)}, bf16[96,2048]{1,0:T(8,128)(2,1)S(1)}, u32[]{:S(2)}, u32[]{:S(2)}) collective-permute-start(bf16[96,2048]{1,0:T(8,128)(2,1)} %get-tuple-element.306), channel_id=1, source_target_pairs={{0,16},{8,24},{16,0},{24,8},{1,17},{9,25},{17,1},{25,9},{2,18},{10... | collective-permute-start | bytes 1179656 | tf_op jit(solution)/shard_map/ppermute | solution.py:45
  245.3 14.9 %collective-permute-start.50 = (bf16[48,4096]{1,0:T(8,128)(2,1)S(1)}, bf16[48,4096]{1,0:T(8,128)(2,1)S(1)}, u32[]{:S(2)}, u32[]{:S(2)}) collective-permute-start(bf16[48,4096]{1,0:T(8,128)(2,1)S(1)} %get-tuple-element.309), channel_id=1, source_target_pairs={{0,16},{8,24},{16,0},{24,8},{1,17},{9,25},{17,1},{25,9},{2,18},{10... | collective-permute-start | bytes 1179656 | tf_op jit(solution)/shard_map/ppermute | solution.py:45
  246.6 13.6 %collective-permute-start.51 = (bf16[48,4096]{1,0:T(8,128)(2,1)S(1)}, bf16[48,4096]{1,0:T(8,128)(2,1)S(1)}, u32[]{:S(2)}, u32[]{:S(2)}) collective-permute-start(bf16[48,4096]{1,0:T(8,128)(2,1)S(1)} %get-tuple-element.310), channel_id=1, source_target_pairs={{0,1},{1,0},{2,3},{3,2},{4,5},{5,4},{6,7},{7,6},{8,9},{9,8},{10,11... | collective-permute-start | bytes 1179656 | tf_op jit(solution)/shard_map/ppermute | solution.py:45
  264.0 27.8 %collective-permute-start.53 = (bf16[96,4096]{1,0:T(8,128)(2,1)}, bf16[96,4096]{1,0:T(8,128)(2,1)S(1)}, u32[]{:S(2)}, u32[]{:S(2)}) collective-permute-start(bf16[96,4096]{1,0:T(8,128)(2,1)} %get-tuple-element.321), channel_id=1, source_target_pairs={{0,1},{1,0},{2,3},{3,2},{4,5},{5,4},{6,7},{7,6},{8,9},{9,8},{10,11... | collective-permute-start | bytes 2359304 | tf_op jit(solution)/shard_map/ppermute | solution.py:45
  265.1 26.7 %collective-permute-start.54 = (bf16[96,4096]{1,0:T(8,128)(2,1)}, bf16[96,4096]{1,0:T(8,128)(2,1)S(1)}, u32[]{:S(2)}, u32[]{:S(2)}) collective-permute-start(bf16[96,4096]{1,0:T(8,128)(2,1)} %get-tuple-element.322), channel_id=1, source_target_pairs={{0,16},{8,24},{16,0},{24,8},{1,17},{9,25},{17,1},{25,9},{2,18},{10... | collective-permute-start | bytes 2359304 | tf_op jit(solution)/shard_map/ppermute | solution.py:45
  267.9 24.0 %collective-permute-start.52 = (bf16[48,2048]{1,0:T(8,128)(2,1)}, bf16[48,2048]{1,0:T(8,128)(2,1)S(1)}, u32[]{:S(2)}, u32[]{:S(2)}) collective-permute-start(bf16[48,2048]{1,0:T(8,128)(2,1)} %get-tuple-element.316), channel_id=1, source_target_pairs={{0,2},{1,3},{2,0},{3,1},{4,6},{5,7},{6,4},{7,5},{8,10},{9,11},{10,... | collective-permute-start | bytes 589832 | tf_op jit(solution)/shard_map/ppermute | solution.py:45
  291.9 14.1 %collective-permute-start.55 = (bf16[384,3840]{1,0:T(8,128)(2,1)}, bf16[384,3840]{1,0:T(8,128)(2,1)}, u32[]{:S(2)}, u32[]{:S(2)}) collective-permute-start(bf16[384,3840]{1,0:T(8,128)(2,1)} %get-tuple-element.333), channel_id=1, source_target_pairs={{0,8},{8,0},{16,24},{24,16},{1,9},{9,1},{17,25},{25,17},{2,10},{10... | collective-permute-start | bytes 8847368 | tf_op jit(solution)/shard_map/ppermute | solution.py:45
  295.7 38.4 %collective-permute-start.57 = (bf16[48,4096]{1,0:T(8,128)(2,1)}, bf16[48,4096]{1,0:T(8,128)(2,1)S(1)}, u32[]{:S(2)}, u32[]{:S(2)}) collective-permute-start(bf16[48,4096]{1,0:T(8,128)(2,1)} %get-tuple-element.345), channel_id=1, source_target_pairs={{0,2},{1,3},{2,0},{3,1},{4,6},{5,7},{6,4},{7,5},{8,10},{9,11},{10,... | collective-permute-start | bytes 1179656 | tf_op jit(solution)/shard_map/ppermute | solution.py:45
  312.5 21.6 %collective-permute-start.58 = (bf16[48,3840]{1,0:T(8,128)(2,1)S(1)}, bf16[48,3840]{1,0:T(8,128)(2,1)S(1)}, u32[]{:S(2)}, u32[]{:S(2)}) collective-permute-start(bf16[48,3840]{1,0:T(8,128)(2,1)S(1)} %get-tuple-element.347), channel_id=1, source_target_pairs={{0,16},{8,24},{16,0},{24,8},{1,17},{9,25},{17,1},{25,9},{2,18},{10... | collective-permute-start | bytes 1105928 | tf_op jit(solution)/shard_map/ppermute | solution.py:45
  313.9 20.2 %collective-permute-start.59 = (bf16[48,3840]{1,0:T(8,128)(2,1)S(1)}, bf16[48,3840]{1,0:T(8,128)(2,1)S(1)}, u32[]{:S(2)}, u32[]{:S(2)}) collective-permute-start(bf16[48,3840]{1,0:T(8,128)(2,1)S(1)} %get-tuple-element.348), channel_id=1, source_target_pairs={{0,1},{1,0},{2,3},{3,2},{4,5},{5,4},{6,7},{7,6},{8,9},{9,8},{10,11... | collective-permute-start | bytes 1105928 | tf_op jit(solution)/shard_map/ppermute | solution.py:45
  316.6 17.5 %collective-permute-start.56 = (bf16[24,2048]{1,0:T(8,128)(2,1)}, bf16[24,2048]{1,0:T(8,128)(2,1)S(1)}, u32[]{:S(2)}, u32[]{:S(2)}) collective-permute-start(bf16[24,2048]{1,0:T(8,128)(2,1)} %get-tuple-element.341), channel_id=1, source_target_pairs={{0,4},{1,5},{2,6},{3,7},{4,0},{5,1},{6,2},{7,3},{8,12},{9,13},{10,... | collective-permute-start | bytes 294920 | tf_op jit(solution)/shard_map/ppermute | solution.py:45
  334.8 25.6 %collective-permute-start.60 = (bf16[384,1152]{1,0:T(8,128)(2,1)}, bf16[384,1152]{1,0:T(8,128)(2,1)S(1)}, u32[]{:S(2)}, u32[]{:S(2)}) collective-permute-start(bf16[384,1152]{1,0:T(8,128)(2,1)} %get-tuple-element.355), channel_id=1, source_target_pairs={{0,8},{8,0},{16,24},{24,16},{1,9},{9,1},{17,25},{25,17},{2,10},{10... | collective-permute-start | bytes 2654216 | tf_op jit(solution)/shard_map/ppermute | solution.py:45
  337.9 22.4 %collective-permute-start.61 = (bf16[96,3840]{1,0:T(8,128)(2,1)}, bf16[96,3840]{1,0:T(8,128)(2,1)S(1)}, u32[]{:S(2)}, u32[]{:S(2)}) collective-permute-start(bf16[96,3840]{1,0:T(8,128)(2,1)} %get-tuple-element.360), channel_id=1, source_target_pairs={{0,1},{1,0},{2,3},{3,2},{4,5},{5,4},{6,7},{7,6},{8,9},{9,8},{10,11... | collective-permute-start | bytes 2211848 | tf_op jit(solution)/shard_map/ppermute | solution.py:45
  338.7 21.6 %collective-permute-start.62 = (bf16[96,3840]{1,0:T(8,128)(2,1)}, bf16[96,3840]{1,0:T(8,128)(2,1)S(1)}, u32[]{:S(2)}, u32[]{:S(2)}) collective-permute-start(bf16[96,3840]{1,0:T(8,128)(2,1)} %get-tuple-element.361), channel_id=1, source_target_pairs={{0,16},{8,24},{16,0},{24,8},{1,17},{9,25},{17,1},{25,9},{2,18},{10... | collective-permute-start | bytes 2211848 | tf_op jit(solution)/shard_map/ppermute | solution.py:45
  341.4 18.9 %collective-permute-start.63 = (bf16[24,4096]{1,0:T(8,128)(2,1)}, bf16[24,4096]{1,0:T(8,128)(2,1)S(1)}, u32[]{:S(2)}, u32[]{:S(2)}) collective-permute-start(bf16[24,4096]{1,0:T(8,128)(2,1)} %get-tuple-element.364), channel_id=1, source_target_pairs={{0,4},{1,5},{2,6},{3,7},{4,0},{5,1},{6,2},{7,3},{8,12},{9,13},{10,... | collective-permute-start | bytes 589832 | tf_op jit(solution)/shard_map/ppermute | solution.py:45
  365.0 11.2 %collective-permute-start.71 = (bf16[48,1280]{1,0:T(8,128)(2,1)S(1)}, bf16[48,1280]{1,0:T(8,128)(2,1)}, u32[]{:S(2)}, u32[]{:S(2)}) collective-permute-start(bf16[48,1280]{1,0:T(8,128)(2,1)S(1)} %get-tuple-element.396), channel_id=1, source_target_pairs={{0,16},{8,24},{16,0},{24,8},{1,17},{9,25},{17,1},{25,9},{2,18},{10... | collective-permute-start | bytes 368648 | tf_op jit(solution)/shard_map/ppermute | solution.py:45
  366.3 9.9 %collective-permute-start.72 = (bf16[48,1280]{1,0:T(8,128)(2,1)S(1)}, bf16[48,1280]{1,0:T(8,128)(2,1)}, u32[]{:S(2)}, u32[]{:S(2)}) collective-permute-start(bf16[48,1280]{1,0:T(8,128)(2,1)S(1)} %get-tuple-element.398), channel_id=1, source_target_pairs={{0,1},{1,0},{2,3},{3,2},{4,5},{5,4},{6,7},{7,6},{8,9},{9,8},{10,11... | collective-permute-start | bytes 368648 | tf_op jit(solution)/shard_map/ppermute | solution.py:45
  370.2 10.3 %collective-permute-start.64 = (bf16[48,1152]{1,0:T(8,128)(2,1)S(1)}, bf16[48,1152]{1,0:T(8,128)(2,1)S(1)}, u32[]{:S(2)}, u32[]{:S(2)}) collective-permute-start(bf16[48,1152]{1,0:T(8,128)(2,1)S(1)} %get-tuple-element.383), channel_id=1, source_target_pairs={{0,16},{8,24},{16,0},{24,8},{1,17},{9,25},{17,1},{25,9},{2,18},{10... | collective-permute-start | bytes 331784 | tf_op jit(solution)/shard_map/ppermute | solution.py:45
  374.4 19.6 %collective-permute-start.77 = (bf16[48,3840]{1,0:T(8,128)(2,1)}, bf16[48,3840]{1,0:T(8,128)(2,1)S(1)}, u32[]{:S(2)}, u32[]{:S(2)}) collective-permute-start(bf16[48,3840]{1,0:T(8,128)(2,1)} %get-tuple-element.412), channel_id=1, source_target_pairs={{0,2},{1,3},{2,0},{3,1},{4,6},{5,7},{6,4},{7,5},{8,10},{9,11},{10,... | collective-permute-start | bytes 1105928 | tf_op jit(solution)/shard_map/ppermute | solution.py:45
  389.3 14.7 %collective-permute-start.75 = (bf16[48,1280]{1,0:T(8,128)(2,1)}, bf16[48,1280]{1,0:T(8,128)(2,1)S(1)}, u32[]{:S(2)}, u32[]{:S(2)}) collective-permute-start(bf16[48,1280]{1,0:T(8,128)(2,1)} %get-tuple-element.402), channel_id=1, source_target_pairs={{0,2},{1,3},{2,0},{3,1},{4,6},{5,7},{6,4},{7,5},{8,10},{9,11},{10,... | collective-permute-start | bytes 368648 | tf_op jit(solution)/shard_map/ppermute | solution.py:45
  396.7 40.5 %collective-permute-start.78 = (bf16[24,3840]{1,0:T(8,128)(2,1)}, bf16[24,3840]{1,0:T(8,128)(2,1)S(1)}, u32[]{:S(2)}, u32[]{:S(2)}) collective-permute-start(bf16[24,3840]{1,0:T(8,128)(2,1)} %get-tuple-element.414), channel_id=1, source_target_pairs={{0,4},{1,5},{2,6},{3,7},{4,0},{5,1},{6,2},{7,3},{8,12},{9,13},{10,... | collective-permute-start | bytes 552968 | tf_op jit(solution)/shard_map/ppermute | solution.py:45
  401.5 38.1 %collective-permute-start.69 = (bf16[24,1152]{1,0:T(8,128)(2,1)}, bf16[24,1152]{1,0:T(8,128)(2,1)S(1)}, u32[]{:S(2)}, u32[]{:S(2)}) collective-permute-start(bf16[24,1152]{1,0:T(8,128)(2,1)} %get-tuple-element.391), channel_id=1, source_target_pairs={{0,4},{1,5},{2,6},{3,7},{4,0},{5,1},{6,2},{7,3},{8,12},{9,13},{10,... | collective-permute-start | bytes 165896 | tf_op jit(solution)/shard_map/ppermute | solution.py:45
  406.3 33.4 %collective-permute-start.76 = (bf16[24,1280]{1,0:T(8,128)(2,1)}, bf16[24,1280]{1,0:T(8,128)(2,1)S(1)}, u32[]{:S(2)}, u32[]{:S(2)}) collective-permute-start(bf16[24,1280]{1,0:T(8,128)(2,1)} %get-tuple-element.404), channel_id=1, source_target_pairs={{0,4},{1,5},{2,6},{3,7},{4,0},{5,1},{6,2},{7,3},{8,12},{9,13},{10,... | collective-permute-start | bytes 184328 | tf_op jit(solution)/shard_map/ppermute | solution.py:45
  420.7 15.9 %collective-permute-start.83 = (f32[32,12]{0,1:T(8,128)S(1)}, f32[32,12]{0,1:T(8,128)S(1)}, u32[]{:S(2)}, u32[]{:S(2)}) collective-permute-start(f32[32,12]{0,1:T(8,128)S(1)} %add.48), channel_id=1, source_target_pairs={{0,2},{1,3},{2,0},{3,1},{4,6},{5,7},{6,4},{7,5},{8,10},{9,11},{10,... | collective-permute-start | bytes 4616 | tf_op jit(solution)/shard_map/ppermute | solution.py:45
  (136 other events, 931.7 us)
